TPU v7x, 32 devices: a whole 2x2x4 slice. The times are simulated.
32 devices in a mesh: survey: 2 (over y), inline: 4 (over z), xline: 2 (over x), depth: 2 (over core).
Axes of the slice: x: 2, y: 2, z: 4, core: 2. Of those that a mesh axis runs over, the one named last changes fastest.
Arguments:
- seismic: bfloat16 [128, 64, 512], P(('survey', 'inline'), 'xline', 'depth'), parts along dimension 0, may hold values from -64 to 64
- trace_live: int32 [128, 64], P(('survey', 'inline'), 'xline'), parts along dimension 0, may hold values from 0 to 1
- filter_taps: bfloat16 [3, 96, 5], replicated, may hold values from -2.6875 to 2.6875
Outputs:
- whitened: bfloat16 [96, 64, 32, 256], P(None, ('survey', 'inline'), 'xline', 'depth'), parts along dimension 1
- factor: float32 [192, 96], P('survey'), parts along dimension 0
There are 2 independent parts, one for each index of `survey`. A program takes and returns all parts, laid end to end along the dimension named above; an argument that names none is the same for every part. Nothing has to cross between parts.
All inputs are finite; a program needn't handle non-finite values.
Results may differ from a plain program's by a relative error of at most 0.0039.
The roundings to bfloat16 on the way count: a program that leaves them out, or rounds other values in their place, can miss the bound.
Values may be sent and summed in bfloat16 or wider, within the bound.
No kernel may reach another device: no remote copies, remote signals or barrier semaphores. Data moves between devices by JAX's collectives and lax.ppermute only.
A program may use at most 64 MiB of HBM per device.

v0:
```python
import jax
import jax.numpy as jnp
from jax import lax
from jax.sharding import PartitionSpec as P

ORIENT = 32
LEVELS = 3
TAPS = 5
CHAN = 96


def extended(value, sides, width):
    for axis, dim in sides:
        size, length = (lax.axis_size(axis), value.shape[dim])
        up = [(i, (i + 1) % size) for i in range(size - 1)]
        down = [(j, i) for i, j in up]
        last = lax.slice_in_dim(value, length - width, length, axis=dim)
        initial = lax.slice_in_dim(value, 0, width, axis=dim)
        before = lax.ppermute(last, axis, up)
        after = lax.ppermute(initial, axis, down)
        value = jnp.concatenate([before, value, after], axis=dim)
    return value


def banded(tap_rows, dilation, length, reach):
    outputs = length // 2
    width = length + 2 * reach
    out_index = jnp.arange(outputs, dtype=jnp.int32)[None, :, None]
    in_index = jnp.arange(width, dtype=jnp.int32)[None, None, :]
    total = jnp.zeros((tap_rows.shape[0], outputs, width), jnp.float32)
    for k in range(TAPS):
        target = 2 * out_index + reach + dilation[:, None, None] * (k - TAPS // 2)
        total = total + jnp.where(
            in_index == target, tap_rows[:, k, None, None].astype(jnp.float32), 0.0
        )
    return total.astype(jnp.bfloat16)


def local(seismic, trace_live, filter_taps):
    reach = TAPS // 2 * 2 ** (LEVELS - 1)
    il_len, xl_len, t_len = seismic.shape
    weights = trace_live.astype(jnp.bfloat16)
    brick = seismic * weights[:, :, None]
    padded = extended(brick, (("inline", 0), ("xline", 1), ("depth", 2)), reach)
    row_mask = trace_live[0::2, 0::2].astype(jnp.float32)
    dilation = 2 ** (jnp.arange(CHAN, dtype=jnp.int32) // ORIENT)
    blocks_count = CHAN // 8
    inline_mats = banded(filter_taps[0], dilation, il_len, reach).reshape(
        blocks_count, 8, il_len // 2, -1
    )
    xline_mats = banded(filter_taps[1], dilation, xl_len, reach).reshape(
        blocks_count, 8, xl_len // 2, -1
    )
    time_mats = banded(filter_taps[2], dilation, t_len, reach).reshape(
        blocks_count, 8, t_len // 2, -1
    )

    def one_block(mats):
        inline_mat, xline_mat, time_mat = mats
        first = jnp.einsum(
            "cop,pqt->coqt", inline_mat, padded, preferred_element_type=jnp.float32
        ).astype(jnp.bfloat16)
        second = jnp.einsum(
            "csq,coqt->cost", xline_mat, first, preferred_element_type=jnp.float32
        ).astype(jnp.bfloat16)
        third = jnp.einsum("cut,cost->cosu", time_mat, second, preferred_element_type=jnp.float32)
        return (third * row_mask[None, :, :, None]).astype(jnp.bfloat16)

    attributes = lax.map(one_block, (inline_mats, xline_mats, time_mats))
    attributes = attributes.reshape(CHAN, il_len // 2, xl_len // 2, t_len // 2)
    live_rows = jnp.sum(row_mask)
    flat = attributes.reshape(CHAN, -1)
    gram = jnp.dot(flat, flat.T, preferred_element_type=jnp.float32)
    count = live_rows * jnp.float32(t_len // 2)
    gram, count = lax.psum((gram, count), ("inline", "xline", "depth"))
    lower = jnp.linalg.cholesky(gram / count)
    inverse = jax.scipy.linalg.solve_triangular(lower, jnp.eye(CHAN, dtype=jnp.float32), lower=True)
    inverse_low = inverse.astype(jnp.bfloat16)
    whitened = jnp.dot(inverse_low, flat, preferred_element_type=jnp.float32)
    whitened = whitened.astype(jnp.bfloat16).reshape(CHAN, il_len // 2, xl_len // 2, t_len // 2)
    return (whitened, lower.T)


def solution(mesh):
    placed = (P(("survey", "inline"), "xline", "depth"), P(("survey", "inline"), "xline"), P())
    return jax.shard_map(
        local,
        mesh=mesh,
        in_specs=placed,
        out_specs=(P(None, ("survey", "inline"), "xline", "depth"), P("survey", None)),
        check_vma=False,
    )
```

profile of v0, /device:TPU:0, one launch (start us, length us, event | category | flops | bytes accessed | tf_op | source)
XLA Modules:
  0.0 182.4 jit_solution(15267018123131024979)
XLA Ops:
  2.4 4.9 %collective-permute-start = (bf16[8,32,256]{2,1,0:T(8,128)(2,1)S(1)}, bf16[8,32,256]{2,1,0:T(8,128)(2,1)S(1)}, u32[]{:S(2)}, u32[]{:S(2)}) collective-permute-start(bf16[8,32,256]{2,1,0:T(8,128)(2,1)S(1)} %get-tuple-element.79), channel_id=1, source_target_pairs={{0,4},{4,8},{8,12},{1,5},{5,9},{9,13},{2,6},{6,10},{10,14},{3,7},{... | collective-permute-start | bytes 393224 | tf_op jit(solution)/shard_map/ppermute | solution.py:19
  12.0 2.0 %add_convert_fusion.2 = bf16[12,8,8,32]{3,2,1,0:T(8,128)(2,1)} fusion(f32[12,8]{1,0:T(8,128)S(1)} %reshape.649, s32[12,8,8]{2,1,0:T(8,128)S(1)} %get-tuple-element.97, f32[12,8]{1,0:T(8,128)S(1)} %reshape.648, s32[12,8,8]{2,1,0:T(8,128)S(1)} %get-tuple-element.96, f32[12,8]{1,0:T(8,128)S(1)} %reshape.647, s32[8]{0:T(128)S(1)} %multiply_add_fusion.3, ...), kind=kLoop, calls=%fused_computation.36 | loop fusion | flops 368640 | bytes 63392 | tf_op jit(solution)/shard_map/convert_element_type | solution.py:36
  14.0 15.2 %add_convert_fusion = bf16[12,8,128,272]{2,3,1,0:T(8,128)(2,1)} fusion(f32[12,8]{1,0:T(8,128)S(1)} %reshape.659, s32[12,8,128]{2,1,0:T(8,128)S(1)} %get-tuple-element.89, f32[12,8]{1,0:T(8,128)S(1)} %reshape.658, s32[12,8,128]{2,1,0:T(8,128)S(1)} %get-tuple-element.88, f32[12,8]{1,0:T(8,128)S(1)} %reshape.657, s32[128]{0:T(128)S(1)} %multiply_add_fusion.1, ...), kind=kLoop, calls=%fused_computation.20 | loop fusion | flops 50135040 | bytes 6883712 | tf_op jit(solution)/shard_map/convert_element_type | solution.py:36
  29.3 3.4 %collective-permute-start.2 = (bf16[32,8,256]{2,1,0:T(8,128)(2,1)S(1)}, bf16[32,8,256]{2,1,0:T(8,128)(2,1)S(1)}, u32[]{:S(2)}, u32[]{:S(2)}) collective-permute-start(bf16[32,8,256]{2,1,0:T(8,128)(2,1)S(1)} %get-tuple-element.77), channel_id=1, source_target_pairs={{0,2},{1,3},{4,6},{5,7},{8,10},{9,11},{12,14},{13,15},{16,18},{17,... | collective-permute-start | bytes 393224 | tf_op jit(solution)/shard_map/ppermute | solution.py:19
  34.1 2.5 %add_convert_fusion.1 = bf16[12,8,16,48]{3,2,1,0:T(8,128)(2,1)} fusion(f32[12,8]{1,0:T(8,128)S(1)} %reshape.654, s32[12,8,16]{2,1,0:T(8,128)S(1)} %get-tuple-element.93, f32[12,8]{1,0:T(8,128)S(1)} %reshape.653, s32[12,8,16]{2,1,0:T(8,128)S(1)} %get-tuple-element.92, f32[12,8]{1,0:T(8,128)S(1)} %reshape.652, s32[16]{0:T(128)S(1)} %multiply_add_fusion.2, ...), kind=kLoop, calls=%fused_computation.30 | loop fusion | flops 1105920 | bytes 174016 | tf_op jit(solution)/shard_map/convert_element_type | solution.py:36
  36.6 3.0 %collective-permute-done.3 = bf16[32,8,256]{2,1,0:T(8,128)(2,1)S(1)} collective-permute-done((bf16[32,8,256]{2,1,0:T(8,128)(2,1)S(1)}, bf16[32,8,256]{2,1,0:T(8,128)(2,1)S(1)}, u32[]{:S(2)}, u32[]{:S(2)}) %collective-permute-start.3) | collective-permute-done | bytes 131104 | tf_op jit(solution)/shard_map/ppermute | solution.py:20
  45.6 47.2 %while.10 = (s32[]{:T(128)}, bf16[12,8,8,16,128]{4,3,2,1,0:T(8,128)(2,1)}, bf16[12,8,8,32]{3,2,1,0:T(8,128)(2,1)}, bf16[32,48,272]{2,1,0:T(8,128)(2,1)S(1)}, bf1...) while((s32[]{:T(128)}, ...), condition=%wide.region_1.2_spmd, body=%wide.region_0.1_spmd.sunk | while | flops 152059904 | bytes 5048417 | solution.py:69
  45.6 1.5 fusion.47
  47.1 2.5 %fusion.48 = bf16[12,8,8,16,128]{4,3,2,1,0:T(8,128)(2,1)} fusion(bf16[12,8,8,16,128]{4,3,2,1,0:T(8,128)(2,1)} %get-tuple-element.159, s32[]{:T(128)S(6)} %copy.55, bf16[8,8,48,272]{3,1,2,0:T(8,128)(2,1)S(1)} %fusion.47, bf16[12,8,128,272]{2,3,1,0:T(8,128)(2,1)} %get-tuple-element.171, f32[8,16]{1,0:T(8,128)S(1)} %get-tuple-element.172, ...), kind=kOutput, calls=%fused_computation.10.clone.1 | convolution fusion | flops 98582528 | bytes 2525184 | tf_op jit(solution)/shard_map/while/body/eval_jaxpr/cut,cost->cosu/dot_general | solution.py:66
  49.6 1.5 fusion.47
  51.0 2.5 %fusion.48 = bf16[12,8,8,16,128]{4,3,2,1,0:T(8,128)(2,1)} fusion(bf16[12,8,8,16,128]{4,3,2,1,0:T(8,128)(2,1)} %get-tuple-element.159, s32[]{:T(128)S(6)} %copy.55, bf16[8,8,48,272]{3,1,2,0:T(8,128)(2,1)S(1)} %fusion.47, bf16[12,8,128,272]{2,3,1,0:T(8,128)(2,1)} %get-tuple-element.171, f32[8,16]{1,0:T(8,128)S(1)} %get-tuple-element.172, ...), kind=kOutput, calls=%fused_computation.10.clone.1 | convolution fusion | flops 98582528 | bytes 2525184 | tf_op jit(solution)/shard_map/while/body/eval_jaxpr/cut,cost->cosu/dot_general | solution.py:66
  53.5 1.5 fusion.47
  55.0 2.5 %fusion.48 = bf16[12,8,8,16,128]{4,3,2,1,0:T(8,128)(2,1)} fusion(bf16[12,8,8,16,128]{4,3,2,1,0:T(8,128)(2,1)} %get-tuple-element.159, s32[]{:T(128)S(6)} %copy.55, bf16[8,8,48,272]{3,1,2,0:T(8,128)(2,1)S(1)} %fusion.47, bf16[12,8,128,272]{2,3,1,0:T(8,128)(2,1)} %get-tuple-element.171, f32[8,16]{1,0:T(8,128)S(1)} %get-tuple-element.172, ...), kind=kOutput, calls=%fused_computation.10.clone.1 | convolution fusion | flops 98582528 | bytes 2525184 | tf_op jit(solution)/shard_map/while/body/eval_jaxpr/cut,cost->cosu/dot_general | solution.py:66
  57.4 1.5 fusion.47
  58.9 2.5 %fusion.48 = bf16[12,8,8,16,128]{4,3,2,1,0:T(8,128)(2,1)} fusion(bf16[12,8,8,16,128]{4,3,2,1,0:T(8,128)(2,1)} %get-tuple-element.159, s32[]{:T(128)S(6)} %copy.55, bf16[8,8,48,272]{3,1,2,0:T(8,128)(2,1)S(1)} %fusion.47, bf16[12,8,128,272]{2,3,1,0:T(8,128)(2,1)} %get-tuple-element.171, f32[8,16]{1,0:T(8,128)S(1)} %get-tuple-element.172, ...), kind=kOutput, calls=%fused_computation.10.clone.1 | convolution fusion | flops 98582528 | bytes 2525184 | tf_op jit(solution)/shard_map/while/body/eval_jaxpr/cut,cost->cosu/dot_general | solution.py:66
  61.4 1.5 fusion.47
  62.8 2.5 %fusion.48 = bf16[12,8,8,16,128]{4,3,2,1,0:T(8,128)(2,1)} fusion(bf16[12,8,8,16,128]{4,3,2,1,0:T(8,128)(2,1)} %get-tuple-element.159, s32[]{:T(128)S(6)} %copy.55, bf16[8,8,48,272]{3,1,2,0:T(8,128)(2,1)S(1)} %fusion.47, bf16[12,8,128,272]{2,3,1,0:T(8,128)(2,1)} %get-tuple-element.171, f32[8,16]{1,0:T(8,128)S(1)} %get-tuple-element.172, ...), kind=kOutput, calls=%fused_computation.10.clone.1 | convolution fusion | flops 98582528 | bytes 2525184 | tf_op jit(solution)/shard_map/while/body/eval_jaxpr/cut,cost->cosu/dot_general | solution.py:66
  65.3 1.5 fusion.47
  66.8 2.5 %fusion.48 = bf16[12,8,8,16,128]{4,3,2,1,0:T(8,128)(2,1)} fusion(bf16[12,8,8,16,128]{4,3,2,1,0:T(8,128)(2,1)} %get-tuple-element.159, s32[]{:T(128)S(6)} %copy.55, bf16[8,8,48,272]{3,1,2,0:T(8,128)(2,1)S(1)} %fusion.47, bf16[12,8,128,272]{2,3,1,0:T(8,128)(2,1)} %get-tuple-element.171, f32[8,16]{1,0:T(8,128)S(1)} %get-tuple-element.172, ...), kind=kOutput, calls=%fused_computation.10.clone.1 | convolution fusion | flops 98582528 | bytes 2525184 | tf_op jit(solution)/shard_map/while/body/eval_jaxpr/cut,cost->cosu/dot_general | solution.py:66
  69.2 1.5 fusion.47
  70.7 2.5 %fusion.48 = bf16[12,8,8,16,128]{4,3,2,1,0:T(8,128)(2,1)} fusion(bf16[12,8,8,16,128]{4,3,2,1,0:T(8,128)(2,1)} %get-tuple-element.159, s32[]{:T(128)S(6)} %copy.55, bf16[8,8,48,272]{3,1,2,0:T(8,128)(2,1)S(1)} %fusion.47, bf16[12,8,128,272]{2,3,1,0:T(8,128)(2,1)} %get-tuple-element.171, f32[8,16]{1,0:T(8,128)S(1)} %get-tuple-element.172, ...), kind=kOutput, calls=%fused_computation.10.clone.1 | convolution fusion | flops 98582528 | bytes 2525184 | tf_op jit(solution)/shard_map/while/body/eval_jaxpr/cut,cost->cosu/dot_general | solution.py:66
  74.6 2.5 %fusion.48 = bf16[12,8,8,16,128]{4,3,2,1,0:T(8,128)(2,1)} fusion(bf16[12,8,8,16,128]{4,3,2,1,0:T(8,128)(2,1)} %get-tuple-element.159, s32[]{:T(128)S(6)} %copy.55, bf16[8,8,48,272]{3,1,2,0:T(8,128)(2,1)S(1)} %fusion.47, bf16[12,8,128,272]{2,3,1,0:T(8,128)(2,1)} %get-tuple-element.171, f32[8,16]{1,0:T(8,128)S(1)} %get-tuple-element.172, ...), kind=kOutput, calls=%fused_computation.10.clone.1 | convolution fusion | flops 98582528 | bytes 2525184 | tf_op jit(solution)/shard_map/while/body/eval_jaxpr/cut,cost->cosu/dot_general | solution.py:66
  77.1 1.5 fusion.47
  78.6 2.5 %fusion.48 = bf16[12,8,8,16,128]{4,3,2,1,0:T(8,128)(2,1)} fusion(bf16[12,8,8,16,128]{4,3,2,1,0:T(8,128)(2,1)} %get-tuple-element.159, s32[]{:T(128)S(6)} %copy.55, bf16[8,8,48,272]{3,1,2,0:T(8,128)(2,1)S(1)} %fusion.47, bf16[12,8,128,272]{2,3,1,0:T(8,128)(2,1)} %get-tuple-element.171, f32[8,16]{1,0:T(8,128)S(1)} %get-tuple-element.172, ...), kind=kOutput, calls=%fused_computation.10.clone.1 | convolution fusion | flops 98582528 | bytes 2525184 | tf_op jit(solution)/shard_map/while/body/eval_jaxpr/cut,cost->cosu/dot_general | solution.py:66
  82.5 2.5 %fusion.48 = bf16[12,8,8,16,128]{4,3,2,1,0:T(8,128)(2,1)} fusion(bf16[12,8,8,16,128]{4,3,2,1,0:T(8,128)(2,1)} %get-tuple-element.159, s32[]{:T(128)S(6)} %copy.55, bf16[8,8,48,272]{3,1,2,0:T(8,128)(2,1)S(1)} %fusion.47, bf16[12,8,128,272]{2,3,1,0:T(8,128)(2,1)} %get-tuple-element.171, f32[8,16]{1,0:T(8,128)S(1)} %get-tuple-element.172, ...), kind=kOutput, calls=%fused_computation.10.clone.1 | convolution fusion | flops 98582528 | bytes 2525184 | tf_op jit(solution)/shard_map/while/body/eval_jaxpr/cut,cost->cosu/dot_general | solution.py:66
  86.4 2.5 %fusion.48 = bf16[12,8,8,16,128]{4,3,2,1,0:T(8,128)(2,1)} fusion(bf16[12,8,8,16,128]{4,3,2,1,0:T(8,128)(2,1)} %get-tuple-element.159, s32[]{:T(128)S(6)} %copy.55, bf16[8,8,48,272]{3,1,2,0:T(8,128)(2,1)S(1)} %fusion.47, bf16[12,8,128,272]{2,3,1,0:T(8,128)(2,1)} %get-tuple-element.171, f32[8,16]{1,0:T(8,128)S(1)} %get-tuple-element.172, ...), kind=kOutput, calls=%fused_computation.10.clone.1 | convolution fusion | flops 98582528 | bytes 2525184 | tf_op jit(solution)/shard_map/while/body/eval_jaxpr/cut,cost->cosu/dot_general | solution.py:66
  90.4 2.5 %fusion.48 = bf16[12,8,8,16,128]{4,3,2,1,0:T(8,128)(2,1)} fusion(bf16[12,8,8,16,128]{4,3,2,1,0:T(8,128)(2,1)} %get-tuple-element.159, s32[]{:T(128)S(6)} %copy.55, bf16[8,8,48,272]{3,1,2,0:T(8,128)(2,1)S(1)} %fusion.47, bf16[12,8,128,272]{2,3,1,0:T(8,128)(2,1)} %get-tuple-element.171, f32[8,16]{1,0:T(8,128)S(1)} %get-tuple-element.172, ...), kind=kOutput, calls=%fused_computation.10.clone.1 | convolution fusion | flops 98582528 | bytes 2525184 | tf_op jit(solution)/shard_map/while/body/eval_jaxpr/cut,cost->cosu/dot_general | solution.py:66
  92.8 4.1 %reshape_reshape.3 = bf16[96,16384]{1,0:T(8,128)(2,1)S(1)} reshape(bf16[12,8,8,16,128]{4,3,2,1,0:T(8,128)(2,1)} %get-tuple-element.39) | data formatting | bytes 6291456 | tf_op jit(solution)/shard_map/reshape;reshape | solution.py:72
  97.9 61.1 %all-reduce = (f32[96,96]{0,1:T(8,128)S(1)}, f32[]{:T(128)}) all-reduce(f32[96,96]{0,1:T(8,128)S(1)} %fusion.32, f32[]{:T(128)S(6)} %mul.321), channel_id=1, replica_groups=mesh['survey'=2,'inline'=4,'xline'=2,'depth'=2] {'inline','xline','depth'}, use_global_device_ids=true, to_apply=%region_2.3 | all-reduce | flops 9217 | bytes 73736 | tf_op jit(solution)/shard_map/psum | solution.py:75
  160.5 8.8 %cholesky.17 = f32[96,96]{1,0:T(8,128)S(1)} custom-call(f32[96,96]{1,0:T(8,128)S(1)} %fusion.23), custom_call_target="Cholesky" | custom-call | tf_op jit(solution)/shard_map/jit(cholesky)/cholesky | solution.py:76
  171.3 7.4 %custom-call.7 = f32[1,96,96]{1,2,0:T(8,128)S(1)} custom-call(f32[1,96,96]{2,1,0:T(8,128)S(1)} %get-tuple-element.82), custom_call_target="InvertDiagBlocksLowerTriangular" | custom-call | tf_op jit(solution)/shard_map/jit(_solve_triangular)/triangular_solve | solution.py:77
  179.9 2.6 %copy.23 = bf16[12,8,128,128]{3,2,1,0:T(8,128)(2,1)} copy(bf16[12,8,128,128]{3,1,2,0:T(8,128)(2,1)S(1)} %fusion.21) | data formatting | bytes 6291456
  (63 shorter events, 24.5 us)
Async XLA Ops:
  2.4 26.9 %collective-permute-start = (bf16[8,32,256]{2,1,0:T(8,128)(2,1)S(1)}, bf16[8,32,256]{2,1,0:T(8,128)(2,1)S(1)}, u32[]{:S(2)}, u32[]{:S(2)}) collective-permute-start(bf16[8,32,256]{2,1,0:T(8,128)(2,1)S(1)} %get-tuple-element.79), channel_id=1, source_target_pairs={{0,4},{4,8},{8,12},{1,5},{5,9},{9,13},{2,6},{6,10},{10,14},{3,7},{... | collective-permute-start | bytes 393224 | tf_op jit(solution)/shard_map/ppermute | solution.py:19
  7.4 21.9 %collective-permute-start.1 = (bf16[8,32,256]{2,1,0:T(8,128)(2,1)S(1)}, bf16[8,32,256]{2,1,0:T(8,128)(2,1)S(1)}, u32[]{:S(2)}, u32[]{:S(2)}) collective-permute-start(bf16[8,32,256]{2,1,0:T(8,128)(2,1)S(1)} %get-tuple-element.80), channel_id=1, source_target_pairs={{4,0},{8,4},{12,8},{5,1},{9,5},{13,9},{6,2},{10,6},{14,10},{7,3},{... | collective-permute-start | bytes 393224 | tf_op jit(solution)/shard_map/ppermute | solution.py:20
  29.3 7.2 %collective-permute-start.2 = (bf16[32,8,256]{2,1,0:T(8,128)(2,1)S(1)}, bf16[32,8,256]{2,1,0:T(8,128)(2,1)S(1)}, u32[]{:S(2)}, u32[]{:S(2)}) collective-permute-start(bf16[32,8,256]{2,1,0:T(8,128)(2,1)S(1)} %get-tuple-element.77), channel_id=1, source_target_pairs={{0,2},{1,3},{4,6},{5,7},{8,10},{9,11},{12,14},{13,15},{16,18},{17,... | collective-permute-start | bytes 393224 | tf_op jit(solution)/shard_map/ppermute | solution.py:19
  32.8 6.9 %collective-permute-start.3 = (bf16[32,8,256]{2,1,0:T(8,128)(2,1)S(1)}, bf16[32,8,256]{2,1,0:T(8,128)(2,1)S(1)}, u32[]{:S(2)}, u32[]{:S(2)}) collective-permute-start(bf16[32,8,256]{2,1,0:T(8,128)(2,1)S(1)} %get-tuple-element.78), channel_id=1, source_target_pairs={{2,0},{3,1},{6,4},{7,5},{10,8},{11,9},{14,12},{15,13},{18,16},{19,... | collective-permute-start | bytes 393224 | tf_op jit(solution)/shard_map/ppermute | solution.py:20
  39.9 3.9 %collective-permute-start.4 = (bf16[32,48,8]{2,1,0:T(8,128)(2,1)S(1)}, bf16[32,48,8]{2,1,0:T(8,128)(2,1)S(1)}, u32[]{:S(2)}, u32[]{:S(2)}) collective-permute-start(bf16[32,48,8]{2,1,0:T(8,128)(2,1)S(1)} %get-tuple-element.75), channel_id=1, source_target_pairs={{0,1},{2,3},{4,5},{6,7},{8,9},{10,11},{12,13},{14,15},{16,17},{18,... | collective-permute-start | bytes 73736 | tf_op jit(solution)/shard_map/ppermute | solution.py:19
  41.2 3.6 %collective-permute-start.5 = (bf16[32,48,8]{2,1,0:T(8,128)(2,1)S(1)}, bf16[32,48,8]{2,1,0:T(8,128)(2,1)S(1)}, u32[]{:S(2)}, u32[]{:S(2)}) collective-permute-start(bf16[32,48,8]{2,1,0:T(8,128)(2,1)S(1)} %get-tuple-element.76), channel_id=1, source_target_pairs={{1,0},{3,2},{5,4},{7,6},{9,8},{11,10},{13,12},{15,14},{17,16},{19,... | collective-permute-start | bytes 73736 | tf_op jit(solution)/shard_map/ppermute | solution.py:20
where the time goes:
time: 184 us; the launch traced here: 182 us
  blocking collectives  61.1 us (33%)
  matrix products  49.3 us (27%)
  other arithmetic  42.2 us (23%)
  starting transfers between devices  13.5 us (7%)
  local copies, waits for them, and re-layouts  10.6 us (6%)
  waiting for transfers between devices  4.07 us (2%)
    psum x1, blocking collectives, local(): gram, count = lax.psum((gram, count), ('inline', 'xline', 'depth'))  61.1 us
    dot_general x12, matrix products, one_block(): jnp.einsum('cut,cost->cosu', time_mat, second, preferred_element_type=jnp...  29.5 us
    convert_element_type x3, other arithmetic, banded(): return total.astype(jnp.bfloat16)  19.7 us
    dot_general x12, matrix products, one_block(): jnp.einsum('cop,pqt->coqt', inline_mat, padded, preferred_element_type=jn...  17.6 us
    ppermute x3, starting transfers between devices, extended(): before = lax.ppermute(last, axis, up)  9.65 us
    another operation x3, other arithmetic, local(): lower = jnp.linalg.cholesky(gram / count)  9.45 us
    another operation x1, other arithmetic, local(): jax.scipy.linalg.solve_triangular(lower, jnp.eye(CHAN, dtype=jnp.float32)...  7.36 us
    another operation x1, local copies, waits for them, and re-layouts, local(): flat = attributes.reshape(CHAN, -1)  4.13 us
  transfers between devices with their start and end apart: 6, of which 2 were waited for; matrix products, arithmetic and copies ran while one was open for 13% of the time, Pallas kernels for 0%

commit v1 on v0

v1 whole, which is shorter than its diff:
```python
import functools

import jax
import jax.numpy as jnp
from jax import lax
from jax.experimental import pallas as pl
from jax.experimental.pallas import tpu as pltpu
from jax.sharding import PartitionSpec as P

ORIENT = 32
TAPS = 5
CHAN = 96
REACH = 8
KEPT = 5
F32 = jnp.float32
BF16 = jnp.bfloat16
VMEM_LIMIT = 56 * 1024 * 1024


def iota(shape, dim):
    return lax.broadcasted_iota(jnp.int32, shape, dim)


def rounded(value):
    return value.astype(BF16).astype(F32)


def ones_where(mask):
    return jnp.where(mask, 1.0, 0.0).astype(BF16)


def dot(a, b):
    return jnp.dot(a, b, preferred_element_type=F32)


def shifted(value, axis, step):
    size = lax.axis_size(axis)
    return lax.ppermute(value, axis, [(i, i + step) for i in range(size) if 0 <= i + step < size])


def swapped(value, axis, bit):
    size = lax.axis_size(axis)
    return lax.ppermute(value, axis, [(i, i ^ bit) for i in range(size)])


def summed(value, axes):
    other = None
    for axis in axes:
        size = lax.axis_size(axis)
        assert size & (size - 1) == 0
        bit = 1
        while bit < size:
            if other is not None:
                value = value + other
            other = swapped(value, axis, bit)
            bit *= 2
    return value, other


def halo_select(level, odd, stored, x_left, depth_first):
    dilation = 2 ** level
    rows, cols = 256, TAPS * 128
    lane = iota((1, cols), 1)
    k = lane // 128
    within = lane % 128
    place = (within + 4) % 8 - 4
    q = ((within + 4) // 8) % 16
    j = 2 * q + dilation * (k - 2)
    slot = jnp.where(j < 0, 40 + j, j)
    if stored == 48:
        slot = jnp.where(j >= 32, j + 8, slot)
    else:
        slot = jnp.where((j < 0) & (x_left == 0), -999999, slot)
        slot = jnp.where((j >= 32) & (x_left == 1), -999999, slot)
    if odd:
        source = 4 * stored + slot
        source = jnp.where((place == -1) & (depth_first == 0), source, -1)
    else:
        source = jnp.where(place >= 0, place, place + 4) * stored + slot
        source = jnp.where((place >= 0) & (depth_first == 0), -1, source)
        source = jnp.where((place < 0) & (depth_first == 1), -1, source)
    return ones_where(iota((rows, cols), 0) == source)


def attributes_kernel(
    two_sided, place_ref, live_smem, live_ref, taps_ref, own_ref, before_ref, after_ref, xh_ref, dh_ref,
    attr_ref, gram_ref, bands, first0, first12, halo2, w2, w3, planes,
):
    x_left = place_ref[0]
    depth_first = place_ref[1]
    stored = 48 if two_sided else 40

    for k in range(TAPS):
        w2[k] = jnp.broadcast_to(taps_ref[1, :, k : k + 1], (CHAN, 128))
        w3[k] = jnp.broadcast_to(taps_ref[2, :, k : k + 1], (CHAN, 128))
    lane32 = iota((ORIENT, 128), 1)
    for level in range(3):
        cs = slice(level * ORIENT, (level + 1) * ORIENT)
        cols = [jnp.broadcast_to(taps_ref[0, cs, k : k + 1], (ORIENT, 128)) for k in range(TAPS)]
        for o in range(8):
            total = jnp.zeros((ORIENT, 128), F32)
            for k in range(TAPS):
                total = jnp.where(lane32 == REACH + 2 * o + 2 ** level * (k - 2), cols[k], total)
            bands[pl.ds(level * 256 + o * ORIENT, ORIENT), :] = total.astype(BF16)

    n = iota((256, 256), 1)
    pick = ones_where(iota((256, 256), 0) == jnp.where(n < 128, 2 * n, 2 * n - 255))
    r = iota((512, 512), 0)
    c = iota((512, 512), 1)
    turn = ones_where((c // 16 == r % 32) & (c % 16 == r // 32))
    own = dot(own_ref[...], pick).astype(BF16).reshape(16, 32, 256)
    before = dot(before_ref[...], pick).astype(BF16).reshape(8, 32, 256)
    after = dot(after_ref[...], pick).astype(BF16).reshape(8, 32, 256)
    for half in range(2):
        js = slice(half * 16, half * 16 + 16)
        block = jnp.concatenate([before[:, js], own[:, js], after[:, js]], axis=0).reshape(512, 256)
        planes[8 + half * 16 : 24 + half * 16] = dot(turn, block).astype(BF16).reshape(16, 32, 256)
    turn_x = ones_where((c % 256 // 8 == r % 32) & (c // 256 * 8 + c % 8 == r // 32))
    if two_sided:
        sides = dot(xh_ref[...], pick).astype(BF16)
    else:
        got = dot(xh_ref[...], pick)
        left = jnp.where(x_left == 1, 1.0, 0.0)
        sides = jnp.concatenate([got * left, got * (1.0 - left)], axis=0).astype(BF16)
    edges = dot(turn_x, sides).astype(BF16).reshape(16, 32, 256)
    planes[0:8] = edges[0:8]
    planes[40:48] = edges[8:16]

    a0 = bands[0:256, 0:32]
    a12 = bands[256:768, 0:32]

    def level0_first(j, _):
        first0[j] = rounded(dot(a0, planes[j + 6]))
        return 0

    lax.fori_loop(0, 35, level0_first, 0)

    def even_first(pair, _):
        both = jnp.concatenate([planes[4 * pair, :, 0:128], planes[4 * pair + 2, :, 0:128]], axis=1)
        out = rounded(dot(a12, both))
        first12[2 * pair] = out[:, 0:128]
        first12[2 * pair + 1] = out[:, 128:256]
        return 0

    lax.fori_loop(0, 12, even_first, 0)

    for index, (level, odd) in enumerate(((0, False), (0, True), (1, False), (2, False))):
        cols = dot(dh_ref[...], halo_select(level, odd, stored, x_left, depth_first)).astype(BF16)
        part = rounded(dot(bands[level * 256 : level * 256 + 256, 0:32], cols))
        cs = slice(level * ORIENT, (level + 1) * ORIENT)
        total = jnp.zeros((256, 128), F32)
        for k in range(TAPS):
            total = total + part[:, k * 128 : k * 128 + 128] * jnp.concatenate([w2[k, cs]] * 8, axis=0)
        halo2[index] = rounded(total)
    lane256 = iota((256, 128), 1)
    w3_0, w3_1, w3_4 = [jnp.concatenate([w3[k, 0:ORIENT]] * 8, axis=0) for k in (0, 1, 4)]
    halo2[0] = jnp.where(lane256 % 8 == 7, halo2[0] * w3_0 + halo2[1] * w3_1, halo2[0] * w3_4)

    lane = iota((16, 128), 1)

    def tap_rows(ref, level, c16):
        start = pl.multiple_of(level * ORIENT + c16 * 16, 16)
        return [ref[k, pl.ds(start, 16), :] for k in range(TAPS)], start

    def rolled(value, shift):
        return pltpu.roll(value, shift % 128, 1) if shift % 128 else value

    def level0_rest(step, _):
        o, c16 = step // 2, step % 2
        rows = pl.ds(pl.multiple_of(o * ORIENT + c16 * 16, 16), 16)
        s2, start = tap_rows(w2, 0, c16)
        s3, _ = tap_rows(w3, 0, c16)
        halo = halo2[0, rows, :]
        for q in range(16):
            even = sum(s2[k] * first0[2 * q + k, rows, 0:128] for k in range(TAPS))
            odd = sum(s2[k] * first0[2 * q + k, rows, 128:256] for k in range(TAPS))
            even, odd = rounded(even), rounded(odd)
            mine = rolled(halo, -8 * q)
            back = jnp.where(lane == 127, mine, s3[0] * even + s3[1] * odd)
            ahead = jnp.where(lane == 0, mine, s3[4] * even)
            total = s3[2] * even + s3[3] * odd + rolled(back, 1) + rolled(ahead, -1)
            total = total * live_smem[2 * o, 2 * q].astype(F32)
            attr_ref[o * 16 + q, pl.ds(start, 16), :] = total.astype(BF16)
        return 0

    lax.fori_loop(0, 16, level0_rest, 0)

    def even_rest(level):
        unit = 2 ** (level - 1)

        def body(step, _):
            o, c16 = step // 2, step % 2
            rows = pl.ds(pl.multiple_of((level - 1) * 256 + o * ORIENT + c16 * 16, 16), 16)
            halo_rows = pl.ds(pl.multiple_of(o * ORIENT + c16 * 16, 16), 16)
            s2, start = tap_rows(w2, level, c16)
            s3, _ = tap_rows(w3, level, c16)
            halo = halo2[level + 1, halo_rows, :]
            for q in range(16):
                value = rounded(sum(s2[k] * first12[q + 4 + unit * (k - 2), rows, :] for k in range(TAPS)))
                mine = rolled(halo, -8 * q)
                total = s3[2] * value
                for k in (0, 1, 3, 4):
                    shift = unit * (k - 2)
                    edge = lane < shift if shift > 0 else lane >= 128 + shift
                    total = total + s3[k] * rolled(jnp.where(edge, mine, value), -shift)
                total = total * live_smem[2 * o, 2 * q].astype(F32)
                attr_ref[o * 16 + q, pl.ds(start, 16), :] = total.astype(BF16)
            return 0

        return body

    lax.fori_loop(0, 16, even_rest(1), 0)
    lax.fori_loop(0, 16, even_rest(2), 0)

    def add_gram(o, total):
        for q in range(0, 16, 2):
            both = jnp.concatenate([attr_ref[o * 16 + q], attr_ref[o * 16 + q + 1]], axis=1)
            total = total + lax.dot_general(
                both, both, (((1,), (1,)), ((), ())), preferred_element_type=F32
            )
        return total

    gram = lax.fori_loop(0, 8, add_gram, jnp.zeros((CHAN, CHAN), F32))
    alive = live_ref[...]
    chosen = (iota(alive.shape, 0) % 2 == 0) & (iota(alive.shape, 1) % 2 == 0)
    count = jnp.sum(jnp.where(chosen, alive.astype(F32), 0.0)) * 128.0
    gram_ref[...] = jnp.full((CHAN, 128), count, F32)
    gram_ref[:, 0:CHAN] = gram


def whiten_kernel(mine_ref, other_ref, attr_ref, out_ref, factor_ref, inverse, kron):
    step = pl.program_id(0)

    @pl.when(step == 0)
    def _():
        total = mine_ref[...] + other_ref[...]
        lane = iota((8, 128), 1)
        sub = iota((8, 128), 0)
        count = jnp.broadcast_to(total[0:1, CHAN : CHAN + 1], (8, 128))
        blocks = []
        for g in range(CHAN // 8):
            blocks.append(jnp.where(lane < CHAN, total[8 * g : 8 * g + 8] / count, 0.0))
        row_lane = iota((1, 128), 1)
        for j in range(CHAN):
            g, s = j // 8, j % 8
            row = blocks[g][s : s + 1, :]
            pivot = row[:, j : j + 1]
            scale = lax.rsqrt(pivot)
            recip = 1.0 / pivot
            factor_ref[j : j + 1, :] = (jnp.where(row_lane >= j, row, 0.0) * scale)[:, 0:CHAN]
            unit = jnp.where(row_lane == j, 1.0, row)
            inverse[j : j + 1, :] = jnp.where(row_lane <= j, unit, 0.0) * scale
            if j == CHAN - 1:
                break
            scaled_row = unit * recip
            for h in range(g, CHAN // 8):
                col = blocks[h][:, j : j + 1]
                if h == g:
                    col = jnp.where(sub[:, 0:1] > s, col, 0.0)
                blocks[h] = jnp.where(lane == j, 0.0, blocks[h]) - col * scaled_row
        low = inverse[:, 0:CHAN].astype(BF16)
        spread = ones_where(iota((CHAN, 768), 0) == iota((CHAN, 768), 1) % CHAN)
        wide = dot(low, spread).astype(BF16)
        tall = ones_where(iota((768, CHAN), 0) // 8 == iota((768, CHAN), 1))
        full = dot(tall, wide)
        keep = iota((768, 768), 0) % 8 == iota((768, 768), 1) // CHAN
        kron[...] = jnp.where(keep, full, 0.0).astype(BF16)

    weights = kron[...]
    halves = []
    for half in range(2):
        pair = [
            attr_ref[pl.ds((2 * step + i) * 16 + 8 * half, 8)].reshape(768, 128) for i in range(2)
        ]
        halves.append(dot(weights, jnp.concatenate(pair, axis=1)))
    for i in range(2):
        both = [half[:, i * 128 : i * 128 + 128].reshape(CHAN, 8, 128) for half in halves]
        out_ref[:, i] = jnp.concatenate(both, axis=1).astype(BF16)


def local(seismic, trace_live, filter_taps):
    il_len, xl_len, t_len = seismic.shape
    assert (il_len, xl_len, t_len) == (16, 32, 256) and lax.axis_size("depth") == 2
    live = seismic * trace_live.astype(BF16)[:, :, None]
    taps = filter_taps.astype(F32)
    x_index = lax.axis_index("xline")
    d_index = lax.axis_index("depth")
    two_sided = lax.axis_size("xline") > 2

    before = shifted(live[il_len - REACH :], "inline", 1)
    after = shifted(live[:REACH], "inline", -1)

    def stack(js):
        return jnp.concatenate([before[:, js], live[:, js], after[:, js]], axis=0)

    low, high = slice(0, REACH), slice(xl_len - REACH, xl_len)
    if two_sided:
        xh = [shifted(stack(high), "xline", 1), shifted(stack(low), "xline", -1)]
    else:
        xh = [swapped(jnp.where(x_index == 0, stack(high), stack(low)), "xline", 1)]
    whole = jnp.concatenate([jnp.concatenate([before, live, after], axis=0)] + xh, axis=1)
    last = jnp.concatenate(
        [whole[:, :, t] for t in (t_len - 8, t_len - 6, t_len - 4, t_len - 2, t_len - 1)], axis=1
    )
    initial = jnp.concatenate([whole[:, :, t] for t in (0, 2, 4, 6, 7)], axis=1)
    dh = jnp.where(d_index == 0, last, initial)
    dh = jnp.pad(dh, ((0, 0), (0, 256 - dh.shape[1])))
    dh = swapped(dh, "depth", 1)

    place = jnp.stack([(x_index == 1).astype(jnp.int32), (d_index == 0).astype(jnp.int32)])
    vmem = pl.BlockSpec(memory_space=pltpu.VMEM)
    smem = pl.BlockSpec(memory_space=pltpu.SMEM)
    xrows = jnp.concatenate([x.reshape(256, t_len) for x in xh], axis=0)
    attr, gram = pl.pallas_call(
        functools.partial(attributes_kernel, two_sided),
        out_shape=(
            jax.ShapeDtypeStruct((128, CHAN, 128), BF16),
            jax.ShapeDtypeStruct((CHAN, 128), F32),
        ),
        in_specs=[smem, smem] + [vmem] * 7,
        out_specs=(vmem, vmem),
        scratch_shapes=[
            pltpu.VMEM((768, 128), BF16),
            pltpu.VMEM((35, 256, 256), F32),
            pltpu.VMEM((24, 512, 128), F32),
            pltpu.VMEM((4, 256, 128), F32),
            pltpu.VMEM((TAPS, CHAN, 128), F32),
            pltpu.VMEM((TAPS, CHAN, 128), F32),
            pltpu.VMEM((48, 32, 256), BF16),
        ],
        compiler_params=pltpu.CompilerParams(vmem_limit_bytes=VMEM_LIMIT),
        name="attributes",
    )(
        place, trace_live, trace_live, taps, live.reshape(512, t_len),
        before.reshape(256, t_len), after.reshape(256, t_len), xrows, dh,
    )

    mine, other = summed(gram, ("depth", "xline", "inline"))
    out, factor = pl.pallas_call(
        whiten_kernel,
        grid=(4,),
        out_shape=(
            jax.ShapeDtypeStruct((CHAN, 8, 16, 128), BF16),
            jax.ShapeDtypeStruct((CHAN, CHAN), F32),
        ),
        in_specs=[vmem] * 3,
        out_specs=(
            pl.BlockSpec((CHAN, 2, 16, 128), lambda i: (0, i, 0, 0)),
            pl.BlockSpec((CHAN, CHAN), lambda i: (0, 0)),
        ),
        scratch_shapes=[pltpu.VMEM((CHAN, 128), F32), pltpu.VMEM((768, 768), BF16)],
        compiler_params=pltpu.CompilerParams(vmem_limit_bytes=VMEM_LIMIT),
        name="whiten",
    )(mine, other, attr)
    return out, factor


def solution(mesh):
    placed = (P(("survey", "inline"), "xline", "depth"), P(("survey", "inline"), "xline"), P())
    return jax.shard_map(
        local,
        mesh=mesh,
        in_specs=placed,
        out_specs=(P(None, ("survey", "inline"), "xline", "depth"), P("survey", None)),
        check_vma=False,
    )
```

time: 184 us -> 87.6 us (0.48)
  blocking collectives: 61.1 us -> 0 us
  matrix products: 49.3 us -> 0 us
  Pallas kernels: 0 us -> 46.4 us
  other arithmetic: 42.2 us -> 3.34 us
  waiting for transfers between devices: 4.07 us -> 13.6 us
  local copies, waits for them, and re-layouts: 10.6 us -> 6.55 us
  starting transfers between devices: 13.5 us -> 16.7 us
    psum x1 -> x0, blocking collectives: 61.1 us -> none  [local(): gram, count = lax.psum((gram, count), ('inline', 'xline', 'depth'))]
    dot_general x26 -> x0, matrix products: 49 us -> none  [the longest x12 29.5 us: one_block(): jnp.einsum('cut,cost->cosu', time_mat, second, preferred_element_type=jnp...]
    pallas_call x0 -> x2, Pallas kernels: none -> 46.4 us  [the longest x1 31.6 us: local(): pl.pallas_call(functools.partial(attributes_kernel, two_sided), out_shape...]
    convert_element_type x7 -> x1, other arithmetic: 20.4 us -> 0.7 us  [local(): live = seismic * trace_live.astype(BF16)[:, :, None]]
    another operation x4 -> x1, other arithmetic: 16.8 us -> 0.65 us  [local(): jnp.stack([(x_index == 1).astype(jnp.int32), (d_index == 0).astype(jnp.in...]
    ppermute x6 -> x8, waiting for transfers between devices: 4.07 us -> 13.6 us  [the longest x6 10.9 us: swapped(): return lax.ppermute(value, axis, [(i, i ^ bit) for i in range(size)])]
    another operation x1 -> x0, local copies, waits for them, and re-layouts: 4.13 us -> none  [local(): flat = attributes.reshape(CHAN, -1)]
    ppermute x6 -> x8, starting transfers between devices: 13.5 us -> 16.7 us  [the longest x6 9.81 us: swapped(): return lax.ppermute(value, axis, [(i, i ^ bit) for i in range(size)])]
  transfers between devices with their start and end apart: 6 -> 8, of which waited for: 2 -> 7; matrix products, arithmetic and copies ran while one was open for 13% -> 2% of each run, Pallas kernels for 0% -> 0%
where the time goes in v1:
time: 87.6 us; the launch traced here: 87.3 us
  Pallas kernels  46.4 us (53%)
  starting transfers between devices  16.7 us (19%)
  waiting for transfers between devices  13.6 us (16%)
  local copies, waits for them, and re-layouts  6.55 us (7%)
  other arithmetic  3.34 us (4%)
    pallas_call x1, Pallas kernels, local(): pl.pallas_call(functools.partial(attributes_kernel, two_sided), out_shape...  31.6 us
    pallas_call x1, Pallas kernels, local(): pl.pallas_call(whiten_kernel, grid=(4,), out_shape=(jax.ShapeDtypeStruct(...  14.8 us
    ppermute x6, waiting for transfers between devices, swapped(): return lax.ppermute(value, axis, [(i, i ^ bit) for i in range(size)])  10.9 us
    ppermute x6, starting transfers between devices, swapped(): return lax.ppermute(value, axis, [(i, i ^ bit) for i in range(size)])  9.81 us
    ppermute x2, starting transfers between devices, shifted(): lax.ppermute(value, axis, [(i, i + step) for i in range(size) if 0 <= i +...  6.86 us
    unnamed x26, local copies, waits for them, and re-layouts  4.68 us
    ppermute x2, waiting for transfers between devices, shifted(): lax.ppermute(value, axis, [(i, i + step) for i in range(size) if 0 <= i +...  2.69 us
  transfers between devices with their start and end apart: 8, of which 7 were waited for; matrix products, arithmetic and copies ran while one was open for 2% of the time, Pallas kernels for 0%

profile of v1, /device:TPU:0, one launch (start us, length us, event | category | flops | bytes accessed | tf_op | source)
XLA Modules:
  0.0 87.3 jit_solution(15230104941429034192)
XLA Ops:
  0.6 0.7 convert_element_type.11
  1.3 1.1 %broadcast_multiply_fusion = bf16[16,32,256]{2,1,0:T(8,128)(2,1)S(1)} fusion(bf16[16,32,256]{2,1,0:T(8,128)(2,1)} %param.3, bf16[16,32]{1,0:T(8,128)(2,1)S(1)} %convert_element_type.11), kind=kLoop, calls=%fused_computation.2 | loop fusion | flops 131072 | bytes 525312 | tf_op jit(solution)/shard_map/mul | solution.py:284
  2.5 1.3 %collective-permute-start.1 = (bf16[8,32,256]{2,1,0:T(8,128)(2,1)S(1)}, bf16[8,32,256]{2,1,0:T(8,128)(2,1)S(1)}, u32[]{:S(2)}, u32[]{:S(2)}) collective-permute-start(bf16[8,32,256]{2,1,0:T(8,128)(2,1)S(1)} %get-tuple-element.18), channel_id=1, source_target_pairs={{4,0},{8,4},{12,8},{5,1},{9,5},{13,9},{6,2},{10,6},{14,10},{7,3},{... | collective-permute-start | bytes 393224 | tf_op jit(solution)/shard_map/ppermute | solution.py:38
  3.8 5.6 %collective-permute-start = (bf16[8,32,256]{2,1,0:T(8,128)(2,1)S(1)}, bf16[8,32,256]{2,1,0:T(8,128)(2,1)S(1)}, u32[]{:S(2)}, u32[]{:S(2)}) collective-permute-start(bf16[8,32,256]{2,1,0:T(8,128)(2,1)S(1)} %get-tuple-element.19), channel_id=1, source_target_pairs={{0,4},{4,8},{8,12},{1,5},{5,9},{9,13},{2,6},{6,10},{10,14},{3,7},{... | collective-permute-start | bytes 393224 | tf_op jit(solution)/shard_map/ppermute | solution.py:38
  9.4 1.5 %collective-permute-done.1 = bf16[8,32,256]{2,1,0:T(8,128)(2,1)S(1)} collective-permute-done((bf16[8,32,256]{2,1,0:T(8,128)(2,1)S(1)}, bf16[8,32,256]{2,1,0:T(8,128)(2,1)S(1)}, u32[]{:S(2)}, u32[]{:S(2)}) %collective-permute-start.1) | collective-permute-done | bytes 131104 | tf_op jit(solution)/shard_map/ppermute | solution.py:38
  10.9 1.2 %collective-permute-done = bf16[8,32,256]{2,1,0:T(8,128)(2,1)S(1)} collective-permute-done((bf16[8,32,256]{2,1,0:T(8,128)(2,1)S(1)}, bf16[8,32,256]{2,1,0:T(8,128)(2,1)S(1)}, u32[]{:S(2)}, u32[]{:S(2)}) %collective-permute-start) | collective-permute-done | bytes 131104 | tf_op jit(solution)/shard_map/ppermute | solution.py:38
  12.1 1.8 %collective-permute-start.2 = (bf16[32,8,256]{2,1,0:T(8,128)(2,1)S(1)}, bf16[32,8,256]{2,1,0:T(8,128)(2,1)S(1)}, u32[]{:S(2)}, u32[]{:S(2)}) collective-permute-start(bf16[32,8,256]{2,1,0:T(8,128)(2,1)S(1)} %maximum_select_fusion), channel_id=1, source_target_pairs={{0,2},{2,0},{1,3},{3,1},{4,6},{6,4},{5,7},{7,5},{8,10},{10,8},{9,1... | collective-permute-start | bytes 393224 | tf_op jit(solution)/shard_map/ppermute | solution.py:43
  13.9 3.3 %collective-permute-done.2 = bf16[32,8,256]{2,1,0:T(8,128)(2,1)S(1)} collective-permute-done((bf16[32,8,256]{2,1,0:T(8,128)(2,1)S(1)}, bf16[32,8,256]{2,1,0:T(8,128)(2,1)S(1)}, u32[]{:S(2)}, u32[]{:S(2)}) %collective-permute-start.2) | collective-permute-done | bytes 131104 | tf_op jit(solution)/shard_map/ppermute | solution.py:43
  17.1 0.6 copy-done.3
  17.8 0.8 fusion
  19.2 0.3 copy.46
  19.5 0.3 copy.45
  19.8 0.3 copy.44
  20.1 0.3 copy.43
  20.4 0.3 copy.42
  20.7 0.3 copy.41
  20.9 0.3 copy.40
  21.8 0.7 add_convert_fusion.place_ref
  22.5 0.8 copy.38.taps_ref
  23.3 0.6 copy-done.6
  23.9 31.6 %attributes.1 = (bf16[128,96,128]{2,1,0:T(8,128)(2,1)}, f32[96,128]{1,0:T(8,128)}) custom-call(s32[2]{0:T(128)} %add_convert_fusion.place_ref, s32[16,32]{1,0:T(8,128)} %live_ref.1, s32[16,32]{1,0:T(8,128)} %live_ref.1, f32[3,96,5]{2,1,0:T(8,128)} %copy.38.taps_ref, bf16[512,256]{1,0:T(8,128)(2,1)} %bitcast.16, bf16[256,256]{1,0:T(8,128)(2,1)} %bitcast.18, ...), custom_call_target="tpu_custom_call" | custom-call | tf_op jit(solution)/shard_map/attributes/pallas_call | solution.py:314
  55.5 0.5 collective-permute-start.4
  56.0 1.1 %collective-permute-done.4 = f32[96,128]{1,0:T(8,128)S(1)} collective-permute-done((f32[96,128]{1,0:T(8,128)}, f32[96,128]{1,0:T(8,128)S(1)}, u32[]{:S(2)}, u32[]{:S(2)}) %collective-permute-start.4) | collective-permute-done | bytes 49184 | tf_op jit(solution)/shard_map/ppermute | solution.py:43
  57.1 0.8 add.11
  57.9 1.7 %collective-permute-start.5 = (f32[96,128]{1,0:T(8,128)S(1)}, f32[96,128]{1,0:T(8,128)S(1)}, u32[]{:S(2)}, u32[]{:S(2)}) collective-permute-start(f32[96,128]{1,0:T(8,128)S(1)} %add.11), channel_id=1, source_target_pairs={{0,2},{2,0},{1,3},{3,1},{4,6},{6,4},{5,7},{7,5},{8,10},{10,8},{9,1... | collective-permute-start | bytes 147464 | tf_op jit(solution)/shard_map/ppermute | solution.py:43
  59.5 2.4 %collective-permute-done.5 = f32[96,128]{1,0:T(8,128)S(1)} collective-permute-done((f32[96,128]{1,0:T(8,128)S(1)}, f32[96,128]{1,0:T(8,128)S(1)}, u32[]{:S(2)}, u32[]{:S(2)}) %collective-permute-start.5) | collective-permute-done | bytes 49184 | tf_op jit(solution)/shard_map/ppermute | solution.py:43
  62.0 2.5 %collective-permute-start.6 = (f32[96,128]{1,0:T(8,128)S(1)}, f32[96,128]{1,0:T(8,128)S(1)}, u32[]{:S(2)}, u32[]{:S(2)}) collective-permute-start(f32[96,128]{1,0:T(8,128)S(1)} %add.12), channel_id=1, source_target_pairs={{0,4},{4,0},{8,12},{12,8},{1,5},{5,1},{9,13},{13,9},{2,6},{6,2},{1... | collective-permute-start | bytes 147464 | tf_op jit(solution)/shard_map/ppermute | solution.py:43
  64.5 2.1 %collective-permute-done.6 = f32[96,128]{1,0:T(8,128)S(1)} collective-permute-done((f32[96,128]{1,0:T(8,128)S(1)}, f32[96,128]{1,0:T(8,128)S(1)}, u32[]{:S(2)}, u32[]{:S(2)}) %collective-permute-start.6) | collective-permute-done | bytes 49184 | tf_op jit(solution)/shard_map/ppermute | solution.py:43
  66.6 3.3 %collective-permute-start.7 = (f32[96,128]{1,0:T(8,128)S(1)}, f32[96,128]{1,0:T(8,128)S(1)}, u32[]{:S(2)}, u32[]{:S(2)}) collective-permute-start(f32[96,128]{1,0:T(8,128)S(1)} %add.13.mine_ref), channel_id=1, source_target_pairs={{0,8},{4,12},{8,0},{12,4},{1,9},{5,13},{9,1},{13,5},{2,10},{6,14},... | collective-permute-start | bytes 147464 | tf_op jit(solution)/shard_map/ppermute | solution.py:43
  69.9 2.1 %collective-permute-done.7.other_ref = f32[96,128]{1,0:T(8,128)S(1)} collective-permute-done((f32[96,128]{1,0:T(8,128)S(1)}, f32[96,128]{1,0:T(8,128)S(1)}, u32[]{:S(2)}, u32[]{:S(2)}) %collective-permute-start.7) | collective-permute-done | bytes 49184 | tf_op jit(solution)/shard_map/ppermute | solution.py:43
  71.9 0.6 copy-done.5
  72.5 14.8 %whiten.1 = (bf16[96,8,16,128]{3,2,1,0:T(8,128)(2,1)}, f32[96,96]{1,0:T(8,128)}) custom-call(f32[96,128]{1,0:T(8,128)} %copy-done.4, f32[96,128]{1,0:T(8,128)} %copy-done.5, bf16[128,96,128]{2,1,0:T(8,128)(2,1)} %get-tuple-element.5.attr_ref), custom_call_target="tpu_custom_call" | custom-call | tf_op jit(solution)/shard_map/whiten/pallas_call | solution.py:339
  (30 shorter events, 1.3 us)
Async XLA Ops:
  2.4 15.4 %copy-start = (bf16[16,32,256]{2,1,0:T(8,128)(2,1)}, bf16[16,32,256]{2,1,0:T(8,128)(2,1)S(1)}, u32[]{:S(2)}) copy-start(bf16[16,32,256]{2,1,0:T(8,128)(2,1)S(1)} %broadcast_multiply_fusion) | copy-start | bytes 786436
  2.5 8.4 %collective-permute-start.1 = (bf16[8,32,256]{2,1,0:T(8,128)(2,1)S(1)}, bf16[8,32,256]{2,1,0:T(8,128)(2,1)S(1)}, u32[]{:S(2)}, u32[]{:S(2)}) collective-permute-start(bf16[8,32,256]{2,1,0:T(8,128)(2,1)S(1)} %get-tuple-element.18), channel_id=1, source_target_pairs={{4,0},{8,4},{12,8},{5,1},{9,5},{13,9},{6,2},{10,6},{14,10},{7,3},{... | collective-permute-start | bytes 393224 | tf_op jit(solution)/shard_map/ppermute | solution.py:38
  3.8 8.3 %collective-permute-start = (bf16[8,32,256]{2,1,0:T(8,128)(2,1)S(1)}, bf16[8,32,256]{2,1,0:T(8,128)(2,1)S(1)}, u32[]{:S(2)}, u32[]{:S(2)}) collective-permute-start(bf16[8,32,256]{2,1,0:T(8,128)(2,1)S(1)} %get-tuple-element.19), channel_id=1, source_target_pairs={{0,4},{4,8},{8,12},{1,5},{5,9},{9,13},{2,6},{6,10},{10,14},{3,7},{... | collective-permute-start | bytes 393224 | tf_op jit(solution)/shard_map/ppermute | solution.py:38
  10.9 6.3 %copy-start.1 = (bf16[8,32,256]{2,1,0:T(8,128)(2,1)}, bf16[8,32,256]{2,1,0:T(8,128)(2,1)S(1)}, u32[]{:S(2)}) copy-start(bf16[8,32,256]{2,1,0:T(8,128)(2,1)S(1)} %collective-permute-done.1) | copy-start | bytes 393220
  12.1 5.1 %copy-start.2 = (bf16[8,32,256]{2,1,0:T(8,128)(2,1)}, bf16[8,32,256]{2,1,0:T(8,128)(2,1)S(1)}, u32[]{:S(2)}) copy-start(bf16[8,32,256]{2,1,0:T(8,128)(2,1)S(1)} %collective-permute-done) | copy-start | bytes 393220
  12.1 5.0 %collective-permute-start.2 = (bf16[32,8,256]{2,1,0:T(8,128)(2,1)S(1)}, bf16[32,8,256]{2,1,0:T(8,128)(2,1)S(1)}, u32[]{:S(2)}, u32[]{:S(2)}) collective-permute-start(bf16[32,8,256]{2,1,0:T(8,128)(2,1)S(1)} %maximum_select_fusion), channel_id=1, source_target_pairs={{0,2},{2,0},{1,3},{3,1},{4,6},{6,4},{5,7},{7,5},{8,10},{10,8},{9,1... | collective-permute-start | bytes 393224 | tf_op jit(solution)/shard_map/ppermute | solution.py:43
  17.1 0.6 copy-start.3
  19.5 2.9 %copy-start.7 = (bf16[3,96,5]{1,0,2:T(4,128)(2,1)S(1)}, bf16[3,96,5]{1,0,2:T(4,128)(2,1)}, u32[]{:S(2)}) copy-start(bf16[3,96,5]{1,0,2:T(4,128)(2,1)} %param.5) | copy-start | bytes 8644
  21.7 1.5 %collective-permute-start.3 = (bf16[32,256]{1,0:T(8,128)(2,1)S(1)}, bf16[32,256]{1,0:T(8,128)(2,1)S(1)}, u32[]{:S(2)}, u32[]{:S(2)}) collective-permute-start(bf16[32,256]{1,0:T(8,128)(2,1)S(1)} %pad.4), channel_id=1, source_target_pairs={{0,1},{1,0},{2,3},{3,2},{4,5},{5,4},{6,7},{7,6},{8,9},{9,8},{10,11... | collective-permute-start | bytes 49160 | tf_op jit(solution)/shard_map/ppermute | solution.py:43
  23.3 0.6 copy-start.6
  55.5 1.6 %collective-permute-start.4 = (f32[96,128]{1,0:T(8,128)}, f32[96,128]{1,0:T(8,128)S(1)}, u32[]{:S(2)}, u32[]{:S(2)}) collective-permute-start(f32[96,128]{1,0:T(8,128)} %get-tuple-element.4), channel_id=1, source_target_pairs={{0,1},{1,0},{2,3},{3,2},{4,5},{5,4},{6,7},{7,6},{8,9},{9,8},{10,11... | collective-permute-start | bytes 147464 | tf_op jit(solution)/shard_map/ppermute | solution.py:43
  57.9 4.1 %collective-permute-start.5 = (f32[96,128]{1,0:T(8,128)S(1)}, f32[96,128]{1,0:T(8,128)S(1)}, u32[]{:S(2)}, u32[]{:S(2)}) collective-permute-start(f32[96,128]{1,0:T(8,128)S(1)} %add.11), channel_id=1, source_target_pairs={{0,2},{2,0},{1,3},{3,1},{4,6},{6,4},{5,7},{7,5},{8,10},{10,8},{9,1... | collective-permute-start | bytes 147464 | tf_op jit(solution)/shard_map/ppermute | solution.py:43
  62.0 4.6 %collective-permute-start.6 = (f32[96,128]{1,0:T(8,128)S(1)}, f32[96,128]{1,0:T(8,128)S(1)}, u32[]{:S(2)}, u32[]{:S(2)}) collective-permute-start(f32[96,128]{1,0:T(8,128)S(1)} %add.12), channel_id=1, source_target_pairs={{0,4},{4,0},{8,12},{12,8},{1,5},{5,1},{9,13},{13,9},{2,6},{6,2},{1... | collective-permute-start | bytes 147464 | tf_op jit(solution)/shard_map/ppermute | solution.py:43
  66.6 5.4 %copy-start.4 = (f32[96,128]{1,0:T(8,128)}, f32[96,128]{1,0:T(8,128)S(1)}, u32[]{:S(2)}) copy-start(f32[96,128]{1,0:T(8,128)S(1)} %add.13.mine_ref) | copy-start | bytes 147460
  66.6 5.3 %collective-permute-start.7 = (f32[96,128]{1,0:T(8,128)S(1)}, f32[96,128]{1,0:T(8,128)S(1)}, u32[]{:S(2)}, u32[]{:S(2)}) collective-permute-start(f32[96,128]{1,0:T(8,128)S(1)} %add.13.mine_ref), channel_id=1, source_target_pairs={{0,8},{4,12},{8,0},{12,4},{1,9},{5,13},{9,1},{13,5},{2,10},{6,14},... | collective-permute-start | bytes 147464 | tf_op jit(solution)/shard_map/ppermute | solution.py:43
  71.9 0.6 copy-start.5

commit v2 on v1

--- a/solution.py
+++ b/solution.py
@@ -1,4 +1,5 @@
 import functools
+import math
 
 import jax
 import jax.numpy as jnp
@@ -38,26 +39,36 @@
     return lax.ppermute(value, axis, [(i, i + step) for i in range(size) if 0 <= i + step < size])
 
 
-def swapped(value, axis, bit):
+def flipped(value, flips):
+    axes = tuple(axis for axis, _ in flips)
+    sizes = [lax.axis_size(axis) for axis in axes]
+    pairs = []
+    for source in range(math.prod(sizes)):
+        target, rest, stride = 0, source, 1
+        for size, (_, bit) in reversed(list(zip(sizes, flips))):
+            target += ((rest % size) ^ bit) * stride
+            rest, stride = rest // size, stride * size
+        pairs.append((source, target))
+    return lax.ppermute(value, axes, pairs)
+
+
+def bits_of(axis):
     size = lax.axis_size(axis)
-    return lax.ppermute(value, axis, [(i, i ^ bit) for i in range(size)])
-
-
-def summed(value, axes):
-    other = None
-    for axis in axes:
-        size = lax.axis_size(axis)
-        assert size & (size - 1) == 0
-        bit = 1
-        while bit < size:
-            if other is not None:
-                value = value + other
-            other = swapped(value, axis, bit)
-            bit *= 2
-    return value, other
-
-
-def halo_select(level, odd, stored, x_left, depth_first):
+    assert size & (size - 1) == 0
+    return [(axis, 2 ** i) for i in range(size.bit_length() - 1)]
+
+
+def summed(value):
+    x_bits, il_bits = bits_of("xline"), bits_of("inline")
+    for bit in bits_of("depth") + x_bits[1:] + il_bits[2:]:
+        value = value + flipped(value, [bit])
+    one, two = il_bits[0], x_bits[0]
+    a, b, c = flipped(value, [one]), flipped(value, [two]), flipped(value, [one, two])
+    value = (value + a) + (b + c)
+    return value, flipped(value, [il_bits[1]])
+
+
+def halo_select(level, stored, x_left, depth_first):
     dilation = 2 ** level
     rows, cols = 256, TAPS * 128
     lane = iota((1, cols), 1)
@@ -72,19 +83,29 @@
     else:
         slot = jnp.where((j < 0) & (x_left == 0), -999999, slot)
         slot = jnp.where((j >= 32) & (x_left == 1), -999999, slot)
-    if odd:
-        source = 4 * stored + slot
-        source = jnp.where((place == -1) & (depth_first == 0), source, -1)
-    else:
-        source = jnp.where(place >= 0, place, place + 4) * stored + slot
-        source = jnp.where((place >= 0) & (depth_first == 0), -1, source)
-        source = jnp.where((place < 0) & (depth_first == 1), -1, source)
+    kept = jnp.where(place >= 0, place, place + 4)
+    if level == 0:
+        kept = jnp.where(place == -2, 4, kept)
+    source = kept * stored + slot
+    source = jnp.where((place >= 0) & (depth_first == 0), -1, source)
+    source = jnp.where((place < 0) & (depth_first == 1), -1, source)
     return ones_where(iota((rows, cols), 0) == source)
+
+
+def shift_matrix(shifts, odd):
+    lane = iota((1, 128 * len(shifts)), 1)
+    source = lane % 128
+    for i, shift in enumerate(shifts):
+        source = jnp.where(lane // 128 == i, source + shift, source)
+    past = (source + 128) % 128 + 128 - (1 if odd else 0)
+    source = jnp.where(source < 0, past, jnp.where(source >= 128, past, source))
+    return ones_where(iota((256, 128 * len(shifts)), 0) == source)
 
 
 def attributes_kernel(
     two_sided, place_ref, live_smem, live_ref, taps_ref, own_ref, before_ref, after_ref, xh_ref, dh_ref,
     attr_ref, gram_ref, bands, first0, first12, halo2, w2, w3, planes,
+    moves0e, moves0o, moves1, moves2,
 ):
     x_left = place_ref[0]
     depth_first = place_ref[1]
@@ -133,7 +154,7 @@
         first0[j] = rounded(dot(a0, planes[j + 6]))
         return 0
 
-    lax.fori_loop(0, 35, level0_first, 0)
+    lax.fori_loop(0, 35, level0_first, 0, unroll=7)
 
     def even_first(pair, _):
         both = jnp.concatenate([planes[4 * pair, :, 0:128], planes[4 * pair + 2, :, 0:128]], axis=1)
@@ -142,85 +163,92 @@
         first12[2 * pair + 1] = out[:, 128:256]
         return 0
 
-    lax.fori_loop(0, 12, even_first, 0)
-
-    for index, (level, odd) in enumerate(((0, False), (0, True), (1, False), (2, False))):
-        cols = dot(dh_ref[...], halo_select(level, odd, stored, x_left, depth_first)).astype(BF16)
+    lax.fori_loop(0, 12, even_first, 0, unroll=4)
+
+    n = iota((1, 256), 1)
+    kept = n // stored
+    sample = 2 * kept - jnp.where(kept == 4, 1, 0) + jnp.where(depth_first == 1, 0, 120)
+    sample = jnp.where(kept < KEPT, sample, -1)
+    spread = ones_where(iota((128, 256), 0) == sample)
+    rows = 32 * stored
+    wide = dot(dh_ref[...].reshape(rows, 128), spread)
+    wide = jnp.where(iota((rows, 256), 0) % stored == n % stored, wide, 0.0).astype(BF16)
+    gather = ones_where(iota((32, rows), 1) // stored == iota((32, rows), 0))
+    lanes = dot(gather, wide).astype(BF16)
+    for level in range(3):
+        cols = dot(lanes, halo_select(level, stored, x_left, depth_first)).astype(BF16)
         part = rounded(dot(bands[level * 256 : level * 256 + 256, 0:32], cols))
         cs = slice(level * ORIENT, (level + 1) * ORIENT)
         total = jnp.zeros((256, 128), F32)
         for k in range(TAPS):
             total = total + part[:, k * 128 : k * 128 + 128] * jnp.concatenate([w2[k, cs]] * 8, axis=0)
-        halo2[index] = rounded(total)
-    lane256 = iota((256, 128), 1)
-    w3_0, w3_1, w3_4 = [jnp.concatenate([w3[k, 0:ORIENT]] * 8, axis=0) for k in (0, 1, 4)]
-    halo2[0] = jnp.where(lane256 % 8 == 7, halo2[0] * w3_0 + halo2[1] * w3_1, halo2[0] * w3_4)
-
-    lane = iota((16, 128), 1)
-
-    def tap_rows(ref, level, c16):
-        start = pl.multiple_of(level * ORIENT + c16 * 16, 16)
-        return [ref[k, pl.ds(start, 16), :] for k in range(TAPS)], start
-
-    def rolled(value, shift):
-        return pltpu.roll(value, shift % 128, 1) if shift % 128 else value
-
-    def level0_rest(step, _):
-        o, c16 = step // 2, step % 2
-        rows = pl.ds(pl.multiple_of(o * ORIENT + c16 * 16, 16), 16)
-        s2, start = tap_rows(w2, 0, c16)
-        s3, _ = tap_rows(w3, 0, c16)
-        halo = halo2[0, rows, :]
-        for q in range(16):
-            even = sum(s2[k] * first0[2 * q + k, rows, 0:128] for k in range(TAPS))
-            odd = sum(s2[k] * first0[2 * q + k, rows, 128:256] for k in range(TAPS))
-            even, odd = rounded(even), rounded(odd)
-            mine = rolled(halo, -8 * q)
-            back = jnp.where(lane == 127, mine, s3[0] * even + s3[1] * odd)
-            ahead = jnp.where(lane == 0, mine, s3[4] * even)
-            total = s3[2] * even + s3[3] * odd + rolled(back, 1) + rolled(ahead, -1)
-            total = total * live_smem[2 * o, 2 * q].astype(F32)
-            attr_ref[o * 16 + q, pl.ds(start, 16), :] = total.astype(BF16)
-        return 0
-
-    lax.fori_loop(0, 16, level0_rest, 0)
-
-    def even_rest(level):
+        halo2[level] = total.astype(BF16)
+
+    moves0e[...] = shift_matrix((-1, 1), False)
+    moves0o[...] = shift_matrix((-1,), True)
+    moves1[...] = shift_matrix((-2, -1, 1, 2), False)
+    moves2[...] = shift_matrix((-4, -2, 2, 4), False)
+
+    def crossline(level, q, o):
+        cs = slice(level * ORIENT, (level + 1) * ORIENT)
+        s2 = [w2[k, cs] for k in range(TAPS)]
+        if level == 0:
+            rows = slice(o * ORIENT, (o + 1) * ORIENT)
+            return [
+                sum(s2[k] * first0[2 * q + k, rows, half] for k in range(TAPS)).astype(BF16)
+                for half in (slice(0, 128), slice(128, 256))
+            ]
+        rows = slice((level - 1) * 256 + o * ORIENT, (level - 1) * 256 + (o + 1) * ORIENT)
         unit = 2 ** (level - 1)
-
-        def body(step, _):
-            o, c16 = step // 2, step % 2
-            rows = pl.ds(pl.multiple_of((level - 1) * 256 + o * ORIENT + c16 * 16, 16), 16)
-            halo_rows = pl.ds(pl.multiple_of(o * ORIENT + c16 * 16, 16), 16)
-            s2, start = tap_rows(w2, level, c16)
-            s3, _ = tap_rows(w3, level, c16)
-            halo = halo2[level + 1, halo_rows, :]
-            for q in range(16):
-                value = rounded(sum(s2[k] * first12[q + 4 + unit * (k - 2), rows, :] for k in range(TAPS)))
-                mine = rolled(halo, -8 * q)
-                total = s3[2] * value
-                for k in (0, 1, 3, 4):
-                    shift = unit * (k - 2)
-                    edge = lane < shift if shift > 0 else lane >= 128 + shift
-                    total = total + s3[k] * rolled(jnp.where(edge, mine, value), -shift)
-                total = total * live_smem[2 * o, 2 * q].astype(F32)
-                attr_ref[o * 16 + q, pl.ds(start, 16), :] = total.astype(BF16)
-            return 0
-
-        return body
-
-    lax.fori_loop(0, 16, even_rest(1), 0)
-    lax.fori_loop(0, 16, even_rest(2), 0)
-
-    def add_gram(o, total):
-        for q in range(0, 16, 2):
-            both = jnp.concatenate([attr_ref[o * 16 + q], attr_ref[o * 16 + q + 1]], axis=1)
+        total = sum(s2[k] * first12[q + 4 + unit * (k - 2), rows, :] for k in range(TAPS))
+        return [total.astype(BF16)]
+
+    def one_q(q):
+        lane = iota((1, 128), 1)
+        place = jnp.where(lane < 4, lane, jnp.where(lane >= 124, lane - 128, -9999))
+        source = jnp.where(place < -8, -1, (8 * q + place + 128) % 128)
+        turn_q = ones_where(iota((128, 128), 0) == source)
+        for level in range(3):
+            cs = slice(level * ORIENT, (level + 1) * ORIENT)
+            halo = dot(halo2[level], turn_q).astype(BF16)
+            both = [crossline(level, q, o) for o in range(8)]
+            even = jnp.concatenate([b[0] for b in both], axis=0)
+            joined = jnp.concatenate([even, halo], axis=1)
+            if level == 0:
+                odd = jnp.concatenate([b[1] for b in both], axis=0)
+                moved = dot(joined, moves0e[...])
+                moved_odd = dot(jnp.concatenate([odd, halo], axis=1), moves0o[...])
+            else:
+                moved = dot(joined, (moves1 if level == 1 else moves2)[...])
+            s3 = [w3[k, cs] for k in range(TAPS)]
+            for o in range(8):
+                rows = slice(o * ORIENT, (o + 1) * ORIENT)
+                terms = [s3[2] * even[rows].astype(F32)]
+                order = (0, 4) if level == 0 else (0, 1, 3, 4)
+                for i, k in enumerate(order):
+                    terms.append(s3[k] * moved[rows, i * 128 : i * 128 + 128])
+                if level == 0:
+                    terms.append(s3[1] * moved_odd[rows])
+                    terms.append(s3[3] * odd[rows].astype(F32))
+                total = sum(terms) * live_smem[2 * o, 2 * q].astype(F32)
+                attr_ref[o * 16 + q, cs, :] = total.astype(BF16)
+
+    def add_gram(q, total):
+        for o in range(0, 8, 2):
+            both = jnp.concatenate([attr_ref[o * 16 + q], attr_ref[o * 16 + 16 + q]], axis=1)
             total = total + lax.dot_general(
                 both, both, (((1,), (1,)), ((), ())), preferred_element_type=F32
             )
         return total
 
-    gram = lax.fori_loop(0, 8, add_gram, jnp.zeros((CHAN, CHAN), F32))
+    def next_q(q, total):
+        total = add_gram(q - 1, total)
+        one_q(q)
+        return total
+
+    one_q(0)
+    gram = lax.fori_loop(1, 16, next_q, jnp.zeros((CHAN, CHAN), F32))
+    gram = add_gram(15, gram)
     alive = live_ref[...]
     chosen = (iota(alive.shape, 0) % 2 == 0) & (iota(alive.shape, 1) % 2 == 0)
     count = jnp.sum(jnp.where(chosen, alive.astype(F32), 0.0)) * 128.0
@@ -241,23 +269,45 @@
         for g in range(CHAN // 8):
             blocks.append(jnp.where(lane < CHAN, total[8 * g : 8 * g + 8] / count, 0.0))
         row_lane = iota((1, 128), 1)
-        for j in range(CHAN):
-            g, s = j // 8, j % 8
-            row = blocks[g][s : s + 1, :]
-            pivot = row[:, j : j + 1]
+
+        def finish(j, row, pivot):
             scale = lax.rsqrt(pivot)
-            recip = 1.0 / pivot
             factor_ref[j : j + 1, :] = (jnp.where(row_lane >= j, row, 0.0) * scale)[:, 0:CHAN]
             unit = jnp.where(row_lane == j, 1.0, row)
             inverse[j : j + 1, :] = jnp.where(row_lane <= j, unit, 0.0) * scale
-            if j == CHAN - 1:
+
+        def spread_lane(block, j):
+            return jnp.broadcast_to(block[:, j : j + 1], (8, 128))
+
+        def spread_row(block, i):
+            return jnp.broadcast_to(block[i : i + 1, :], (8, 128))
+
+        for j in range(0, CHAN, 2):
+            g, s = j // 8, j % 8
+            top = blocks[g]
+            col0, col1 = spread_lane(top, j), spread_lane(top, j + 1)
+            row0, row1 = spread_row(top, s), spread_row(top, s + 1)
+            a, b, c = spread_row(col0, s), spread_row(col0, s + 1), spread_row(col1, s + 1)
+            recip = 1.0 / (a * c - b * b)
+            ratio = b / a
+            rest1 = row1 - ratio * jnp.where(lane == j, 1.0, row0)
+            rest1 = jnp.where(lane == j, -ratio, rest1)
+            finish(j, row0[0:1], a[0:1])
+            finish(j + 1, rest1[0:1], (c - b * ratio)[0:1])
+            if j == CHAN - 2:
                 break
-            scaled_row = unit * recip
+            unit0 = jnp.where(lane == j, 1.0, jnp.where(lane == j + 1, 0.0, row0))
+            unit1 = jnp.where(lane == j, 0.0, jnp.where(lane == j + 1, 1.0, row1))
+            up0 = (c * unit0 - b * unit1) * recip
+            up1 = (a * unit1 - b * unit0) * recip
             for h in range(g, CHAN // 8):
-                col = blocks[h][:, j : j + 1]
-                if h == g:
-                    col = jnp.where(sub[:, 0:1] > s, col, 0.0)
-                blocks[h] = jnp.where(lane == j, 0.0, blocks[h]) - col * scaled_row
+                if h > g:
+                    col0, col1 = spread_lane(blocks[h], j), spread_lane(blocks[h], j + 1)
+                else:
+                    col0 = jnp.where(sub > s + 1, col0, 0.0)
+                    col1 = jnp.where(sub > s + 1, col1, 0.0)
+                cleared = jnp.where((lane == j) | (lane == j + 1), 0.0, blocks[h])
+                blocks[h] = cleared - (col0 * up0 + col1 * up1)
         low = inverse[:, 0:CHAN].astype(BF16)
         spread = ones_where(iota((CHAN, 768), 0) == iota((CHAN, 768), 1) % CHAN)
         wide = dot(low, spread).astype(BF16)
@@ -297,15 +347,13 @@
     if two_sided:
         xh = [shifted(stack(high), "xline", 1), shifted(stack(low), "xline", -1)]
     else:
-        xh = [swapped(jnp.where(x_index == 0, stack(high), stack(low)), "xline", 1)]
-    whole = jnp.concatenate([jnp.concatenate([before, live, after], axis=0)] + xh, axis=1)
-    last = jnp.concatenate(
-        [whole[:, :, t] for t in (t_len - 8, t_len - 6, t_len - 4, t_len - 2, t_len - 1)], axis=1
-    )
-    initial = jnp.concatenate([whole[:, :, t] for t in (0, 2, 4, 6, 7)], axis=1)
-    dh = jnp.where(d_index == 0, last, initial)
-    dh = jnp.pad(dh, ((0, 0), (0, 256 - dh.shape[1])))
-    dh = swapped(dh, "depth", 1)
+        xh = [flipped(jnp.where(x_index == 0, stack(high), stack(low)), [("xline", 1)])]
+    def edge(ts):
+        rows = jnp.concatenate([before[:, :, ts], live[:, :, ts], after[:, :, ts]], axis=0)
+        return jnp.concatenate([rows] + [x[:, :, ts] for x in xh], axis=1)
+
+    dh = jnp.where(d_index == 0, edge(slice(t_len - 128, t_len)), edge(slice(0, 128)))
+    dh = flipped(dh, [("depth", 1)])
 
     place = jnp.stack([(x_index == 1).astype(jnp.int32), (d_index == 0).astype(jnp.int32)])
     vmem = pl.BlockSpec(memory_space=pltpu.VMEM)
@@ -323,10 +371,14 @@
             pltpu.VMEM((768, 128), BF16),
             pltpu.VMEM((35, 256, 256), F32),
             pltpu.VMEM((24, 512, 128), F32),
-            pltpu.VMEM((4, 256, 128), F32),
+            pltpu.VMEM((3, 256, 128), BF16),
             pltpu.VMEM((TAPS, CHAN, 128), F32),
             pltpu.VMEM((TAPS, CHAN, 128), F32),
             pltpu.VMEM((48, 32, 256), BF16),
+            pltpu.VMEM((256, 256), BF16),
+            pltpu.VMEM((256, 128), BF16),
+            pltpu.VMEM((256, 512), BF16),
+            pltpu.VMEM((256, 512), BF16),
         ],
         compiler_params=pltpu.CompilerParams(vmem_limit_bytes=VMEM_LIMIT),
         name="attributes",
@@ -335,7 +387,7 @@
         before.reshape(256, t_len), after.reshape(256, t_len), xrows, dh,
     )
 
-    mine, other = summed(gram, ("depth", "xline", "inline"))
+    mine, other = summed(gram)
     out, factor = pl.pallas_call(
         whiten_kernel,
         grid=(4,),

time: 87.6 us -> 69.8 us (0.80)
  Pallas kernels: 46.4 us -> 33.3 us
  local copies, waits for them, and re-layouts: 6.55 us -> 2.28 us
    pallas_call x1, Pallas kernels: 31.6 us -> 20.1 us  [local(): pl.pallas_call(functools.partial(attributes_kernel, two_sided), out_shape...]
    unnamed x26 -> x16, local copies, waits for them, and re-layouts: 4.68 us -> 1.33 us
    pallas_call x1, Pallas kernels: 14.8 us -> 13.2 us  [local(): pl.pallas_call(whiten_kernel, grid=(4,), out_shape=(jax.ShapeDtypeStruct(...]
    ppermute x6 -> x7, starting transfers between devices: 9.81 us -> 9.25 us  [flipped(): return lax.ppermute(value, axes, pairs)]
    ppermute x6 -> x7, waiting for transfers between devices: 10.9 us -> 11 us  [flipped(): return lax.ppermute(value, axes, pairs)]
  transfers between devices with their start and end apart: 8 -> 9, of which waited for: 7 -> 9; matrix products, arithmetic and copies ran while one was open for 2% -> 2% of each run, Pallas kernels for 0% -> 0%
where the time goes in v2:
time: 69.8 us; the launch traced here: 69.5 us
  Pallas kernels  33.3 us (48%)
  starting transfers between devices  16.1 us (23%)
  waiting for transfers between devices  13.7 us (20%)
  other arithmetic  3.38 us (5%)
  local copies, waits for them, and re-layouts  2.28 us (3%)
  between operations  0.79 us (1%)
    pallas_call x1, Pallas kernels, local(): pl.pallas_call(functools.partial(attributes_kernel, two_sided), out_shape...  20.1 us
    pallas_call x1, Pallas kernels, local(): pl.pallas_call(whiten_kernel, grid=(4,), out_shape=(jax.ShapeDtypeStruct(...  13.2 us
    ppermute x7, waiting for transfers between devices, flipped(): return lax.ppermute(value, axes, pairs)  11 us
    ppermute x7, starting transfers between devices, flipped(): return lax.ppermute(value, axes, pairs)  9.25 us
    ppermute x2, starting transfers between devices, shifted(): lax.ppermute(value, axis, [(i, i + step) for i in range(size) if 0 <= i +...  6.86 us
    ppermute x2, waiting for transfers between devices, shifted(): lax.ppermute(value, axis, [(i, i + step) for i in range(size) if 0 <= i +...  2.63 us
  transfers between devices with their start and end apart: 9, of which 9 were waited for; matrix products, arithmetic and copies ran while one was open for 2% of the time, Pallas kernels for 0%

profile of v2, /device:TPU:0, one launch (start us, length us, event | category | flops | bytes accessed | tf_op | source)
XLA Modules:
  0.0 69.5 jit_solution(10814133191846256582)
XLA Ops:
  0.6 0.0 copy-start.7
  0.6 0.7 %convert_element_type.9 = bf16[16,32]{1,0:T(8,128)(2,1)S(1)} convert(s32[16,32]{1,0:T(8,128)} %live_ref.1) | non-fusion elementwise | flops 512 | bytes 3072 | tf_op jit(solution)/shard_map/convert_element_type | solution.py:334
  1.3 1.1 %broadcast_multiply_fusion = bf16[16,32,256]{2,1,0:T(8,128)(2,1)S(1)} fusion(bf16[16,32,256]{2,1,0:T(8,128)(2,1)} %param.3, bf16[16,32]{1,0:T(8,128)(2,1)S(1)} %convert_element_type.9), kind=kLoop, calls=%fused_computation.2 | loop fusion | flops 131072 | bytes 525312 | tf_op jit(solution)/shard_map/mul | solution.py:334
  2.4 0.0 copy-start
  2.5 1.3 %collective-permute-start.1 = (bf16[8,32,256]{2,1,0:T(8,128)(2,1)S(1)}, bf16[8,32,256]{2,1,0:T(8,128)(2,1)S(1)}, u32[]{:S(2)}, u32[]{:S(2)}) collective-permute-start(bf16[8,32,256]{2,1,0:T(8,128)(2,1)S(1)} %get-tuple-element.10), channel_id=1, source_target_pairs={{4,0},{8,4},{12,8},{5,1},{9,5},{13,9},{6,2},{10,6},{14,10},{7,3},{... | collective-permute-start | bytes 393224 | tf_op jit(solution)/shard_map/ppermute | solution.py:39
  3.8 5.6 %collective-permute-start = (bf16[8,32,256]{2,1,0:T(8,128)(2,1)S(1)}, bf16[8,32,256]{2,1,0:T(8,128)(2,1)S(1)}, u32[]{:S(2)}, u32[]{:S(2)}) collective-permute-start(bf16[8,32,256]{2,1,0:T(8,128)(2,1)S(1)} %get-tuple-element.11), channel_id=1, source_target_pairs={{0,4},{4,8},{8,12},{1,5},{5,9},{9,13},{2,6},{6,10},{10,14},{3,7},{... | collective-permute-start | bytes 393224 | tf_op jit(solution)/shard_map/ppermute | solution.py:39
  9.4 1.5 %collective-permute-done.1 = bf16[8,32,256]{2,1,0:T(8,128)(2,1)S(1)} collective-permute-done((bf16[8,32,256]{2,1,0:T(8,128)(2,1)S(1)}, bf16[8,32,256]{2,1,0:T(8,128)(2,1)S(1)}, u32[]{:S(2)}, u32[]{:S(2)}) %collective-permute-start.1) | collective-permute-done | bytes 131104 | tf_op jit(solution)/shard_map/ppermute | solution.py:39
  10.9 1.2 %collective-permute-done = bf16[8,32,256]{2,1,0:T(8,128)(2,1)S(1)} collective-permute-done((bf16[8,32,256]{2,1,0:T(8,128)(2,1)S(1)}, bf16[8,32,256]{2,1,0:T(8,128)(2,1)S(1)}, u32[]{:S(2)}, u32[]{:S(2)}) %collective-permute-start) | collective-permute-done | bytes 131104 | tf_op jit(solution)/shard_map/ppermute | solution.py:39
  12.1 1.8 %collective-permute-start.2 = (bf16[32,8,256]{2,1,0:T(8,128)(2,1)S(1)}, bf16[32,8,256]{2,1,0:T(8,128)(2,1)S(1)}, u32[]{:S(2)}, u32[]{:S(2)}) collective-permute-start(bf16[32,8,256]{2,1,0:T(8,128)(2,1)S(1)} %maximum_select_fusion.1), channel_id=1, source_target_pairs={{0,2},{2,0},{1,3},{3,1},{4,6},{6,4},{5,7},{7,5},{8,10},{10,8},{9,1... | collective-permute-start | bytes 393224 | tf_op jit(solution)/shard_map/ppermute | solution.py:52
  13.9 3.2 %collective-permute-done.2 = bf16[32,8,256]{2,1,0:T(8,128)(2,1)S(1)} collective-permute-done((bf16[32,8,256]{2,1,0:T(8,128)(2,1)S(1)}, bf16[32,8,256]{2,1,0:T(8,128)(2,1)S(1)}, u32[]{:S(2)}, u32[]{:S(2)}) %collective-permute-start.2) | collective-permute-done | bytes 131104 | tf_op jit(solution)/shard_map/ppermute | solution.py:52
  17.2 0.1 maximum_select_fusion
  17.3 0.1 collective-permute-start.3
  17.3 0.0 copy-done.7
  17.4 0.8 %copy.6.taps_ref = f32[3,96,5]{2,1,0:T(8,128)} copy(bf16[3,96,5]{1,0,2:T(4,128)(2,1)S(1)} %copy-done.7) | data formatting | bytes 8640 | tf_op jit(solution)/shard_map/convert_element_type | solution.py:335
  18.2 0.6 add_convert_fusion.place_ref
  18.8 0.2 collective-permute-done.3.dh_ref
  19.0 0.7 %copy-done.4 = bf16[32,40,128]{2,1,0:T(8,128)(2,1)} copy-done((bf16[32,40,128]{2,1,0:T(8,128)(2,1)}, bf16[32,40,128]{2,1,0:T(8,128)(2,1)S(1)}, u32[]{:S(2)}) %copy-start.4) | copy-done | bytes 327704
  19.7 20.1 %attributes.1 = (bf16[128,96,128]{2,1,0:T(8,128)(2,1)}, f32[96,128]{1,0:T(8,128)}) custom-call(s32[2]{0:T(128)} %add_convert_fusion.place_ref, s32[16,32]{1,0:T(8,128)} %live_ref.1, s32[16,32]{1,0:T(8,128)} %live_ref.1, f32[3,96,5]{2,1,0:T(8,128)} %copy.6.taps_ref, bf16[512,256]{1,0:T(8,128)(2,1)} %bitcast.6, bf16[256,256]{1,0:T(8,128)(2,1)} %bitcast.8, ...), custom_call_target="tpu_custom_call" | custom-call | tf_op jit(solution)/shard_map/attributes/pallas_call | solution.py:362
  39.7 0.3 collective-permute-start.4
  40.1 1.1 %collective-permute-done.4 = f32[96,128]{1,0:T(8,128)S(1)} collective-permute-done((f32[96,128]{1,0:T(8,128)}, f32[96,128]{1,0:T(8,128)S(1)}, u32[]{:S(2)}, u32[]{:S(2)}) %collective-permute-start.4) | collective-permute-done | bytes 49184 | tf_op jit(solution)/shard_map/ppermute | solution.py:52
  41.2 0.8 %add.12 = f32[96,128]{1,0:T(8,128)S(1)} add(f32[96,128]{1,0:T(8,128)} %get-tuple-element.4, f32[96,128]{1,0:T(8,128)S(1)} %collective-permute-done.4) | non-fusion elementwise | flops 12288 | bytes 147456 | tf_op jit(solution)/shard_map/add | solution.py:64
  42.0 3.6 %collective-permute-start.7 = (f32[96,128]{1,0:T(8,128)S(1)}, f32[96,128]{1,0:T(8,128)S(1)}, u32[]{:S(2)}, u32[]{:S(2)}) collective-permute-start(f32[96,128]{1,0:T(8,128)S(1)} %add.12), channel_id=1, source_target_pairs={{0,6},{2,4},{4,2},{6,0},{8,14},{10,12},{12,10},{14,8},{1,7},{3,5},... | collective-permute-start | bytes 147464 | tf_op jit(solution)/shard_map/ppermute | solution.py:52
  45.6 0.4 collective-permute-start.6
  46.0 0.3 collective-permute-start.5
  46.2 1.6 %collective-permute-done.7 = f32[96,128]{1,0:T(8,128)S(1)} collective-permute-done((f32[96,128]{1,0:T(8,128)S(1)}, f32[96,128]{1,0:T(8,128)S(1)}, u32[]{:S(2)}, u32[]{:S(2)}) %collective-permute-start.7) | collective-permute-done | bytes 49184 | tf_op jit(solution)/shard_map/ppermute | solution.py:52
  47.8 1.9 %collective-permute-done.6 = f32[96,128]{1,0:T(8,128)S(1)} collective-permute-done((f32[96,128]{1,0:T(8,128)S(1)}, f32[96,128]{1,0:T(8,128)S(1)}, u32[]{:S(2)}, u32[]{:S(2)}) %collective-permute-start.6) | collective-permute-done | bytes 49184 | tf_op jit(solution)/shard_map/ppermute | solution.py:52
  49.7 0.4 collective-permute-done.5
  50.1 0.0 copy-start.5
  50.1 2.8 %collective-permute-start.8 = (f32[96,128]{1,0:T(8,128)S(1)}, f32[96,128]{1,0:T(8,128)S(1)}, u32[]{:S(2)}, u32[]{:S(2)}) collective-permute-start(f32[96,128]{1,0:T(8,128)S(1)} %add_add_fusion.mine_ref), channel_id=1, source_target_pairs={{0,8},{4,12},{8,0},{12,4},{1,9},{5,13},{9,1},{13,5},{2,10},{6,14},... | collective-permute-start | bytes 147464 | tf_op jit(solution)/shard_map/ppermute | solution.py:52
  52.9 2.8 %collective-permute-done.8.other_ref = f32[96,128]{1,0:T(8,128)S(1)} collective-permute-done((f32[96,128]{1,0:T(8,128)S(1)}, f32[96,128]{1,0:T(8,128)S(1)}, u32[]{:S(2)}, u32[]{:S(2)}) %collective-permute-start.8) | collective-permute-done | bytes 49184 | tf_op jit(solution)/shard_map/ppermute | solution.py:52
  55.7 0.6 copy-done.6
  56.3 13.2 %whiten.1 = (bf16[96,8,16,128]{3,2,1,0:T(8,128)(2,1)}, f32[96,96]{1,0:T(8,128)}) custom-call(f32[96,128]{1,0:T(8,128)} %copy-done.5, f32[96,128]{1,0:T(8,128)} %copy-done.6, bf16[128,96,128]{2,1,0:T(8,128)(2,1)} %get-tuple-element.5.attr_ref), custom_call_target="tpu_custom_call" | custom-call | tf_op jit(solution)/shard_map/whiten/pallas_call | solution.py:391
  (20 shorter events, 0.2 us)
Async XLA Ops:
  0.6 16.7 %copy-start.7 = (bf16[3,96,5]{1,0,2:T(4,128)(2,1)S(1)}, bf16[3,96,5]{1,0,2:T(4,128)(2,1)}, u32[]{:S(2)}) copy-start(bf16[3,96,5]{1,0,2:T(4,128)(2,1)} %param.5) | copy-start | bytes 8644
  2.4 16.5 %copy-start = (bf16[16,32,256]{2,1,0:T(8,128)(2,1)}, bf16[16,32,256]{2,1,0:T(8,128)(2,1)S(1)}, u32[]{:S(2)}) copy-start(bf16[16,32,256]{2,1,0:T(8,128)(2,1)S(1)} %broadcast_multiply_fusion) | copy-start | bytes 786436
  2.5 8.4 %collective-permute-start.1 = (bf16[8,32,256]{2,1,0:T(8,128)(2,1)S(1)}, bf16[8,32,256]{2,1,0:T(8,128)(2,1)S(1)}, u32[]{:S(2)}, u32[]{:S(2)}) collective-permute-start(bf16[8,32,256]{2,1,0:T(8,128)(2,1)S(1)} %get-tuple-element.10), channel_id=1, source_target_pairs={{4,0},{8,4},{12,8},{5,1},{9,5},{13,9},{6,2},{10,6},{14,10},{7,3},{... | collective-permute-start | bytes 393224 | tf_op jit(solution)/shard_map/ppermute | solution.py:39
  3.8 8.3 %collective-permute-start = (bf16[8,32,256]{2,1,0:T(8,128)(2,1)S(1)}, bf16[8,32,256]{2,1,0:T(8,128)(2,1)S(1)}, u32[]{:S(2)}, u32[]{:S(2)}) collective-permute-start(bf16[8,32,256]{2,1,0:T(8,128)(2,1)S(1)} %get-tuple-element.11), channel_id=1, source_target_pairs={{0,4},{4,8},{8,12},{1,5},{5,9},{9,13},{2,6},{6,10},{10,14},{3,7},{... | collective-permute-start | bytes 393224 | tf_op jit(solution)/shard_map/ppermute | solution.py:39
  10.9 8.1 %copy-start.1 = (bf16[8,32,256]{2,1,0:T(8,128)(2,1)}, bf16[8,32,256]{2,1,0:T(8,128)(2,1)S(1)}, u32[]{:S(2)}) copy-start(bf16[8,32,256]{2,1,0:T(8,128)(2,1)S(1)} %collective-permute-done.1) | copy-start | bytes 393220
  12.1 6.9 %copy-start.2 = (bf16[8,32,256]{2,1,0:T(8,128)(2,1)}, bf16[8,32,256]{2,1,0:T(8,128)(2,1)S(1)}, u32[]{:S(2)}) copy-start(bf16[8,32,256]{2,1,0:T(8,128)(2,1)S(1)} %collective-permute-done) | copy-start | bytes 393220
  12.1 5.0 %collective-permute-start.2 = (bf16[32,8,256]{2,1,0:T(8,128)(2,1)S(1)}, bf16[32,8,256]{2,1,0:T(8,128)(2,1)S(1)}, u32[]{:S(2)}, u32[]{:S(2)}) collective-permute-start(bf16[32,8,256]{2,1,0:T(8,128)(2,1)S(1)} %maximum_select_fusion.1), channel_id=1, source_target_pairs={{0,2},{2,0},{1,3},{3,1},{4,6},{6,4},{5,7},{7,5},{8,10},{10,8},{9,1... | collective-permute-start | bytes 393224 | tf_op jit(solution)/shard_map/ppermute | solution.py:52
  17.1 1.8 %copy-start.3 = (bf16[32,8,256]{2,1,0:T(8,128)(2,1)}, bf16[32,8,256]{2,1,0:T(8,128)(2,1)S(1)}, u32[]{:S(2)}) copy-start(bf16[32,8,256]{2,1,0:T(8,128)(2,1)S(1)} %collective-permute-done.2) | copy-start | bytes 393220
  17.3 1.7 %collective-permute-start.3 = (bf16[32,40,128]{2,1,0:T(8,128)(2,1)S(1)}, bf16[32,40,128]{2,1,0:T(8,128)(2,1)S(1)}, u32[]{:S(2)}, u32[]{:S(2)}) collective-permute-start(bf16[32,40,128]{2,1,0:T(8,128)(2,1)S(1)} %maximum_select_fusion), channel_id=1, source_target_pairs={{0,1},{1,0},{2,3},{3,2},{4,5},{5,4},{6,7},{7,6},{8,9},{9,8},{10,11... | collective-permute-start | bytes 983048 | tf_op jit(solution)/shard_map/ppermute | solution.py:52
  19.0 0.7 %copy-start.4 = (bf16[32,40,128]{2,1,0:T(8,128)(2,1)}, bf16[32,40,128]{2,1,0:T(8,128)(2,1)S(1)}, u32[]{:S(2)}) copy-start(bf16[32,40,128]{2,1,0:T(8,128)(2,1)S(1)} %collective-permute-done.3.dh_ref) | copy-start | bytes 983044
  39.7 1.4 %collective-permute-start.4 = (f32[96,128]{1,0:T(8,128)}, f32[96,128]{1,0:T(8,128)S(1)}, u32[]{:S(2)}, u32[]{:S(2)}) collective-permute-start(f32[96,128]{1,0:T(8,128)} %get-tuple-element.4), channel_id=1, source_target_pairs={{0,1},{1,0},{2,3},{3,2},{4,5},{5,4},{6,7},{7,6},{8,9},{9,8},{10,11... | collective-permute-start | bytes 147464 | tf_op jit(solution)/shard_map/ppermute | solution.py:52
  42.0 5.9 %collective-permute-start.7 = (f32[96,128]{1,0:T(8,128)S(1)}, f32[96,128]{1,0:T(8,128)S(1)}, u32[]{:S(2)}, u32[]{:S(2)}) collective-permute-start(f32[96,128]{1,0:T(8,128)S(1)} %add.12), channel_id=1, source_target_pairs={{0,6},{2,4},{4,2},{6,0},{8,14},{10,12},{12,10},{14,8},{1,7},{3,5},... | collective-permute-start | bytes 147464 | tf_op jit(solution)/shard_map/ppermute | solution.py:52
  45.6 4.1 %collective-permute-start.6 = (f32[96,128]{1,0:T(8,128)S(1)}, f32[96,128]{1,0:T(8,128)S(1)}, u32[]{:S(2)}, u32[]{:S(2)}) collective-permute-start(f32[96,128]{1,0:T(8,128)S(1)} %add.12), channel_id=1, source_target_pairs={{0,2},{2,0},{1,3},{3,1},{4,6},{6,4},{5,7},{7,5},{8,10},{10,8},{9,1... | collective-permute-start | bytes 147464 | tf_op jit(solution)/shard_map/ppermute | solution.py:52
  46.0 4.1 %collective-permute-start.5 = (f32[96,128]{1,0:T(8,128)S(1)}, f32[96,128]{1,0:T(8,128)S(1)}, u32[]{:S(2)}, u32[]{:S(2)}) collective-permute-start(f32[96,128]{1,0:T(8,128)S(1)} %add.12), channel_id=1, source_target_pairs={{0,4},{4,0},{8,12},{12,8},{1,5},{5,1},{9,13},{13,9},{2,6},{6,2},{1... | collective-permute-start | bytes 147464 | tf_op jit(solution)/shard_map/ppermute | solution.py:52
  50.1 5.6 %copy-start.5 = (f32[96,128]{1,0:T(8,128)}, f32[96,128]{1,0:T(8,128)S(1)}, u32[]{:S(2)}) copy-start(f32[96,128]{1,0:T(8,128)S(1)} %add_add_fusion.mine_ref) | copy-start | bytes 147460
  50.1 5.6 %collective-permute-start.8 = (f32[96,128]{1,0:T(8,128)S(1)}, f32[96,128]{1,0:T(8,128)S(1)}, u32[]{:S(2)}, u32[]{:S(2)}) collective-permute-start(f32[96,128]{1,0:T(8,128)S(1)} %add_add_fusion.mine_ref), channel_id=1, source_target_pairs={{0,8},{4,12},{8,0},{12,4},{1,9},{5,13},{9,1},{13,5},{2,10},{6,14},... | collective-permute-start | bytes 147464 | tf_op jit(solution)/shard_map/ppermute | solution.py:52
  55.7 0.6 copy-start.6

commit v3 on v2

--- a/solution.py
+++ b/solution.py
@@ -15,7 +15,8 @@
 KEPT = 5
 F32 = jnp.float32
 BF16 = jnp.bfloat16
-VMEM_LIMIT = 56 * 1024 * 1024
+ATTR_VMEM = 30 * 1024 * 1024
+WHITEN_VMEM = 14 * 1024 * 1024
 
 
 def iota(shape, dim):
@@ -92,12 +93,12 @@
     return ones_where(iota((rows, cols), 0) == source)
 
 
-def shift_matrix(shifts, odd):
+def shift_matrix(shifts):
     lane = iota((1, 128 * len(shifts)), 1)
     source = lane % 128
     for i, shift in enumerate(shifts):
         source = jnp.where(lane // 128 == i, source + shift, source)
-    past = (source + 128) % 128 + 128 - (1 if odd else 0)
+    past = (source + 128) % 128 + 128
     source = jnp.where(source < 0, past, jnp.where(source >= 128, past, source))
     return ones_where(iota((256, 128 * len(shifts)), 0) == source)
 
@@ -105,7 +106,7 @@
 def attributes_kernel(
     two_sided, place_ref, live_smem, live_ref, taps_ref, own_ref, before_ref, after_ref, xh_ref, dh_ref,
     attr_ref, gram_ref, bands, first0, first12, halo2, w2, w3, planes,
-    moves0e, moves0o, moves1, moves2,
+    moves1, moves2,
 ):
     x_left = place_ref[0]
     depth_first = place_ref[1]
@@ -182,56 +183,55 @@
         total = jnp.zeros((256, 128), F32)
         for k in range(TAPS):
             total = total + part[:, k * 128 : k * 128 + 128] * jnp.concatenate([w2[k, cs]] * 8, axis=0)
-        halo2[level] = total.astype(BF16)
-
-    moves0e[...] = shift_matrix((-1, 1), False)
-    moves0o[...] = shift_matrix((-1,), True)
-    moves1[...] = shift_matrix((-2, -1, 1, 2), False)
-    moves2[...] = shift_matrix((-4, -2, 2, 4), False)
-
-    def crossline(level, q, o):
+        total = rounded(total)
+        if level == 0:
+            w3_0, w3_1, w3_4 = [jnp.concatenate([w3[k, cs]] * 8, axis=0) for k in (0, 1, 4)]
+            before_first = total * w3_0 + pltpu.roll(total, 1, 1) * w3_1
+            total = jnp.where(iota((256, 128), 1) % 8 == 7, before_first, total * w3_4)
+        halo2[level] = total
+
+    moves1[...] = shift_matrix((-2, -1, 1, 2))
+    moves2[...] = shift_matrix((-4, -2, 2, 4))
+
+    def crossline(level, q, o, half=0):
         cs = slice(level * ORIENT, (level + 1) * ORIENT)
         s2 = [w2[k, cs] for k in range(TAPS)]
         if level == 0:
             rows = slice(o * ORIENT, (o + 1) * ORIENT)
-            return [
-                sum(s2[k] * first0[2 * q + k, rows, half] for k in range(TAPS)).astype(BF16)
-                for half in (slice(0, 128), slice(128, 256))
-            ]
+            ts = slice(half * 128, half * 128 + 128)
+            return sum(s2[k] * first0[2 * q + k, rows, ts] for k in range(TAPS))
         rows = slice((level - 1) * 256 + o * ORIENT, (level - 1) * 256 + (o + 1) * ORIENT)
         unit = 2 ** (level - 1)
-        total = sum(s2[k] * first12[q + 4 + unit * (k - 2), rows, :] for k in range(TAPS))
-        return [total.astype(BF16)]
+        return sum(s2[k] * first12[q + 4 + unit * (k - 2), rows, :] for k in range(TAPS))
 
     def one_q(q):
-        lane = iota((1, 128), 1)
-        place = jnp.where(lane < 4, lane, jnp.where(lane >= 124, lane - 128, -9999))
-        source = jnp.where(place < -8, -1, (8 * q + place + 128) % 128)
-        turn_q = ones_where(iota((128, 128), 0) == source)
-        for level in range(3):
-            cs = slice(level * ORIENT, (level + 1) * ORIENT)
-            halo = dot(halo2[level], turn_q).astype(BF16)
-            both = [crossline(level, q, o) for o in range(8)]
-            even = jnp.concatenate([b[0] for b in both], axis=0)
-            joined = jnp.concatenate([even, halo], axis=1)
-            if level == 0:
-                odd = jnp.concatenate([b[1] for b in both], axis=0)
-                moved = dot(joined, moves0e[...])
-                moved_odd = dot(jnp.concatenate([odd, halo], axis=1), moves0o[...])
-            else:
-                moved = dot(joined, (moves1 if level == 1 else moves2)[...])
-            s3 = [w3[k, cs] for k in range(TAPS)]
+        align = jnp.where(q == 0, 0, 128 - 8 * q)
+
+        def put(o, level, total):
+            total = total * live_smem[2 * o, 2 * q].astype(F32)
+            attr_ref[o * 16 + q, level * ORIENT : (level + 1) * ORIENT, :] = total.astype(BF16)
+
+        for level in (1, 2):
+            halo = pltpu.roll(halo2[level], align, 1).astype(BF16)
+            value = jnp.concatenate([crossline(level, q, o).astype(BF16) for o in range(8)], axis=0)
+            joined = jnp.concatenate([value, halo], axis=1)
+            moved = dot(joined, (moves1 if level == 1 else moves2)[...])
+            s3 = [w3[k, level * ORIENT : (level + 1) * ORIENT] for k in range(TAPS)]
             for o in range(8):
                 rows = slice(o * ORIENT, (o + 1) * ORIENT)
-                terms = [s3[2] * even[rows].astype(F32)]
-                order = (0, 4) if level == 0 else (0, 1, 3, 4)
-                for i, k in enumerate(order):
-                    terms.append(s3[k] * moved[rows, i * 128 : i * 128 + 128])
-                if level == 0:
-                    terms.append(s3[1] * moved_odd[rows])
-                    terms.append(s3[3] * odd[rows].astype(F32))
-                total = sum(terms) * live_smem[2 * o, 2 * q].astype(F32)
-                attr_ref[o * 16 + q, cs, :] = total.astype(BF16)
+                total = s3[2] * value[rows].astype(F32)
+                for i, k in enumerate((0, 1, 3, 4)):
+                    total = total + s3[k] * moved[rows, i * 128 : i * 128 + 128]
+                put(o, level, total)
+        lane = iota((ORIENT, 128), 1)
+        s3 = [w3[k, 0:ORIENT] for k in range(TAPS)]
+        for o in range(8):
+            even, odd = rounded(crossline(0, q, o, 0)), rounded(crossline(0, q, o, 1))
+            halo = pltpu.roll(halo2[0, o * ORIENT : (o + 1) * ORIENT], align, 1)
+            back = jnp.where(lane == 127, halo, s3[0] * even + s3[1] * odd)
+            ahead = jnp.where(lane == 0, halo, s3[4] * even)
+            moved = pltpu.roll(back, 1, 1) + pltpu.roll(ahead, 127, 1)
+            put(o, 0, s3[2] * even + s3[3] * odd + moved)
 
     def add_gram(q, total):
         for o in range(0, 8, 2):
@@ -270,11 +270,10 @@
             blocks.append(jnp.where(lane < CHAN, total[8 * g : 8 * g + 8] / count, 0.0))
         row_lane = iota((1, 128), 1)
 
-        def finish(j, row, pivot):
+        def finish(j, row, inv_row, pivot):
             scale = lax.rsqrt(pivot)
             factor_ref[j : j + 1, :] = (jnp.where(row_lane >= j, row, 0.0) * scale)[:, 0:CHAN]
-            unit = jnp.where(row_lane == j, 1.0, row)
-            inverse[j : j + 1, :] = jnp.where(row_lane <= j, unit, 0.0) * scale
+            inverse[j : j + 1, :] = jnp.where(row_lane <= j, inv_row, 0.0) * scale
 
         def spread_lane(block, j):
             return jnp.broadcast_to(block[:, j : j + 1], (8, 128))
@@ -282,32 +281,58 @@
         def spread_row(block, i):
             return jnp.broadcast_to(block[i : i + 1, :], (8, 128))
 
-        for j in range(0, CHAN, 2):
+        for j in range(0, CHAN, 4):
             g, s = j // 8, j % 8
             top = blocks[g]
-            col0, col1 = spread_lane(top, j), spread_lane(top, j + 1)
-            row0, row1 = spread_row(top, s), spread_row(top, s + 1)
-            a, b, c = spread_row(col0, s), spread_row(col0, s + 1), spread_row(col1, s + 1)
-            recip = 1.0 / (a * c - b * b)
-            ratio = b / a
-            rest1 = row1 - ratio * jnp.where(lane == j, 1.0, row0)
-            rest1 = jnp.where(lane == j, -ratio, rest1)
-            finish(j, row0[0:1], a[0:1])
-            finish(j + 1, rest1[0:1], (c - b * ratio)[0:1])
-            if j == CHAN - 2:
+            cols = [spread_lane(top, j + i) for i in range(4)]
+            rows = [spread_row(top, s + i) for i in range(4)]
+            d = [[spread_row(cols[min(m, i)], s + max(m, i)) for i in range(4)] for m in range(4)]
+            p_inv = 1.0 / (d[0][0] * d[1][1] - d[0][1] * d[0][1])
+            adj = [[d[1][1], -d[0][1]], [-d[0][1], d[0][0]]]
+            h = [
+                [(d[2 + m][0] * adj[0][i] + d[2 + m][1] * adj[1][i]) * p_inv for i in range(2)]
+                for m in range(2)
+            ]
+            t = [
+                [d[2 + m][2 + i] - (h[m][0] * d[0][2 + i] + h[m][1] * d[1][2 + i]) for i in range(2)]
+                for m in range(2)
+            ]
+            t01 = t[1][0]
+            t_inv = 1.0 / (t[0][0] * t[1][1] - t01 * t01)
+            unit = []
+            for i in range(4):
+                value = rows[i]
+                for m in range(4):
+                    value = jnp.where(lane == j + m, 1.0 if m == i else 0.0, value)
+                unit.append(value)
+            below = [unit[2 + m] - (h[m][0] * unit[0] + h[m][1] * unit[1]) for m in range(2)]
+            up2 = (t[1][1] * below[0] - t01 * below[1]) * t_inv
+            up3 = (t[0][0] * below[1] - t01 * below[0]) * t_inv
+            inner = [unit[0] * d[1][1] - unit[1] * d[0][1], unit[1] * d[0][0] - unit[0] * d[0][1]]
+            up0 = inner[0] * p_inv - (h[0][0] * up2 + h[1][0] * up3)
+            up1 = inner[1] * p_inv - (h[0][1] * up2 + h[1][1] * up3)
+            ups = (up0, up1, up2, up3)
+            ratio0 = d[0][1] / d[0][0]
+            ratio1 = t01 / t[0][0]
+            mix0 = rows[2] - (h[0][0] * rows[0] + h[0][1] * rows[1])
+            mix1 = rows[3] - (h[1][0] * rows[0] + h[1][1] * rows[1])
+            solved = [rows[0], rows[1] - ratio0 * rows[0], mix0, mix1 - ratio1 * mix0]
+            inv_solved = [unit[0], unit[1] - ratio0 * unit[0], below[0], below[1] - ratio1 * below[0]]
+            pivots = [d[0][0], d[1][1] - d[0][1] * ratio0, t[0][0], t[1][1] - t01 * ratio1]
+            for i in range(4):
+                finish(j + i, solved[i][0:1], inv_solved[i][0:1], pivots[i][0:1])
+            if j == CHAN - 4:
                 break
-            unit0 = jnp.where(lane == j, 1.0, jnp.where(lane == j + 1, 0.0, row0))
-            unit1 = jnp.where(lane == j, 0.0, jnp.where(lane == j + 1, 1.0, row1))
-            up0 = (c * unit0 - b * unit1) * recip
-            up1 = (a * unit1 - b * unit0) * recip
-            for h in range(g, CHAN // 8):
-                if h > g:
-                    col0, col1 = spread_lane(blocks[h], j), spread_lane(blocks[h], j + 1)
+            inside = (lane >= j) & (lane < j + 4)
+            for k in range(g, CHAN // 8):
+                if k > g:
+                    cols = [spread_lane(blocks[k], j + i) for i in range(4)]
                 else:
-                    col0 = jnp.where(sub > s + 1, col0, 0.0)
-                    col1 = jnp.where(sub > s + 1, col1, 0.0)
-                cleared = jnp.where((lane == j) | (lane == j + 1), 0.0, blocks[h])
-                blocks[h] = cleared - (col0 * up0 + col1 * up1)
+                    if s == 4:
+                        continue
+                    cols = [jnp.where(sub > s + 3, col, 0.0) for col in cols]
+                change = (cols[0] * ups[0] + cols[1] * ups[1]) + (cols[2] * ups[2] + cols[3] * ups[3])
+                blocks[k] = jnp.where(inside, 0.0, blocks[k]) - change
         low = inverse[:, 0:CHAN].astype(BF16)
         spread = ones_where(iota((CHAN, 768), 0) == iota((CHAN, 768), 1) % CHAN)
         wide = dot(low, spread).astype(BF16)
@@ -371,16 +396,14 @@
             pltpu.VMEM((768, 128), BF16),
             pltpu.VMEM((35, 256, 256), F32),
             pltpu.VMEM((24, 512, 128), F32),
-            pltpu.VMEM((3, 256, 128), BF16),
+            pltpu.VMEM((3, 256, 128), F32),
             pltpu.VMEM((TAPS, CHAN, 128), F32),
             pltpu.VMEM((TAPS, CHAN, 128), F32),
             pltpu.VMEM((48, 32, 256), BF16),
-            pltpu.VMEM((256, 256), BF16),
-            pltpu.VMEM((256, 128), BF16),
             pltpu.VMEM((256, 512), BF16),
             pltpu.VMEM((256, 512), BF16),
         ],
-        compiler_params=pltpu.CompilerParams(vmem_limit_bytes=VMEM_LIMIT),
+        compiler_params=pltpu.CompilerParams(vmem_limit_bytes=ATTR_VMEM),
         name="attributes",
     )(
         place, trace_live, trace_live, taps, live.reshape(512, t_len),
@@ -401,7 +424,7 @@
             pl.BlockSpec((CHAN, CHAN), lambda i: (0, 0)),
         ),
         scratch_shapes=[pltpu.VMEM((CHAN, 128), F32), pltpu.VMEM((768, 768), BF16)],
-        compiler_params=pltpu.CompilerParams(vmem_limit_bytes=VMEM_LIMIT),
+        compiler_params=pltpu.CompilerParams(vmem_limit_bytes=WHITEN_VMEM),
         name="whiten",
     )(mine, other, attr)
     return out, factor

time: 69.8 us -> 57.9 us (0.83)
  Pallas kernels: 33.3 us -> 23.8 us
  local copies, waits for them, and re-layouts: 2.28 us -> 0.29 us
  other arithmetic: 3.38 us -> 2.06 us
  waiting for transfers between devices: 13.7 us -> 14.7 us
    pallas_call x1, Pallas kernels: 20.1 us -> 14.7 us  [local(): pl.pallas_call(functools.partial(attributes_kernel, two_sided), out_shape...]
    pallas_call x1, Pallas kernels: 13.2 us -> 9.06 us  [local(): pl.pallas_call(whiten_kernel, grid=(4,), out_shape=(jax.ShapeDtypeStruct(...]
    unnamed x16 -> x4, local copies, waits for them, and re-layouts: 1.33 us -> 0.01 us
    ppermute x7, waiting for transfers between devices: 11 us -> 12.1 us  [flipped(): return lax.ppermute(value, axes, pairs)]
    add x1, other arithmetic: 0.81 us -> 0.01 us  [summed(): value = value + flipped(value, [bit])]
  transfers between devices with their start and end apart: 9 -> 9, of which waited for: 9 -> 9; matrix products, arithmetic and copies ran while one was open for 2% -> 1% of each run, Pallas kernels for 0% -> 0%
where the time goes in v3:
time: 57.9 us; the launch traced here: 57.6 us
  Pallas kernels  23.8 us (41%)
  starting transfers between devices  16.1 us (28%)
  waiting for transfers between devices  14.7 us (25%)
  other arithmetic  2.06 us (4%)
  between operations  0.77 us (1%)
    pallas_call x1, Pallas kernels, local(): pl.pallas_call(functools.partial(attributes_kernel, two_sided), out_shape...  14.7 us
    ppermute x7, waiting for transfers between devices, flipped(): return lax.ppermute(value, axes, pairs)  12.1 us
    ppermute x7, starting transfers between devices, flipped(): return lax.ppermute(value, axes, pairs)  9.21 us
    pallas_call x1, Pallas kernels, local(): pl.pallas_call(whiten_kernel, grid=(4,), out_shape=(jax.ShapeDtypeStruct(...  9.06 us
    ppermute x2, starting transfers between devices, shifted(): lax.ppermute(value, axis, [(i, i + step) for i in range(size) if 0 <= i +...  6.86 us
    ppermute x2, waiting for transfers between devices, shifted(): lax.ppermute(value, axis, [(i, i + step) for i in range(size) if 0 <= i +...  2.64 us
  transfers between devices with their start and end apart: 9, of which 9 were waited for; matrix products, arithmetic and copies ran while one was open for 1% of the time, Pallas kernels for 0%

profile of v3, /device:TPU:0, one launch (start us, length us, event | category | flops | bytes accessed | tf_op | source)
XLA Modules:
  0.0 57.6 jit_solution(6392868151926189422)
XLA Ops:
  0.6 0.0 copy-start
  0.6 0.0 copy-start.1
  0.6 0.8 %convert_element_type.9 = bf16[16,32]{1,0:T(8,128)(2,1)S(1)} convert(s32[16,32]{1,0:T(8,128)} %live_ref.1) | non-fusion elementwise | flops 512 | bytes 3072 | tf_op jit(solution)/shard_map/convert_element_type | solution.py:359
  1.4 1.1 %broadcast_multiply_fusion = bf16[16,32,256]{2,1,0:T(8,128)(2,1)S(1)} fusion(bf16[16,32,256]{2,1,0:T(8,128)(2,1)} %param.3, bf16[16,32]{1,0:T(8,128)(2,1)S(1)} %convert_element_type.9), kind=kLoop, calls=%fused_computation.2 | loop fusion | flops 131072 | bytes 525312 | tf_op jit(solution)/shard_map/mul | solution.py:359
  2.5 1.3 %collective-permute-start.1 = (bf16[8,32,256]{2,1,0:T(8,128)(2,1)S(1)}, bf16[8,32,256]{2,1,0:T(8,128)(2,1)S(1)}, u32[]{:S(2)}, u32[]{:S(2)}) collective-permute-start(bf16[8,32,256]{2,1,0:T(8,128)(2,1)S(1)} %get-tuple-element.10), channel_id=1, source_target_pairs={{4,0},{8,4},{12,8},{5,1},{9,5},{13,9},{6,2},{10,6},{14,10},{7,3},{... | collective-permute-start | bytes 393224 | tf_op jit(solution)/shard_map/ppermute | solution.py:40
  3.8 5.6 %collective-permute-start = (bf16[8,32,256]{2,1,0:T(8,128)(2,1)S(1)}, bf16[8,32,256]{2,1,0:T(8,128)(2,1)S(1)}, u32[]{:S(2)}, u32[]{:S(2)}) collective-permute-start(bf16[8,32,256]{2,1,0:T(8,128)(2,1)S(1)} %get-tuple-element.11), channel_id=1, source_target_pairs={{0,4},{4,8},{8,12},{1,5},{5,9},{9,13},{2,6},{6,10},{10,14},{3,7},{... | collective-permute-start | bytes 393224 | tf_op jit(solution)/shard_map/ppermute | solution.py:40
  9.5 1.5 %collective-permute-done.1 = bf16[8,32,256]{2,1,0:T(8,128)(2,1)S(1)} collective-permute-done((bf16[8,32,256]{2,1,0:T(8,128)(2,1)S(1)}, bf16[8,32,256]{2,1,0:T(8,128)(2,1)S(1)}, u32[]{:S(2)}, u32[]{:S(2)}) %collective-permute-start.1) | collective-permute-done | bytes 131104 | tf_op jit(solution)/shard_map/ppermute | solution.py:40
  10.9 1.2 %collective-permute-done = bf16[8,32,256]{2,1,0:T(8,128)(2,1)S(1)} collective-permute-done((bf16[8,32,256]{2,1,0:T(8,128)(2,1)S(1)}, bf16[8,32,256]{2,1,0:T(8,128)(2,1)S(1)}, u32[]{:S(2)}, u32[]{:S(2)}) %collective-permute-start) | collective-permute-done | bytes 131104 | tf_op jit(solution)/shard_map/ppermute | solution.py:40
  12.2 1.8 %collective-permute-start.2 = (bf16[32,8,256]{2,1,0:T(8,128)(2,1)S(1)}, bf16[32,8,256]{2,1,0:T(8,128)(2,1)S(1)}, u32[]{:S(2)}, u32[]{:S(2)}) collective-permute-start(bf16[32,8,256]{2,1,0:T(8,128)(2,1)S(1)} %maximum_select_fusion.1), channel_id=1, source_target_pairs={{0,2},{2,0},{1,3},{3,1},{4,6},{6,4},{5,7},{7,5},{8,10},{10,8},{9,1... | collective-permute-start | bytes 393224 | tf_op jit(solution)/shard_map/ppermute | solution.py:53
  14.0 3.2 %collective-permute-done.2 = bf16[32,8,256]{2,1,0:T(8,128)(2,1)S(1)} collective-permute-done((bf16[32,8,256]{2,1,0:T(8,128)(2,1)S(1)}, bf16[32,8,256]{2,1,0:T(8,128)(2,1)S(1)}, u32[]{:S(2)}, u32[]{:S(2)}) %collective-permute-start.2) | collective-permute-done | bytes 131104 | tf_op jit(solution)/shard_map/ppermute | solution.py:53
  17.2 0.1 maximum_select_fusion
  17.3 0.1 collective-permute-start.3
  17.4 0.0 copy-done.1
  17.4 0.1 copy.6.taps_ref
  17.5 0.1 add_convert_fusion.place_ref
  17.6 1.4 %collective-permute-done.3.dh_ref = bf16[32,40,128]{2,1,0:T(8,128)(2,1)S(1)} collective-permute-done((bf16[32,40,128]{2,1,0:T(8,128)(2,1)S(1)}, bf16[32,40,128]{2,1,0:T(8,128)(2,1)S(1)}, u32[]{:S(2)}, u32[]{:S(2)}) %collective-permute-start.3) | collective-permute-done | bytes 327712 | tf_op jit(solution)/shard_map/ppermute | solution.py:53
  19.0 0.0 copy-done
  19.0 14.7 %attributes.1 = (bf16[128,96,128]{2,1,0:T(8,128)(2,1)S(1)}, f32[96,128]{1,0:T(8,128)S(1)}) custom-call(s32[2]{0:T(128)S(1)} %add_convert_fusion.place_ref, s32[16,32]{1,0:T(8,128)S(1)} %copy-done, s32[16,32]{1,0:T(8,128)S(1)} %copy-done, f32[3,96,5]{2,1,0:T(8,128)S(1)} %copy.6.taps_ref, bf16[512,256]{1,0:T(8,128)(2,1)S(1)} %bitcast.6, ...), custom_call_target="tpu_custom_call" | custom-call | tf_op jit(solution)/shard_map/attributes/pallas_call | solution.py:387
  33.7 0.2 collective-permute-start.4
  34.0 1.1 %collective-permute-done.4 = f32[96,128]{1,0:T(8,128)S(1)} collective-permute-done((f32[96,128]{1,0:T(8,128)S(1)}, f32[96,128]{1,0:T(8,128)S(1)}, u32[]{:S(2)}, u32[]{:S(2)}) %collective-permute-start.4) | collective-permute-done | bytes 49184 | tf_op jit(solution)/shard_map/ppermute | solution.py:53
  35.0 3.7 %collective-permute-start.7 = (f32[96,128]{1,0:T(8,128)S(1)}, f32[96,128]{1,0:T(8,128)S(1)}, u32[]{:S(2)}, u32[]{:S(2)}) collective-permute-start(f32[96,128]{1,0:T(8,128)S(1)} %add.12), channel_id=1, source_target_pairs={{0,6},{2,4},{4,2},{6,0},{8,14},{10,12},{12,10},{14,8},{1,7},{3,5},... | collective-permute-start | bytes 147464 | tf_op jit(solution)/shard_map/ppermute | solution.py:53
  38.7 0.4 collective-permute-start.6
  39.1 0.3 collective-permute-start.5
  39.3 1.4 %collective-permute-done.7 = f32[96,128]{1,0:T(8,128)S(1)} collective-permute-done((f32[96,128]{1,0:T(8,128)S(1)}, f32[96,128]{1,0:T(8,128)S(1)}, u32[]{:S(2)}, u32[]{:S(2)}) %collective-permute-start.7) | collective-permute-done | bytes 49184 | tf_op jit(solution)/shard_map/ppermute | solution.py:53
  40.8 2.0 %collective-permute-done.6 = f32[96,128]{1,0:T(8,128)S(1)} collective-permute-done((f32[96,128]{1,0:T(8,128)S(1)}, f32[96,128]{1,0:T(8,128)S(1)}, u32[]{:S(2)}, u32[]{:S(2)}) %collective-permute-start.6) | collective-permute-done | bytes 49184 | tf_op jit(solution)/shard_map/ppermute | solution.py:53
  42.8 0.4 collective-permute-done.5
  43.2 2.8 %collective-permute-start.8 = (f32[96,128]{1,0:T(8,128)S(1)}, f32[96,128]{1,0:T(8,128)S(1)}, u32[]{:S(2)}, u32[]{:S(2)}) collective-permute-start(f32[96,128]{1,0:T(8,128)S(1)} %add_add_fusion.mine_ref), channel_id=1, source_target_pairs={{0,8},{4,12},{8,0},{12,4},{1,9},{5,13},{9,1},{13,5},{2,10},{6,14},... | collective-permute-start | bytes 147464 | tf_op jit(solution)/shard_map/ppermute | solution.py:53
  46.0 2.6 %collective-permute-done.8.other_ref = f32[96,128]{1,0:T(8,128)S(1)} collective-permute-done((f32[96,128]{1,0:T(8,128)S(1)}, f32[96,128]{1,0:T(8,128)S(1)}, u32[]{:S(2)}, u32[]{:S(2)}) %collective-permute-start.8) | collective-permute-done | bytes 49184 | tf_op jit(solution)/shard_map/ppermute | solution.py:53
  48.6 9.1 %whiten.1 = (bf16[96,8,16,128]{3,2,1,0:T(8,128)(2,1)}, f32[96,96]{1,0:T(8,128)}) custom-call(f32[96,128]{1,0:T(8,128)S(1)} %add_add_fusion.mine_ref, f32[96,128]{1,0:T(8,128)S(1)} %collective-permute-done.8.other_ref, bf16[128,96,128]{2,1,0:T(8,128)(2,1)S(1)} %get-tuple-element.5.attr_ref), custom_call_target="tpu_custom_call" | custom-call | tf_op jit(solution)/shard_map/whiten/pallas_call | solution.py:414
  (11 shorter events, 0.2 us)
Async XLA Ops:
  0.6 18.4 %copy-start = (s32[16,32]{1,0:T(8,128)S(1)}, s32[16,32]{1,0:T(8,128)}, u32[]{:S(2)}) copy-start(s32[16,32]{1,0:T(8,128)} %live_ref.1) | copy-start | bytes 6148
  0.6 16.8 %copy-start.1 = (bf16[3,96,5]{1,0,2:T(4,128)(2,1)S(1)}, bf16[3,96,5]{1,0,2:T(4,128)(2,1)}, u32[]{:S(2)}) copy-start(bf16[3,96,5]{1,0,2:T(4,128)(2,1)} %param.5) | copy-start | bytes 8644
  2.5 8.4 %collective-permute-start.1 = (bf16[8,32,256]{2,1,0:T(8,128)(2,1)S(1)}, bf16[8,32,256]{2,1,0:T(8,128)(2,1)S(1)}, u32[]{:S(2)}, u32[]{:S(2)}) collective-permute-start(bf16[8,32,256]{2,1,0:T(8,128)(2,1)S(1)} %get-tuple-element.10), channel_id=1, source_target_pairs={{4,0},{8,4},{12,8},{5,1},{9,5},{13,9},{6,2},{10,6},{14,10},{7,3},{... | collective-permute-start | bytes 393224 | tf_op jit(solution)/shard_map/ppermute | solution.py:40
  3.8 8.3 %collective-permute-start = (bf16[8,32,256]{2,1,0:T(8,128)(2,1)S(1)}, bf16[8,32,256]{2,1,0:T(8,128)(2,1)S(1)}, u32[]{:S(2)}, u32[]{:S(2)}) collective-permute-start(bf16[8,32,256]{2,1,0:T(8,128)(2,1)S(1)} %get-tuple-element.11), channel_id=1, source_target_pairs={{0,4},{4,8},{8,12},{1,5},{5,9},{9,13},{2,6},{6,10},{10,14},{3,7},{... | collective-permute-start | bytes 393224 | tf_op jit(solution)/shard_map/ppermute | solution.py:40
  12.2 5.0 %collective-permute-start.2 = (bf16[32,8,256]{2,1,0:T(8,128)(2,1)S(1)}, bf16[32,8,256]{2,1,0:T(8,128)(2,1)S(1)}, u32[]{:S(2)}, u32[]{:S(2)}) collective-permute-start(bf16[32,8,256]{2,1,0:T(8,128)(2,1)S(1)} %maximum_select_fusion.1), channel_id=1, source_target_pairs={{0,2},{2,0},{1,3},{3,1},{4,6},{6,4},{5,7},{7,5},{8,10},{10,8},{9,1... | collective-permute-start | bytes 393224 | tf_op jit(solution)/shard_map/ppermute | solution.py:53
  17.3 1.7 %collective-permute-start.3 = (bf16[32,40,128]{2,1,0:T(8,128)(2,1)S(1)}, bf16[32,40,128]{2,1,0:T(8,128)(2,1)S(1)}, u32[]{:S(2)}, u32[]{:S(2)}) collective-permute-start(bf16[32,40,128]{2,1,0:T(8,128)(2,1)S(1)} %maximum_select_fusion), channel_id=1, source_target_pairs={{0,1},{1,0},{2,3},{3,2},{4,5},{5,4},{6,7},{7,6},{8,9},{9,8},{10,11... | collective-permute-start | bytes 983048 | tf_op jit(solution)/shard_map/ppermute | solution.py:53
  33.7 1.3 %collective-permute-start.4 = (f32[96,128]{1,0:T(8,128)S(1)}, f32[96,128]{1,0:T(8,128)S(1)}, u32[]{:S(2)}, u32[]{:S(2)}) collective-permute-start(f32[96,128]{1,0:T(8,128)S(1)} %get-tuple-element.4), channel_id=1, source_target_pairs={{0,1},{1,0},{2,3},{3,2},{4,5},{5,4},{6,7},{7,6},{8,9},{9,8},{10,11... | collective-permute-start | bytes 147464 | tf_op jit(solution)/shard_map/ppermute | solution.py:53
  35.0 5.7 %collective-permute-start.7 = (f32[96,128]{1,0:T(8,128)S(1)}, f32[96,128]{1,0:T(8,128)S(1)}, u32[]{:S(2)}, u32[]{:S(2)}) collective-permute-start(f32[96,128]{1,0:T(8,128)S(1)} %add.12), channel_id=1, source_target_pairs={{0,6},{2,4},{4,2},{6,0},{8,14},{10,12},{12,10},{14,8},{1,7},{3,5},... | collective-permute-start | bytes 147464 | tf_op jit(solution)/shard_map/ppermute | solution.py:53
  38.7 4.1 %collective-permute-start.6 = (f32[96,128]{1,0:T(8,128)S(1)}, f32[96,128]{1,0:T(8,128)S(1)}, u32[]{:S(2)}, u32[]{:S(2)}) collective-permute-start(f32[96,128]{1,0:T(8,128)S(1)} %add.12), channel_id=1, source_target_pairs={{0,2},{2,0},{1,3},{3,1},{4,6},{6,4},{5,7},{7,5},{8,10},{10,8},{9,1... | collective-permute-start | bytes 147464 | tf_op jit(solution)/shard_map/ppermute | solution.py:53
  39.1 4.1 %collective-permute-start.5 = (f32[96,128]{1,0:T(8,128)S(1)}, f32[96,128]{1,0:T(8,128)S(1)}, u32[]{:S(2)}, u32[]{:S(2)}) collective-permute-start(f32[96,128]{1,0:T(8,128)S(1)} %add.12), channel_id=1, source_target_pairs={{0,4},{4,0},{8,12},{12,8},{1,5},{5,1},{9,13},{13,9},{2,6},{6,2},{1... | collective-permute-start | bytes 147464 | tf_op jit(solution)/shard_map/ppermute | solution.py:53
  43.2 5.4 %collective-permute-start.8 = (f32[96,128]{1,0:T(8,128)S(1)}, f32[96,128]{1,0:T(8,128)S(1)}, u32[]{:S(2)}, u32[]{:S(2)}) collective-permute-start(f32[96,128]{1,0:T(8,128)S(1)} %add_add_fusion.mine_ref), channel_id=1, source_target_pairs={{0,8},{4,12},{8,0},{12,4},{1,9},{5,13},{9,1},{13,5},{2,10},{6,14},... | collective-permute-start | bytes 147464 | tf_op jit(solution)/shard_map/ppermute | solution.py:53

commit v4 on v3

--- a/solution.py
+++ b/solution.py
@@ -15,7 +15,10 @@
 KEPT = 5
 F32 = jnp.float32
 BF16 = jnp.bfloat16
-ATTR_VMEM = 30 * 1024 * 1024
+LIVE_VMEM = 4 * 1024 * 1024
+INLINE_VMEM = 22 * 1024 * 1024
+CROSS_VMEM = 16 * 1024 * 1024
+ATTR_VMEM = 22 * 1024 * 1024
 WHITEN_VMEM = 14 * 1024 * 1024
 
 
@@ -103,68 +106,181 @@
     return ones_where(iota((256, 128 * len(shifts)), 0) == source)
 
 
-def attributes_kernel(
-    two_sided, place_ref, live_smem, live_ref, taps_ref, own_ref, before_ref, after_ref, xh_ref, dh_ref,
-    attr_ref, gram_ref, bands, first0, first12, halo2, w2, w3, planes,
-    moves1, moves2,
+def side_flags():
+    x_left = jnp.where(lax.axis_index("xline") == 1, 1, 0)
+    depth_first = jnp.where(lax.axis_index("depth") == 0, 1, 0)
+    return x_left, depth_first, lax.axis_index("inline") % 2
+
+
+def live_kernel(trace_ref, seismic_ref, live_ref, near_ref, far_ref):
+    n_il, n_xl, _ = seismic_ref.shape
+    eye = iota((n_xl, n_xl), 0) == iota((n_xl, n_xl), 1)
+    for p in range(n_il):
+        row = jnp.broadcast_to(trace_ref[p : p + 1, :].astype(F32), (n_xl, n_xl))
+        kept = dot(jnp.where(eye, row, 0.0).astype(BF16), seismic_ref[p])
+        live_ref[p * n_xl : (p + 1) * n_xl, :] = kept.astype(BF16)
+    count = REACH * n_xl
+    start = (n_il - REACH) * n_xl
+    odd = side_flags()[2]
+
+    @pl.when(odd == 1)
+    def _():
+        near_ref[...] = live_ref[0:count]
+        far_ref[...] = live_ref[start : start + count]
+
+    @pl.when(odd == 0)
+    def _():
+        near_ref[...] = live_ref[start : start + count]
+        far_ref[...] = live_ref[0:count]
+
+
+def banded(level, taps_ref, bands, il_odd):
+    lane = iota((ORIENT, 128), 1)
+    cs = slice(level * ORIENT, (level + 1) * ORIENT)
+    cols = [jnp.broadcast_to(taps_ref[0, cs, k : k + 1], (ORIENT, 128)) for k in range(TAPS)]
+    for o in range(8):
+        total = jnp.zeros((ORIENT, 128), F32)
+        for k in range(TAPS):
+            p = 2 * o + 2 ** level * (k - 2)
+            if p < 0:
+                place = p + 32 - 8 * il_odd
+            elif p >= 16:
+                place = p + 8 * il_odd
+            else:
+                place = p
+            total = jnp.where(lane == place, cols[k], total)
+        bands[pl.ds(level * 256 + o * ORIENT, ORIENT), :] = total.astype(BF16)
+
+
+def phase_pick():
+    n = iota((256, 256), 1)
+    return ones_where(iota((256, 256), 0) == jnp.where(n < 128, 2 * n, 2 * n - 255))
+
+
+def inline_kernel(
+    taps_ref, own_ref, near_ref, far_ref, bands, w2, w3, first0, first12, edge_ref, planes
 ):
-    x_left = place_ref[0]
-    depth_first = place_ref[1]
-    stored = 48 if two_sided else 40
-
+    _, depth_first, il_odd = side_flags()
+
+    def put_edge(ts):
+        for at, ref in ((0, own_ref), (512, near_ref), (768, far_ref)):
+            edge_ref[at : at + ref.shape[0], :] = ref[:, ts]
+
+    pl.when(depth_first == 1)(lambda: put_edge(slice(128, 256)))
+    pl.when(depth_first == 0)(lambda: put_edge(slice(0, 128)))
     for k in range(TAPS):
         w2[k] = jnp.broadcast_to(taps_ref[1, :, k : k + 1], (CHAN, 128))
         w3[k] = jnp.broadcast_to(taps_ref[2, :, k : k + 1], (CHAN, 128))
-    lane32 = iota((ORIENT, 128), 1)
     for level in range(3):
-        cs = slice(level * ORIENT, (level + 1) * ORIENT)
-        cols = [jnp.broadcast_to(taps_ref[0, cs, k : k + 1], (ORIENT, 128)) for k in range(TAPS)]
-        for o in range(8):
-            total = jnp.zeros((ORIENT, 128), F32)
-            for k in range(TAPS):
-                total = jnp.where(lane32 == REACH + 2 * o + 2 ** level * (k - 2), cols[k], total)
-            bands[pl.ds(level * 256 + o * ORIENT, ORIENT), :] = total.astype(BF16)
-
-    n = iota((256, 256), 1)
-    pick = ones_where(iota((256, 256), 0) == jnp.where(n < 128, 2 * n, 2 * n - 255))
+        banded(level, taps_ref, bands, il_odd)
+
+    pick = phase_pick()
     r = iota((512, 512), 0)
     c = iota((512, 512), 1)
     turn = ones_where((c // 16 == r % 32) & (c % 16 == r // 32))
     own = dot(own_ref[...], pick).astype(BF16).reshape(16, 32, 256)
-    before = dot(before_ref[...], pick).astype(BF16).reshape(8, 32, 256)
-    after = dot(after_ref[...], pick).astype(BF16).reshape(8, 32, 256)
+    near = dot(near_ref[...], pick).astype(BF16).reshape(8, 32, 256)
+    far = dot(far_ref[...], pick).astype(BF16).reshape(8, 32, 256)
     for half in range(2):
         js = slice(half * 16, half * 16 + 16)
-        block = jnp.concatenate([before[:, js], own[:, js], after[:, js]], axis=0).reshape(512, 256)
-        planes[8 + half * 16 : 24 + half * 16] = dot(turn, block).astype(BF16).reshape(16, 32, 256)
-    turn_x = ones_where((c % 256 // 8 == r % 32) & (c // 256 * 8 + c % 8 == r // 32))
-    if two_sided:
-        sides = dot(xh_ref[...], pick).astype(BF16)
-    else:
-        got = dot(xh_ref[...], pick)
-        left = jnp.where(x_left == 1, 1.0, 0.0)
-        sides = jnp.concatenate([got * left, got * (1.0 - left)], axis=0).astype(BF16)
-    edges = dot(turn_x, sides).astype(BF16).reshape(16, 32, 256)
-    planes[0:8] = edges[0:8]
-    planes[40:48] = edges[8:16]
+        block = jnp.concatenate([own[:, js], near[:, js], far[:, js]], axis=0).reshape(512, 256)
+        planes[half * 16 : half * 16 + 16] = dot(turn, block).astype(BF16).reshape(16, 32, 256)
 
     a0 = bands[0:256, 0:32]
     a12 = bands[256:768, 0:32]
+    for j in (0, 1, 34):
+        first0[j] = jnp.zeros((256, 256), F32)
+    for j in (0, 1, 2, 3, 20, 21, 22, 23):
+        first12[j] = jnp.zeros((512, 128), F32)
 
     def level0_first(j, _):
-        first0[j] = rounded(dot(a0, planes[j + 6]))
+        first0[j + 2] = rounded(dot(a0, planes[j]))
         return 0
 
-    lax.fori_loop(0, 35, level0_first, 0, unroll=7)
+    lax.fori_loop(0, 32, level0_first, 0, unroll=8)
 
     def even_first(pair, _):
         both = jnp.concatenate([planes[4 * pair, :, 0:128], planes[4 * pair + 2, :, 0:128]], axis=1)
         out = rounded(dot(a12, both))
-        first12[2 * pair] = out[:, 0:128]
-        first12[2 * pair + 1] = out[:, 128:256]
+        first12[2 * pair + 4] = out[:, 0:128]
+        first12[2 * pair + 5] = out[:, 128:256]
         return 0
 
-    lax.fori_loop(0, 12, even_first, 0, unroll=4)
+    lax.fori_loop(0, 8, even_first, 0, unroll=4)
+
+
+def tall(ref, level, k):
+    return jnp.concatenate([ref[k, level * ORIENT : (level + 1) * ORIENT]] * 8, axis=0)
+
+
+def crossline_kernel(
+    two_sided, bands, w2, first12, xh_ref, extra0, second12, edges, extra1, extra2
+):
+    x_left = side_flags()[0]
+
+    r = iota((512, 512), 0)
+    c = iota((512, 512), 1)
+    turn_x = ones_where((c % 256 // 8 == r % 32) & (c // 256 * 8 + c % 8 == r // 32))
+    got = dot(xh_ref[...], phase_pick())
+    if not two_sided:
+        left = jnp.where(x_left == 1, 1.0, 0.0)
+        got = jnp.concatenate([got * left, got * (1.0 - left)], axis=0)
+    edges[...] = dot(turn_x, got.astype(BF16)).astype(BF16).reshape(16, 32, 256)
+    a0 = bands[0:256, 0:32]
+    a12 = bands[256:768, 0:32]
+    out0 = {j: rounded(dot(a0, edges[slot])) for j, slot in ((-2, 6), (-1, 7), (32, 8))}
+    out12 = {}
+    for slot in (0, 4, 8, 12):
+        both = jnp.concatenate([edges[slot, :, 0:128], edges[slot + 2, :, 0:128]], axis=1)
+        out = rounded(dot(a12, both))
+        e = slot // 2 - 4 if slot < 8 else slot // 2 + 12
+        out12[e], out12[e + 1] = out[:, 0:128], out[:, 128:256]
+
+    extra0[0] = jnp.zeros((256, 256), F32)
+    for slot, q in ((1, 0), (2, 15)):
+        total = jnp.zeros((256, 256), F32)
+        for k in range(TAPS):
+            if 2 * q + k - 2 in out0:
+                total = total + jnp.concatenate([tall(w2, 0, k)] * 2, axis=1) * out0[2 * q + k - 2]
+        extra0[slot] = total
+    for level, extra in ((1, extra1), (2, extra2)):
+        reach = 2 * level
+        extra[0] = jnp.zeros((256, 128), F32)
+        for slot in range(2 * reach):
+            q = slot if slot < reach else 16 - 2 * reach + slot
+            total = jnp.zeros((256, 128), F32)
+            for k in range(TAPS):
+                e = q + level * (k - 2)
+                if e in out12:
+                    total = total + tall(w2, level, k) * out12[e][(level - 1) * 256 : level * 256]
+            extra[slot + 1] = total
+
+    def one_q(q, _):
+        for level in (1, 2):
+            extra = extra1 if level == 1 else extra2
+            reach = 2 * level
+            slot = jnp.where(q < reach, q + 1, jnp.where(q >= 16 - reach, q + 2 * reach - 15, 0))
+            for c16 in range(2):
+                start = level * ORIENT + c16 * 16
+                s2 = [w2[k, start : start + 16] for k in range(TAPS)]
+                for o in range(8):
+                    row = o * ORIENT + c16 * 16
+                    here = slice((level - 1) * 256 + row, (level - 1) * 256 + row + 16)
+                    total = extra[slot, row : row + 16, :]
+                    for k in range(TAPS):
+                        total = total + s2[k] * first12[q + 4 + level * (k - 2), here, :]
+                    second12[q, here, :] = total.astype(BF16)
+        return 0
+
+    lax.fori_loop(0, 16, one_q, 0)
+
+
+def attributes_kernel(
+    two_sided, live_smem, live_ref, bands, w2, w3, first0, extra0, second12, dh_ref,
+    attr_ref, gram_ref, halo2, moves1, moves2,
+):
+    x_left, depth_first, _ = side_flags()
+    stored = 48 if two_sided else 40
 
     n = iota((1, 256), 1)
     kept = n // stored
@@ -179,13 +295,12 @@
     for level in range(3):
         cols = dot(lanes, halo_select(level, stored, x_left, depth_first)).astype(BF16)
         part = rounded(dot(bands[level * 256 : level * 256 + 256, 0:32], cols))
-        cs = slice(level * ORIENT, (level + 1) * ORIENT)
         total = jnp.zeros((256, 128), F32)
         for k in range(TAPS):
-            total = total + part[:, k * 128 : k * 128 + 128] * jnp.concatenate([w2[k, cs]] * 8, axis=0)
+            total = total + part[:, k * 128 : k * 128 + 128] * tall(w2, level, k)
         total = rounded(total)
         if level == 0:
-            w3_0, w3_1, w3_4 = [jnp.concatenate([w3[k, cs]] * 8, axis=0) for k in (0, 1, 4)]
+            w3_0, w3_1, w3_4 = [tall(w3, 0, k) for k in (0, 1, 4)]
             before_first = total * w3_0 + pltpu.roll(total, 1, 1) * w3_1
             total = jnp.where(iota((256, 128), 1) % 8 == 7, before_first, total * w3_4)
         halo2[level] = total
@@ -193,45 +308,45 @@
     moves1[...] = shift_matrix((-2, -1, 1, 2))
     moves2[...] = shift_matrix((-4, -2, 2, 4))
 
-    def crossline(level, q, o, half=0):
-        cs = slice(level * ORIENT, (level + 1) * ORIENT)
-        s2 = [w2[k, cs] for k in range(TAPS)]
-        if level == 0:
-            rows = slice(o * ORIENT, (o + 1) * ORIENT)
-            ts = slice(half * 128, half * 128 + 128)
-            return sum(s2[k] * first0[2 * q + k, rows, ts] for k in range(TAPS))
-        rows = slice((level - 1) * 256 + o * ORIENT, (level - 1) * 256 + (o + 1) * ORIENT)
-        unit = 2 ** (level - 1)
-        return sum(s2[k] * first12[q + 4 + unit * (k - 2), rows, :] for k in range(TAPS))
-
     def one_q(q):
         align = jnp.where(q == 0, 0, 128 - 8 * q)
-
-        def put(o, level, total):
-            total = total * live_smem[2 * o, 2 * q].astype(F32)
-            attr_ref[o * 16 + q, level * ORIENT : (level + 1) * ORIENT, :] = total.astype(BF16)
+        live_q = [live_smem[2 * o, 2 * q].astype(F32) for o in range(8)]
+        lane = iota((16, 128), 1)
+
+        def put(o, start, total):
+            attr_ref[o * 16 + q, start : start + 16, :] = (total * live_q[o]).astype(BF16)
 
         for level in (1, 2):
             halo = pltpu.roll(halo2[level], align, 1).astype(BF16)
-            value = jnp.concatenate([crossline(level, q, o).astype(BF16) for o in range(8)], axis=0)
-            joined = jnp.concatenate([value, halo], axis=1)
-            moved = dot(joined, (moves1 if level == 1 else moves2)[...])
-            s3 = [w3[k, level * ORIENT : (level + 1) * ORIENT] for k in range(TAPS)]
+            value = second12[q, (level - 1) * 256 : level * 256, :]
+            moved = dot(jnp.concatenate([value, halo], axis=1), (moves1 if level == 1 else moves2)[...])
+            for c16 in range(2):
+                start = level * ORIENT + c16 * 16
+                s3 = [w3[k, start : start + 16] for k in range(TAPS)]
+                for o in range(8):
+                    rows = slice(o * ORIENT + c16 * 16, o * ORIENT + c16 * 16 + 16)
+                    total = s3[2] * value[rows].astype(F32)
+                    for i, k in enumerate((0, 1, 3, 4)):
+                        total = total + s3[k] * moved[rows, i * 128 : i * 128 + 128]
+                    put(o, start, total)
+        slot = jnp.where(q == 0, 1, jnp.where(q == 15, 2, 0))
+        for c16 in range(2):
+            s2 = [w2[k, c16 * 16 : c16 * 16 + 16] for k in range(TAPS)]
+            s3 = [w3[k, c16 * 16 : c16 * 16 + 16] for k in range(TAPS)]
             for o in range(8):
-                rows = slice(o * ORIENT, (o + 1) * ORIENT)
-                total = s3[2] * value[rows].astype(F32)
-                for i, k in enumerate((0, 1, 3, 4)):
-                    total = total + s3[k] * moved[rows, i * 128 : i * 128 + 128]
-                put(o, level, total)
-        lane = iota((ORIENT, 128), 1)
-        s3 = [w3[k, 0:ORIENT] for k in range(TAPS)]
-        for o in range(8):
-            even, odd = rounded(crossline(0, q, o, 0)), rounded(crossline(0, q, o, 1))
-            halo = pltpu.roll(halo2[0, o * ORIENT : (o + 1) * ORIENT], align, 1)
-            back = jnp.where(lane == 127, halo, s3[0] * even + s3[1] * odd)
-            ahead = jnp.where(lane == 0, halo, s3[4] * even)
-            moved = pltpu.roll(back, 1, 1) + pltpu.roll(ahead, 127, 1)
-            put(o, 0, s3[2] * even + s3[3] * odd + moved)
+                rows = slice(o * ORIENT + c16 * 16, o * ORIENT + c16 * 16 + 16)
+                both = []
+                for ts in (slice(0, 128), slice(128, 256)):
+                    total = extra0[slot, rows, ts]
+                    for k in range(TAPS):
+                        total = total + s2[k] * first0[2 * q + k, rows, ts]
+                    both.append(rounded(total))
+                even, odd = both
+                halo = pltpu.roll(halo2[0, rows], align, 1)
+                back = jnp.where(lane == 127, halo, s3[0] * even + s3[1] * odd)
+                ahead = jnp.where(lane == 0, halo, s3[4] * even)
+                moved = pltpu.roll(back, 1, 1) + pltpu.roll(ahead, 127, 1)
+                put(o, c16 * 16, s3[2] * even + s3[3] * odd + moved)
 
     def add_gram(q, total):
         for o in range(0, 8, 2):
@@ -356,59 +471,98 @@
 def local(seismic, trace_live, filter_taps):
     il_len, xl_len, t_len = seismic.shape
     assert (il_len, xl_len, t_len) == (16, 32, 256) and lax.axis_size("depth") == 2
-    live = seismic * trace_live.astype(BF16)[:, :, None]
     taps = filter_taps.astype(F32)
     x_index = lax.axis_index("xline")
     d_index = lax.axis_index("depth")
     two_sided = lax.axis_size("xline") > 2
-
-    before = shifted(live[il_len - REACH :], "inline", 1)
-    after = shifted(live[:REACH], "inline", -1)
+    vmem = pl.BlockSpec(memory_space=pltpu.VMEM)
+    smem = pl.BlockSpec(memory_space=pltpu.SMEM)
+
+    live, near, far = pl.pallas_call(
+        live_kernel,
+        out_shape=(
+            jax.ShapeDtypeStruct((il_len * xl_len, t_len), BF16),
+            jax.ShapeDtypeStruct((REACH * xl_len, t_len), BF16),
+            jax.ShapeDtypeStruct((REACH * xl_len, t_len), BF16),
+        ),
+        in_specs=[vmem] * 2,
+        out_specs=(vmem,) * 3,
+        compiler_params=pltpu.CompilerParams(vmem_limit_bytes=LIVE_VMEM),
+        name="live",
+    )(trace_live, seismic)
+    il_size = lax.axis_size("inline")
+    near_pairs = [(i, i ^ 1) for i in range(il_size) if i ^ 1 < il_size]
+    far_pairs = [(i, i - 1 if i % 2 == 0 else i + 1) for i in range(1, il_size)]
+    far_pairs = [(i, j) for i, j in far_pairs if j < il_size]
+    near = lax.ppermute(near, "inline", near_pairs)
+    far = lax.ppermute(far, "inline", far_pairs)
+    parts = [v.reshape(-1, xl_len, t_len) for v in (live, near, far)]
 
     def stack(js):
-        return jnp.concatenate([before[:, js], live[:, js], after[:, js]], axis=0)
+        return jnp.concatenate([v[:, js] for v in parts], axis=0)
 
     low, high = slice(0, REACH), slice(xl_len - REACH, xl_len)
     if two_sided:
         xh = [shifted(stack(high), "xline", 1), shifted(stack(low), "xline", -1)]
     else:
         xh = [flipped(jnp.where(x_index == 0, stack(high), stack(low)), [("xline", 1)])]
-    def edge(ts):
-        rows = jnp.concatenate([before[:, :, ts], live[:, :, ts], after[:, :, ts]], axis=0)
-        return jnp.concatenate([rows] + [x[:, :, ts] for x in xh], axis=1)
-
-    dh = jnp.where(d_index == 0, edge(slice(t_len - 128, t_len)), edge(slice(0, 128)))
+    bands, w2, w3, first0, first12, edge = pl.pallas_call(
+        inline_kernel,
+        out_shape=(
+            jax.ShapeDtypeStruct((3 * 256, 128), BF16),
+            jax.ShapeDtypeStruct((TAPS, CHAN, 128), F32),
+            jax.ShapeDtypeStruct((TAPS, CHAN, 128), F32),
+            jax.ShapeDtypeStruct((35, 256, 256), F32),
+            jax.ShapeDtypeStruct((24, 512, 128), F32),
+            jax.ShapeDtypeStruct((32 * xl_len, 128), BF16),
+        ),
+        in_specs=[vmem] * 4,
+        out_specs=(vmem,) * 6,
+        scratch_shapes=[pltpu.VMEM((32, 32, 256), BF16)],
+        compiler_params=pltpu.CompilerParams(vmem_limit_bytes=INLINE_VMEM),
+        cost_estimate=pl.CostEstimate(flops=4 * 10**9, bytes_accessed=16 * 10**6, transcendentals=0),
+        name="inline",
+    )(taps, live, near, far)
+
+    def side(x):
+        return jnp.where(d_index == 0, x[:, :, t_len - 128 :], x[:, :, :128])
+
+    dh = jnp.concatenate([edge.reshape(32, xl_len, 128)] + [side(x) for x in xh], axis=1)
     dh = flipped(dh, [("depth", 1)])
-
-    place = jnp.stack([(x_index == 1).astype(jnp.int32), (d_index == 0).astype(jnp.int32)])
-    vmem = pl.BlockSpec(memory_space=pltpu.VMEM)
-    smem = pl.BlockSpec(memory_space=pltpu.SMEM)
     xrows = jnp.concatenate([x.reshape(256, t_len) for x in xh], axis=0)
+    extra0, second12 = pl.pallas_call(
+        functools.partial(crossline_kernel, two_sided),
+        out_shape=(
+            jax.ShapeDtypeStruct((3, 256, 256), F32),
+            jax.ShapeDtypeStruct((16, 512, 128), BF16),
+        ),
+        in_specs=[vmem] * 4,
+        out_specs=(vmem,) * 2,
+        scratch_shapes=[
+            pltpu.VMEM((16, 32, 256), BF16),
+            pltpu.VMEM((5, 256, 128), F32),
+            pltpu.VMEM((9, 256, 128), F32),
+        ],
+        compiler_params=pltpu.CompilerParams(vmem_limit_bytes=CROSS_VMEM),
+        cost_estimate=pl.CostEstimate(flops=3 * 10**9, bytes_accessed=9 * 10**6, transcendentals=0),
+        name="crossline",
+    )(bands, w2, first12, xrows)
     attr, gram = pl.pallas_call(
         functools.partial(attributes_kernel, two_sided),
         out_shape=(
             jax.ShapeDtypeStruct((128, CHAN, 128), BF16),
             jax.ShapeDtypeStruct((CHAN, 128), F32),
         ),
-        in_specs=[smem, smem] + [vmem] * 7,
+        in_specs=[smem] + [vmem] * 8,
         out_specs=(vmem, vmem),
         scratch_shapes=[
-            pltpu.VMEM((768, 128), BF16),
-            pltpu.VMEM((35, 256, 256), F32),
-            pltpu.VMEM((24, 512, 128), F32),
             pltpu.VMEM((3, 256, 128), F32),
-            pltpu.VMEM((TAPS, CHAN, 128), F32),
-            pltpu.VMEM((TAPS, CHAN, 128), F32),
-            pltpu.VMEM((48, 32, 256), BF16),
             pltpu.VMEM((256, 512), BF16),
             pltpu.VMEM((256, 512), BF16),
         ],
         compiler_params=pltpu.CompilerParams(vmem_limit_bytes=ATTR_VMEM),
         name="attributes",
-    )(
-        place, trace_live, trace_live, taps, live.reshape(512, t_len),
-        before.reshape(256, t_len), after.reshape(256, t_len), xrows, dh,
-    )
+    )(trace_live, trace_live, bands, w2, w3, first0, extra0, second12, dh)
 
     mine, other = summed(gram)
     out, factor = pl.pallas_call(

time: 57.9 us -> 53.8 us (0.929)
  waiting for transfers between devices: 14.7 us -> 11.8 us
  starting transfers between devices: 16.1 us -> 13.5 us
  local copies, waits for them, and re-layouts: 0.29 us -> 2.49 us
  other arithmetic: 2.06 us -> 0.1 us
  Pallas kernels: 23.8 us -> 24.8 us
    pallas_call x0 -> x3, Pallas kernels: none -> 6.53 us  [the longest x1 3.43 us: local(): pl.pallas_call(inline_kernel, out_shape=(jax.ShapeDtypeStruct((3 * 256, 1...]
    pallas_call x1, Pallas kernels: 14.7 us -> 9.25 us  [local(): pl.pallas_call(functools.partial(attributes_kernel, two_sided), out_shape...]
    ppermute x2, starting transfers between devices: 6.86 us -> 3.74 us  [the longest x1 3.08 us: local(): near = lax.ppermute(near, 'inline', near_pairs)]
    ppermute x7, waiting for transfers between devices: 12.1 us -> 9.82 us  [flipped(): return lax.ppermute(value, axes, pairs)]
    unnamed x4 -> x6, local copies, waits for them, and re-layouts: 0.01 us -> 1.65 us
    mul x1 -> x0, other arithmetic: 1.08 us -> none  [local(): live = seismic * trace_live.astype(BF16)[:, :, None]]
    convert_element_type x1 -> x0, other arithmetic: 0.75 us -> none  [local(): live = seismic * trace_live.astype(BF16)[:, :, None]]
    convert_element_type x1, local copies, waits for them, and re-layouts: 0.14 us -> 0.82 us  [local(): taps = filter_taps.astype(F32)]
  transfers between devices with their start and end apart: 9 -> 9, of which waited for: 9 -> 6; matrix products, arithmetic and copies ran while one was open for 1% -> 2% of each run, Pallas kernels for 0% -> 12%
where the time goes in v4:
time: 53.8 us; the launch traced here: 53.5 us
  Pallas kernels  24.8 us (46%)
  starting transfers between devices  13.5 us (25%)
  waiting for transfers between devices  11.8 us (22%)
  local copies, waits for them, and re-layouts  2.49 us (5%)
  between operations  0.78 us (1%)
    ppermute x7, waiting for transfers between devices, flipped(): return lax.ppermute(value, axes, pairs)  9.82 us
    ppermute x7, starting transfers between devices, flipped(): return lax.ppermute(value, axes, pairs)  9.77 us
    pallas_call x1, Pallas kernels, local(): pl.pallas_call(functools.partial(attributes_kernel, two_sided), out_shape...  9.25 us
    pallas_call x1, Pallas kernels, local(): pl.pallas_call(whiten_kernel, grid=(4,), out_shape=(jax.ShapeDtypeStruct(...  9.06 us
    pallas_call x1, Pallas kernels, local(): pl.pallas_call(inline_kernel, out_shape=(jax.ShapeDtypeStruct((3 * 256, 1...  3.43 us
    ppermute x1, starting transfers between devices, local(): near = lax.ppermute(near, 'inline', near_pairs)  3.08 us
    pallas_call x1, Pallas kernels, local(): pl.pallas_call(functools.partial(crossline_kernel, two_sided), out_shape=...  2.88 us
    ppermute x1, waiting for transfers between devices, local(): near = lax.ppermute(near, 'inline', near_pairs)  1.98 us
  transfers between devices with their start and end apart: 9, of which 6 were waited for; matrix products, arithmetic and copies ran while one was open for 2% of the time, Pallas kernels for 12%

profile of v4, /device:TPU:0, one launch (start us, length us, event | category | flops | bytes accessed | tf_op | source)
XLA Modules:
  0.0 53.5 jit_solution(13345262000171719389)
XLA Ops:
  0.6 0.0 copy-start
  0.6 0.9 %copy-done = bf16[16,32,256]{2,1,0:T(8,128)(2,1)S(1)} copy-done((bf16[16,32,256]{2,1,0:T(8,128)(2,1)S(1)}, bf16[16,32,256]{2,1,0:T(8,128)(2,1)}, u32[]{:S(2)}) %copy-start) | copy-done | bytes 262168
  1.6 0.0 copy-start.1
  1.6 0.7 %copy-done.1 = s32[16,32]{1,0:T(8,128)S(1)} copy-done((s32[16,32]{1,0:T(8,128)S(1)}, s32[16,32]{1,0:T(8,128)}, u32[]{:S(2)}) %copy-start.1) | copy-done | bytes 2072
  2.3 0.2 live.1
  2.5 3.1 %collective-permute-start = (bf16[256,256]{1,0:T(8,128)(2,1)S(1)}, bf16[256,256]{1,0:T(8,128)(2,1)S(1)}, u32[]{:S(2)}, u32[]{:S(2)}) collective-permute-start(bf16[256,256]{1,0:T(8,128)(2,1)S(1)} %get-tuple-element.16), channel_id=1, source_target_pairs={{0,4},{4,0},{8,12},{12,8},{1,5},{5,1},{9,13},{13,9},{2,6},{6,2},{1... | collective-permute-start | bytes 393224 | tf_op jit(solution)/shard_map/ppermute | solution.py:497
  5.6 0.7 %collective-permute-start.1 = (bf16[256,256]{1,0:T(8,128)(2,1)S(1)}, bf16[256,256]{1,0:T(8,128)(2,1)S(1)}, u32[]{:S(2)}, u32[]{:S(2)}) collective-permute-start(bf16[256,256]{1,0:T(8,128)(2,1)S(1)} %get-tuple-element.17), channel_id=1, source_target_pairs={{4,8},{8,4},{5,9},{9,5},{6,10},{10,6},{7,11},{11,7},{20,24},{24,20... | collective-permute-start | bytes 393224 | tf_op jit(solution)/shard_map/ppermute | solution.py:498
  6.3 0.8 %copy.6.taps_ref = f32[3,96,5]{2,1,0:T(8,128)S(1)} copy(bf16[3,96,5]{1,0,2:T(4,128)(2,1)} %param.5) | data formatting | bytes 8640 | tf_op jit(solution)/shard_map/convert_element_type | solution.py:474
  7.1 2.0 %collective-permute-done.near_ref = bf16[256,256]{1,0:T(8,128)(2,1)S(1)} collective-permute-done((bf16[256,256]{1,0:T(8,128)(2,1)S(1)}, bf16[256,256]{1,0:T(8,128)(2,1)S(1)}, u32[]{:S(2)}, u32[]{:S(2)}) %collective-permute-start) | collective-permute-done | bytes 131104 | tf_op jit(solution)/shard_map/ppermute | solution.py:497
  9.1 0.0 collective-permute-done.1.far_ref
  9.2 1.7 %collective-permute-start.2 = (bf16[32,8,256]{2,1,0:T(8,128)(2,1)S(1)}, bf16[32,8,256]{2,1,0:T(8,128)(2,1)S(1)}, u32[]{:S(2)}, u32[]{:S(2)}) collective-permute-start(bf16[32,8,256]{2,1,0:T(8,128)(2,1)S(1)} %maximum_select_fusion), channel_id=1, source_target_pairs={{0,2},{2,0},{1,3},{3,1},{4,6},{6,4},{5,7},{7,5},{8,10},{10,8},{9,1... | collective-permute-start | bytes 393224 | tf_op jit(solution)/shard_map/ppermute | solution.py:56
  10.9 3.4 %inline.1 = (bf16[768,128]{1,0:T(8,128)(2,1)S(1)}, f32[5,96,128]{2,1,0:T(8,128)S(1)}, f32[5,96,128]{2,1,0:T(8,128)S(1)}, f32[35,256,256]{2,1,0:T(8,128)S(1)}, f3...) custom-call(f32[3,96,5]{2,1,0:T(8,128)S(1)} %copy.6.taps_ref, bf16[512,256]{1,0:T(8,128)(2,1)S(1)} %get-tuple-element.15.own_ref, ...), custom_call_target="tpu_custom_call" | custom-call | flops 4000000000 | bytes 16000000 | tf_op jit(solution)/shard_map/inline/pallas_call | solution.py:509
  14.3 0.0 collective-permute-done.2
  14.4 0.1 collective-permute-start.3
  14.5 0.0 copy-start.2
  14.5 2.9 %crossline.1 = (f32[3,256,256]{2,1,0:T(8,128)S(1)}, bf16[16,512,128]{2,1,0:T(8,128)(2,1)S(1)}) custom-call(bf16[768,128]{1,0:T(8,128)(2,1)S(1)} %get-tuple-element.18.bands, f32[5,96,128]{2,1,0:T(8,128)S(1)} %get-tuple-element.19.w2, f32[24,512,128]{2,1,0:T(8,128)S(1)} %get-tuple-element.22.first12, bf16[256,256]{1,0:T(8,128)(2,1)S(1)} %bitcast.6), custom_call_target="tpu_custom_call" | custom-call | flops 3000000000 | bytes 9000000 | tf_op jit(solution)/shard_map/crossline/pallas_call | solution.py:533
  17.4 0.0 collective-permute-done.3.dh_ref
  17.4 0.0 copy-done.2
  17.4 9.2 %attributes.1 = (bf16[128,96,128]{2,1,0:T(8,128)(2,1)S(1)}, f32[96,128]{1,0:T(8,128)S(1)}) custom-call(s32[16,32]{1,0:T(8,128)S(1)} %copy-done.2, s32[16,32]{1,0:T(8,128)S(1)} %copy-done.2, bf16[768,128]{1,0:T(8,128)(2,1)S(1)} %get-tuple-element.18.bands, f32[5,96,128]{2,1,0:T(8,128)S(1)} %get-tuple-element.19.w2, f32[5,96,128]{2,1,0:T(8,128)S(1)} %get-tuple-element.20.w3, ...), custom_call_target="tpu_custom_call" | custom-call | tf_op jit(solution)/shard_map/attributes/pallas_call | solution.py:550
  26.6 0.6 %collective-permute-start.4 = (f32[96,128]{1,0:T(8,128)S(1)}, f32[96,128]{1,0:T(8,128)S(1)}, u32[]{:S(2)}, u32[]{:S(2)}) collective-permute-start(f32[96,128]{1,0:T(8,128)S(1)} %get-tuple-element.26), channel_id=1, source_target_pairs={{0,1},{1,0},{2,3},{3,2},{4,5},{5,4},{6,7},{7,6},{8,9},{9,8},{10,11... | collective-permute-start | bytes 147464 | tf_op jit(solution)/shard_map/ppermute | solution.py:56
  27.2 0.9 %collective-permute-done.4 = f32[96,128]{1,0:T(8,128)S(1)} collective-permute-done((f32[96,128]{1,0:T(8,128)S(1)}, f32[96,128]{1,0:T(8,128)S(1)}, u32[]{:S(2)}, u32[]{:S(2)}) %collective-permute-start.4) | collective-permute-done | bytes 49184 | tf_op jit(solution)/shard_map/ppermute | solution.py:56
  28.1 4.6 %collective-permute-start.5 = (f32[96,128]{1,0:T(8,128)S(1)}, f32[96,128]{1,0:T(8,128)S(1)}, u32[]{:S(2)}, u32[]{:S(2)}) collective-permute-start(f32[96,128]{1,0:T(8,128)S(1)} %add.12), channel_id=1, source_target_pairs={{0,4},{4,0},{8,12},{12,8},{1,5},{5,1},{9,13},{13,9},{2,6},{6,2},{1... | collective-permute-start | bytes 147464 | tf_op jit(solution)/shard_map/ppermute | solution.py:56
  32.7 1.5 %collective-permute-start.6 = (f32[96,128]{1,0:T(8,128)S(1)}, f32[96,128]{1,0:T(8,128)S(1)}, u32[]{:S(2)}, u32[]{:S(2)}) collective-permute-start(f32[96,128]{1,0:T(8,128)S(1)} %add.12), channel_id=1, source_target_pairs={{0,2},{2,0},{1,3},{3,1},{4,6},{6,4},{5,7},{7,5},{8,10},{10,8},{9,1... | collective-permute-start | bytes 147464 | tf_op jit(solution)/shard_map/ppermute | solution.py:56
  34.2 0.0 collective-permute-start.7
  34.2 0.8 %collective-permute-done.5 = f32[96,128]{1,0:T(8,128)S(1)} collective-permute-done((f32[96,128]{1,0:T(8,128)S(1)}, f32[96,128]{1,0:T(8,128)S(1)}, u32[]{:S(2)}, u32[]{:S(2)}) %collective-permute-start.5) | collective-permute-done | bytes 49184 | tf_op jit(solution)/shard_map/ppermute | solution.py:56
  35.0 1.8 %collective-permute-done.6 = f32[96,128]{1,0:T(8,128)S(1)} collective-permute-done((f32[96,128]{1,0:T(8,128)S(1)}, f32[96,128]{1,0:T(8,128)S(1)}, u32[]{:S(2)}, u32[]{:S(2)}) %collective-permute-start.6) | collective-permute-done | bytes 49184 | tf_op jit(solution)/shard_map/ppermute | solution.py:56
  36.8 2.4 %collective-permute-done.7 = f32[96,128]{1,0:T(8,128)S(1)} collective-permute-done((f32[96,128]{1,0:T(8,128)S(1)}, f32[96,128]{1,0:T(8,128)S(1)}, u32[]{:S(2)}, u32[]{:S(2)}) %collective-permute-start.7) | collective-permute-done | bytes 49184 | tf_op jit(solution)/shard_map/ppermute | solution.py:56
  39.2 1.3 %collective-permute-start.8 = (f32[96,128]{1,0:T(8,128)S(1)}, f32[96,128]{1,0:T(8,128)S(1)}, u32[]{:S(2)}, u32[]{:S(2)}) collective-permute-start(f32[96,128]{1,0:T(8,128)S(1)} %add_add_fusion.mine_ref), channel_id=1, source_target_pairs={{0,8},{4,12},{8,0},{12,4},{1,9},{5,13},{9,1},{13,5},{2,10},{6,14},... | collective-permute-start | bytes 147464 | tf_op jit(solution)/shard_map/ppermute | solution.py:56
  40.5 4.0 %collective-permute-done.8.other_ref = f32[96,128]{1,0:T(8,128)S(1)} collective-permute-done((f32[96,128]{1,0:T(8,128)S(1)}, f32[96,128]{1,0:T(8,128)S(1)}, u32[]{:S(2)}, u32[]{:S(2)}) %collective-permute-start.8) | collective-permute-done | bytes 49184 | tf_op jit(solution)/shard_map/ppermute | solution.py:56
  44.5 9.1 %whiten.1 = (bf16[96,8,16,128]{3,2,1,0:T(8,128)(2,1)}, f32[96,96]{1,0:T(8,128)}) custom-call(f32[96,128]{1,0:T(8,128)S(1)} %add_add_fusion.mine_ref, f32[96,128]{1,0:T(8,128)S(1)} %collective-permute-done.8.other_ref, bf16[128,96,128]{2,1,0:T(8,128)(2,1)S(1)} %get-tuple-element.27.attr_ref), custom_call_target="tpu_custom_call" | custom-call | tf_op jit(solution)/shard_map/whiten/pallas_call | solution.py:568
  (8 shorter events, 0.1 us)
Async XLA Ops:
  0.6 1.0 %copy-start = (bf16[16,32,256]{2,1,0:T(8,128)(2,1)S(1)}, bf16[16,32,256]{2,1,0:T(8,128)(2,1)}, u32[]{:S(2)}) copy-start(bf16[16,32,256]{2,1,0:T(8,128)(2,1)} %seismic_ref.1) | copy-start | bytes 786436
  1.6 0.7 %copy-start.1 = (s32[16,32]{1,0:T(8,128)S(1)}, s32[16,32]{1,0:T(8,128)}, u32[]{:S(2)}) copy-start(s32[16,32]{1,0:T(8,128)} %live_ref.1) | copy-start | bytes 6148
  2.5 6.6 %collective-permute-start = (bf16[256,256]{1,0:T(8,128)(2,1)S(1)}, bf16[256,256]{1,0:T(8,128)(2,1)S(1)}, u32[]{:S(2)}, u32[]{:S(2)}) collective-permute-start(bf16[256,256]{1,0:T(8,128)(2,1)S(1)} %get-tuple-element.16), channel_id=1, source_target_pairs={{0,4},{4,0},{8,12},{12,8},{1,5},{5,1},{9,13},{13,9},{2,6},{6,2},{1... | collective-permute-start | bytes 393224 | tf_op jit(solution)/shard_map/ppermute | solution.py:497
  5.6 3.5 %collective-permute-start.1 = (bf16[256,256]{1,0:T(8,128)(2,1)S(1)}, bf16[256,256]{1,0:T(8,128)(2,1)S(1)}, u32[]{:S(2)}, u32[]{:S(2)}) collective-permute-start(bf16[256,256]{1,0:T(8,128)(2,1)S(1)} %get-tuple-element.17), channel_id=1, source_target_pairs={{4,8},{8,4},{5,9},{9,5},{6,10},{10,6},{7,11},{11,7},{20,24},{24,20... | collective-permute-start | bytes 393224 | tf_op jit(solution)/shard_map/ppermute | solution.py:498
  9.2 5.2 %collective-permute-start.2 = (bf16[32,8,256]{2,1,0:T(8,128)(2,1)S(1)}, bf16[32,8,256]{2,1,0:T(8,128)(2,1)S(1)}, u32[]{:S(2)}, u32[]{:S(2)}) collective-permute-start(bf16[32,8,256]{2,1,0:T(8,128)(2,1)S(1)} %maximum_select_fusion), channel_id=1, source_target_pairs={{0,2},{2,0},{1,3},{3,1},{4,6},{6,4},{5,7},{7,5},{8,10},{10,8},{9,1... | collective-permute-start | bytes 393224 | tf_op jit(solution)/shard_map/ppermute | solution.py:56
  14.4 3.0 %collective-permute-start.3 = (bf16[32,40,128]{2,1,0:T(8,128)(2,1)S(1)}, bf16[32,40,128]{2,1,0:T(8,128)(2,1)S(1)}, u32[]{:S(2)}, u32[]{:S(2)}) collective-permute-start(bf16[32,40,128]{2,1,0:T(8,128)(2,1)S(1)} %pad_maximum_fusion), channel_id=1, source_target_pairs={{0,1},{1,0},{2,3},{3,2},{4,5},{5,4},{6,7},{7,6},{8,9},{9,8},{10,11... | collective-permute-start | bytes 983048 | tf_op jit(solution)/shard_map/ppermute | solution.py:56
  14.5 2.9 %copy-start.2 = (s32[16,32]{1,0:T(8,128)S(1)}, s32[16,32]{1,0:T(8,128)}, u32[]{:S(2)}) copy-start(s32[16,32]{1,0:T(8,128)} %live_ref.1) | copy-start | bytes 6148
  26.6 1.4 %collective-permute-start.4 = (f32[96,128]{1,0:T(8,128)S(1)}, f32[96,128]{1,0:T(8,128)S(1)}, u32[]{:S(2)}, u32[]{:S(2)}) collective-permute-start(f32[96,128]{1,0:T(8,128)S(1)} %get-tuple-element.26), channel_id=1, source_target_pairs={{0,1},{1,0},{2,3},{3,2},{4,5},{5,4},{6,7},{7,6},{8,9},{9,8},{10,11... | collective-permute-start | bytes 147464 | tf_op jit(solution)/shard_map/ppermute | solution.py:56
  28.1 6.9 %collective-permute-start.5 = (f32[96,128]{1,0:T(8,128)S(1)}, f32[96,128]{1,0:T(8,128)S(1)}, u32[]{:S(2)}, u32[]{:S(2)}) collective-permute-start(f32[96,128]{1,0:T(8,128)S(1)} %add.12), channel_id=1, source_target_pairs={{0,4},{4,0},{8,12},{12,8},{1,5},{5,1},{9,13},{13,9},{2,6},{6,2},{1... | collective-permute-start | bytes 147464 | tf_op jit(solution)/shard_map/ppermute | solution.py:56
  32.7 4.1 %collective-permute-start.6 = (f32[96,128]{1,0:T(8,128)S(1)}, f32[96,128]{1,0:T(8,128)S(1)}, u32[]{:S(2)}, u32[]{:S(2)}) collective-permute-start(f32[96,128]{1,0:T(8,128)S(1)} %add.12), channel_id=1, source_target_pairs={{0,2},{2,0},{1,3},{3,1},{4,6},{6,4},{5,7},{7,5},{8,10},{10,8},{9,1... | collective-permute-start | bytes 147464 | tf_op jit(solution)/shard_map/ppermute | solution.py:56
  34.2 5.0 %collective-permute-start.7 = (f32[96,128]{1,0:T(8,128)S(1)}, f32[96,128]{1,0:T(8,128)S(1)}, u32[]{:S(2)}, u32[]{:S(2)}) collective-permute-start(f32[96,128]{1,0:T(8,128)S(1)} %add.12), channel_id=1, source_target_pairs={{0,6},{2,4},{4,2},{6,0},{8,14},{10,12},{12,10},{14,8},{1,7},{3,5},... | collective-permute-start | bytes 147464 | tf_op jit(solution)/shard_map/ppermute | solution.py:56
  39.2 5.3 %collective-permute-start.8 = (f32[96,128]{1,0:T(8,128)S(1)}, f32[96,128]{1,0:T(8,128)S(1)}, u32[]{:S(2)}, u32[]{:S(2)}) collective-permute-start(f32[96,128]{1,0:T(8,128)S(1)} %add_add_fusion.mine_ref), channel_id=1, source_target_pairs={{0,8},{4,12},{8,0},{12,4},{1,9},{5,13},{9,1},{13,5},{2,10},{6,14},... | collective-permute-start | bytes 147464 | tf_op jit(solution)/shard_map/ppermute | solution.py:56

commit v5 on v4

--- a/solution.py
+++ b/solution.py
@@ -116,7 +116,7 @@
     n_il, n_xl, _ = seismic_ref.shape
     eye = iota((n_xl, n_xl), 0) == iota((n_xl, n_xl), 1)
     for p in range(n_il):
-        row = jnp.broadcast_to(trace_ref[p : p + 1, :].astype(F32), (n_xl, n_xl))
+        row = jnp.broadcast_to(trace_ref[p : p + 1, :], (n_xl, n_xl))
         kept = dot(jnp.where(eye, row, 0.0).astype(BF16), seismic_ref[p])
         live_ref[p * n_xl : (p + 1) * n_xl, :] = kept.astype(BF16)
     count = REACH * n_xl
@@ -188,13 +188,8 @@
 
     a0 = bands[0:256, 0:32]
     a12 = bands[256:768, 0:32]
-    for j in (0, 1, 34):
-        first0[j] = jnp.zeros((256, 256), F32)
-    for j in (0, 1, 2, 3, 20, 21, 22, 23):
-        first12[j] = jnp.zeros((512, 128), F32)
-
     def level0_first(j, _):
-        first0[j + 2] = rounded(dot(a0, planes[j]))
+        first0[j] = rounded(dot(a0, planes[j]))
         return 0
 
     lax.fori_loop(0, 32, level0_first, 0, unroll=8)
@@ -202,8 +197,8 @@
     def even_first(pair, _):
         both = jnp.concatenate([planes[4 * pair, :, 0:128], planes[4 * pair + 2, :, 0:128]], axis=1)
         out = rounded(dot(a12, both))
-        first12[2 * pair + 4] = out[:, 0:128]
-        first12[2 * pair + 5] = out[:, 128:256]
+        first12[2 * pair] = out[:, 0:128]
+        first12[2 * pair + 1] = out[:, 128:256]
         return 0
 
     lax.fori_loop(0, 8, even_first, 0, unroll=4)
@@ -214,7 +209,7 @@
 
 
 def crossline_kernel(
-    two_sided, bands, w2, first12, xh_ref, extra0, second12, edges, extra1, extra2
+    two_sided, bands, w2, first12, xh_ref, edge0, second12, edges, edge12
 ):
     x_left = side_flags()[0]
 
@@ -228,55 +223,46 @@
     edges[...] = dot(turn_x, got.astype(BF16)).astype(BF16).reshape(16, 32, 256)
     a0 = bands[0:256, 0:32]
     a12 = bands[256:768, 0:32]
-    out0 = {j: rounded(dot(a0, edges[slot])) for j, slot in ((-2, 6), (-1, 7), (32, 8))}
-    out12 = {}
-    for slot in (0, 4, 8, 12):
-        both = jnp.concatenate([edges[slot, :, 0:128], edges[slot + 2, :, 0:128]], axis=1)
+    for i, slot in enumerate((6, 7, 8)):
+        edge0[i] = rounded(dot(a0, edges[slot]))
+    for i in range(4):
+        both = jnp.concatenate([edges[4 * i, :, 0:128], edges[4 * i + 2, :, 0:128]], axis=1)
         out = rounded(dot(a12, both))
-        e = slot // 2 - 4 if slot < 8 else slot // 2 + 12
-        out12[e], out12[e + 1] = out[:, 0:128], out[:, 128:256]
-
-    extra0[0] = jnp.zeros((256, 256), F32)
-    for slot, q in ((1, 0), (2, 15)):
-        total = jnp.zeros((256, 256), F32)
-        for k in range(TAPS):
-            if 2 * q + k - 2 in out0:
-                total = total + jnp.concatenate([tall(w2, 0, k)] * 2, axis=1) * out0[2 * q + k - 2]
-        extra0[slot] = total
-    for level, extra in ((1, extra1), (2, extra2)):
+        edge12[2 * i], edge12[2 * i + 1] = out[:, 0:128], out[:, 128:256]
+
+    def filtered(level, q, plane):
+        for c16 in range(2):
+            start = level * ORIENT + c16 * 16
+            s2 = [w2[k, start : start + 16] for k in range(TAPS)]
+            for o in range(8):
+                row = (level - 1) * 256 + o * ORIENT + c16 * 16
+                here = slice(row, row + 16)
+                total = sum(s2[k] * plane(q + level * (k - 2), here) for k in range(TAPS))
+                second12[q, here, :] = total.astype(BF16)
+
+    def own_plane(e, here):
+        return first12[e, here, :]
+
+    def any_plane(e, here):
+        if 0 <= e < 16:
+            return first12[e, here, :]
+        return edge12[e + 4 if e < 0 else e - 12, here, :]
+
+    for level in (1, 2):
         reach = 2 * level
-        extra[0] = jnp.zeros((256, 128), F32)
-        for slot in range(2 * reach):
-            q = slot if slot < reach else 16 - 2 * reach + slot
-            total = jnp.zeros((256, 128), F32)
-            for k in range(TAPS):
-                e = q + level * (k - 2)
-                if e in out12:
-                    total = total + tall(w2, level, k) * out12[e][(level - 1) * 256 : level * 256]
-            extra[slot + 1] = total
-
-    def one_q(q, _):
-        for level in (1, 2):
-            extra = extra1 if level == 1 else extra2
-            reach = 2 * level
-            slot = jnp.where(q < reach, q + 1, jnp.where(q >= 16 - reach, q + 2 * reach - 15, 0))
-            for c16 in range(2):
-                start = level * ORIENT + c16 * 16
-                s2 = [w2[k, start : start + 16] for k in range(TAPS)]
-                for o in range(8):
-                    row = o * ORIENT + c16 * 16
-                    here = slice((level - 1) * 256 + row, (level - 1) * 256 + row + 16)
-                    total = extra[slot, row : row + 16, :]
-                    for k in range(TAPS):
-                        total = total + s2[k] * first12[q + 4 + level * (k - 2), here, :]
-                    second12[q, here, :] = total.astype(BF16)
-        return 0
-
-    lax.fori_loop(0, 16, one_q, 0)
+
+        def inner(q, _, level=level):
+            filtered(level, q, own_plane)
+            return 0
+
+        lax.fori_loop(reach, 16 - reach, inner, 0)
+        for i in range(reach):
+            filtered(level, i, any_plane)
+            filtered(level, 15 - i, any_plane)
 
 
 def attributes_kernel(
-    two_sided, live_smem, live_ref, bands, w2, w3, first0, extra0, second12, dh_ref,
+    two_sided, live_smem, live_ref, bands, w2, w3, first0, edge0, second12, dh_ref,
     attr_ref, gram_ref, halo2, moves1, moves2,
 ):
     x_left, depth_first, _ = side_flags()
@@ -308,13 +294,14 @@
     moves1[...] = shift_matrix((-2, -1, 1, 2))
     moves2[...] = shift_matrix((-4, -2, 2, 4))
 
-    def one_q(q):
-        align = jnp.where(q == 0, 0, 128 - 8 * q)
+    def one_q(q, plane):
+        align = (128 - 8 * q) % 128
         live_q = [live_smem[2 * o, 2 * q].astype(F32) for o in range(8)]
         lane = iota((16, 128), 1)
 
         def put(o, start, total):
-            attr_ref[o * 16 + q, start : start + 16, :] = (total * live_q[o]).astype(BF16)
+            at = start % ORIENT
+            attr_ref[2 * o + q // 8, start // ORIENT, q % 8, at : at + 16, :] = (total * live_q[o]).astype(BF16)
 
         for level in (1, 2):
             halo = pltpu.roll(halo2[level], align, 1).astype(BF16)
@@ -329,7 +316,6 @@
                     for i, k in enumerate((0, 1, 3, 4)):
                         total = total + s3[k] * moved[rows, i * 128 : i * 128 + 128]
                     put(o, start, total)
-        slot = jnp.where(q == 0, 1, jnp.where(q == 15, 2, 0))
         for c16 in range(2):
             s2 = [w2[k, c16 * 16 : c16 * 16 + 16] for k in range(TAPS)]
             s3 = [w3[k, c16 * 16 : c16 * 16 + 16] for k in range(TAPS)]
@@ -337,9 +323,7 @@
                 rows = slice(o * ORIENT + c16 * 16, o * ORIENT + c16 * 16 + 16)
                 both = []
                 for ts in (slice(0, 128), slice(128, 256)):
-                    total = extra0[slot, rows, ts]
-                    for k in range(TAPS):
-                        total = total + s2[k] * first0[2 * q + k, rows, ts]
+                    total = sum(s2[k] * plane(2 * q + k - 2, rows, ts) for k in range(TAPS))
                     both.append(rounded(total))
                 even, odd = both
                 halo = pltpu.roll(halo2[0, rows], align, 1)
@@ -350,19 +334,35 @@
 
     def add_gram(q, total):
         for o in range(0, 8, 2):
-            both = jnp.concatenate([attr_ref[o * 16 + q], attr_ref[o * 16 + 16 + q]], axis=1)
+            both = jnp.concatenate(
+                [
+                    jnp.concatenate([attr_ref[2 * i + q // 8, level, q % 8] for level in range(3)], axis=0)
+                    for i in (o, o + 1)
+                ],
+                axis=1,
+            )
             total = total + lax.dot_general(
                 both, both, (((1,), (1,)), ((), ())), preferred_element_type=F32
             )
         return total
 
+    def own_plane(j, rows, ts):
+        return first0[j, rows, ts]
+
+    def any_plane(j, rows, ts):
+        if 0 <= j < 32:
+            return first0[j, rows, ts]
+        return edge0[j + 2 if j < 0 else 2, rows, ts]
+
     def next_q(q, total):
         total = add_gram(q - 1, total)
-        one_q(q)
+        one_q(q, own_plane)
         return total
 
-    one_q(0)
-    gram = lax.fori_loop(1, 16, next_q, jnp.zeros((CHAN, CHAN), F32))
+    one_q(0, any_plane)
+    gram = lax.fori_loop(1, 15, next_q, jnp.zeros((CHAN, CHAN), F32))
+    gram = add_gram(14, gram)
+    one_q(15, any_plane)
     gram = add_gram(15, gram)
     alive = live_ref[...]
     chosen = (iota(alive.shape, 0) % 2 == 0) & (iota(alive.shape, 1) % 2 == 0)
@@ -371,101 +371,120 @@
     gram_ref[:, 0:CHAN] = gram
 
 
-def whiten_kernel(mine_ref, other_ref, attr_ref, out_ref, factor_ref, inverse, kron):
-    step = pl.program_id(0)
-
-    @pl.when(step == 0)
-    def _():
-        total = mine_ref[...] + other_ref[...]
-        lane = iota((8, 128), 1)
-        sub = iota((8, 128), 0)
-        count = jnp.broadcast_to(total[0:1, CHAN : CHAN + 1], (8, 128))
-        blocks = []
-        for g in range(CHAN // 8):
-            blocks.append(jnp.where(lane < CHAN, total[8 * g : 8 * g + 8] / count, 0.0))
-        row_lane = iota((1, 128), 1)
-
-        def finish(j, row, inv_row, pivot):
-            scale = lax.rsqrt(pivot)
-            factor_ref[j : j + 1, :] = (jnp.where(row_lane >= j, row, 0.0) * scale)[:, 0:CHAN]
-            inverse[j : j + 1, :] = jnp.where(row_lane <= j, inv_row, 0.0) * scale
-
-        def spread_lane(block, j):
-            return jnp.broadcast_to(block[:, j : j + 1], (8, 128))
-
-        def spread_row(block, i):
-            return jnp.broadcast_to(block[i : i + 1, :], (8, 128))
-
-        for j in range(0, CHAN, 4):
-            g, s = j // 8, j % 8
-            top = blocks[g]
-            cols = [spread_lane(top, j + i) for i in range(4)]
-            rows = [spread_row(top, s + i) for i in range(4)]
-            d = [[spread_row(cols[min(m, i)], s + max(m, i)) for i in range(4)] for m in range(4)]
-            p_inv = 1.0 / (d[0][0] * d[1][1] - d[0][1] * d[0][1])
-            adj = [[d[1][1], -d[0][1]], [-d[0][1], d[0][0]]]
-            h = [
-                [(d[2 + m][0] * adj[0][i] + d[2 + m][1] * adj[1][i]) * p_inv for i in range(2)]
-                for m in range(2)
+def whiten_kernel(mine_ref, other_ref, attr_ref, out_hbm, factor_ref, inverse, kron, out_ref, sems):
+    total = mine_ref[...] + other_ref[...]
+    lane = iota((8, 128), 1)
+    sub = iota((8, 128), 0)
+    count = jnp.broadcast_to(total[0:1, CHAN : CHAN + 1], (8, 128))
+    blocks = []
+    for g in range(CHAN // 8):
+        blocks.append(jnp.where(lane < CHAN, total[8 * g : 8 * g + 8] / count, 0.0))
+
+    n = iota((CHAN, 768), 1)
+    spread = ones_where(iota((CHAN, 768), 0) == n // 256 * ORIENT + n % ORIENT)
+    tall = ones_where(iota((256, ORIENT), 0) // 8 == iota((256, ORIENT), 1))
+
+    def spread_inverse(level):
+        depth = 256 * (level + 1)
+        low = inverse[level * ORIENT : (level + 1) * ORIENT, 0:CHAN].astype(BF16)
+        full = dot(tall, dot(low, spread[:, 0:depth]).astype(BF16))
+        keep = iota((256, depth), 0) % 8 == iota((256, depth), 1) // ORIENT % 8
+        kron[level, :, 0:depth] = jnp.where(keep, full, 0.0).astype(BF16)
+
+    def sent(level):
+        cs = slice(level * ORIENT, (level + 1) * ORIENT)
+        return pltpu.make_async_copy(out_ref.at[cs], out_hbm.at[cs], sems.at[level])
+
+    def whiten_pair(level, pair):
+        depth = 256 * (level + 1)
+        halves = []
+        for half in range(2):
+            rows = [
+                attr_ref[2 * (2 * pair + i) + half, 0 : level + 1].reshape(depth, 128) for i in range(2)
             ]
-            t = [
-                [d[2 + m][2 + i] - (h[m][0] * d[0][2 + i] + h[m][1] * d[1][2 + i]) for i in range(2)]
-                for m in range(2)
-            ]
-            t01 = t[1][0]
-            t_inv = 1.0 / (t[0][0] * t[1][1] - t01 * t01)
-            unit = []
-            for i in range(4):
-                value = rows[i]
-                for m in range(4):
-                    value = jnp.where(lane == j + m, 1.0 if m == i else 0.0, value)
-                unit.append(value)
-            below = [unit[2 + m] - (h[m][0] * unit[0] + h[m][1] * unit[1]) for m in range(2)]
-            up2 = (t[1][1] * below[0] - t01 * below[1]) * t_inv
-            up3 = (t[0][0] * below[1] - t01 * below[0]) * t_inv
-            inner = [unit[0] * d[1][1] - unit[1] * d[0][1], unit[1] * d[0][0] - unit[0] * d[0][1]]
-            up0 = inner[0] * p_inv - (h[0][0] * up2 + h[1][0] * up3)
-            up1 = inner[1] * p_inv - (h[0][1] * up2 + h[1][1] * up3)
-            ups = (up0, up1, up2, up3)
-            ratio0 = d[0][1] / d[0][0]
-            ratio1 = t01 / t[0][0]
-            mix0 = rows[2] - (h[0][0] * rows[0] + h[0][1] * rows[1])
-            mix1 = rows[3] - (h[1][0] * rows[0] + h[1][1] * rows[1])
-            solved = [rows[0], rows[1] - ratio0 * rows[0], mix0, mix1 - ratio1 * mix0]
-            inv_solved = [unit[0], unit[1] - ratio0 * unit[0], below[0], below[1] - ratio1 * below[0]]
-            pivots = [d[0][0], d[1][1] - d[0][1] * ratio0, t[0][0], t[1][1] - t01 * ratio1]
-            for i in range(4):
-                finish(j + i, solved[i][0:1], inv_solved[i][0:1], pivots[i][0:1])
-            if j == CHAN - 4:
-                break
-            inside = (lane >= j) & (lane < j + 4)
-            for k in range(g, CHAN // 8):
-                if k > g:
-                    cols = [spread_lane(blocks[k], j + i) for i in range(4)]
-                else:
-                    if s == 4:
-                        continue
-                    cols = [jnp.where(sub > s + 3, col, 0.0) for col in cols]
-                change = (cols[0] * ups[0] + cols[1] * ups[1]) + (cols[2] * ups[2] + cols[3] * ups[3])
-                blocks[k] = jnp.where(inside, 0.0, blocks[k]) - change
-        low = inverse[:, 0:CHAN].astype(BF16)
-        spread = ones_where(iota((CHAN, 768), 0) == iota((CHAN, 768), 1) % CHAN)
-        wide = dot(low, spread).astype(BF16)
-        tall = ones_where(iota((768, CHAN), 0) // 8 == iota((768, CHAN), 1))
-        full = dot(tall, wide)
-        keep = iota((768, 768), 0) % 8 == iota((768, 768), 1) // CHAN
-        kron[...] = jnp.where(keep, full, 0.0).astype(BF16)
-
-    weights = kron[...]
-    halves = []
-    for half in range(2):
-        pair = [
-            attr_ref[pl.ds((2 * step + i) * 16 + 8 * half, 8)].reshape(768, 128) for i in range(2)
+            halves.append(dot(kron[level, :, 0:depth], jnp.concatenate(rows, axis=1)))
+        for i in range(2):
+            both = [half[:, i * 128 : i * 128 + 128].reshape(ORIENT, 8, 128) for half in halves]
+            out_ref[level * ORIENT : (level + 1) * ORIENT, 2 * pair + i] = jnp.concatenate(
+                both, axis=1
+            ).astype(BF16)
+        if pair == 3:
+            sent(level).start()
+
+    row_lane = iota((1, 128), 1)
+
+    def finish(j, row, inv_row, pivot):
+        scale = lax.rsqrt(pivot)
+        factor_ref[j : j + 1, :] = (jnp.where(row_lane >= j, row, 0.0) * scale)[:, 0:CHAN]
+        inverse[j : j + 1, :] = jnp.where(row_lane <= j, inv_row, 0.0) * scale
+
+    def spread_lane(block, j):
+        return jnp.broadcast_to(block[:, j : j + 1], (8, 128))
+
+    def spread_row(block, i):
+        return jnp.broadcast_to(block[i : i + 1, :], (8, 128))
+
+    for j in range(0, CHAN, 4):
+        g, s = j // 8, j % 8
+        top = blocks[g]
+        cols = [spread_lane(top, j + i) for i in range(4)]
+        rows = [spread_row(top, s + i) for i in range(4)]
+        d = [[spread_row(cols[min(m, i)], s + max(m, i)) for i in range(4)] for m in range(4)]
+        p_inv = 1.0 / (d[0][0] * d[1][1] - d[0][1] * d[0][1])
+        adj = [[d[1][1], -d[0][1]], [-d[0][1], d[0][0]]]
+        h = [
+            [(d[2 + m][0] * adj[0][i] + d[2 + m][1] * adj[1][i]) * p_inv for i in range(2)]
+            for m in range(2)
         ]
-        halves.append(dot(weights, jnp.concatenate(pair, axis=1)))
-    for i in range(2):
-        both = [half[:, i * 128 : i * 128 + 128].reshape(CHAN, 8, 128) for half in halves]
-        out_ref[:, i] = jnp.concatenate(both, axis=1).astype(BF16)
+        t = [
+            [d[2 + m][2 + i] - (h[m][0] * d[0][2 + i] + h[m][1] * d[1][2 + i]) for i in range(2)]
+            for m in range(2)
+        ]
+        t01 = t[1][0]
+        t_inv = 1.0 / (t[0][0] * t[1][1] - t01 * t01)
+        unit = []
+        for i in range(4):
+            value = rows[i]
+            for m in range(4):
+                value = jnp.where(lane == j + m, 1.0 if m == i else 0.0, value)
+            unit.append(value)
+        below = [unit[2 + m] - (h[m][0] * unit[0] + h[m][1] * unit[1]) for m in range(2)]
+        up2 = (t[1][1] * below[0] - t01 * below[1]) * t_inv
+        up3 = (t[0][0] * below[1] - t01 * below[0]) * t_inv
+        inner = [unit[0] * d[1][1] - unit[1] * d[0][1], unit[1] * d[0][0] - unit[0] * d[0][1]]
+        up0 = inner[0] * p_inv - (h[0][0] * up2 + h[1][0] * up3)
+        up1 = inner[1] * p_inv - (h[0][1] * up2 + h[1][1] * up3)
+        ups = (up0, up1, up2, up3)
+        ratio0 = d[0][1] / d[0][0]
+        ratio1 = t01 / t[0][0]
+        mix0 = rows[2] - (h[0][0] * rows[0] + h[0][1] * rows[1])
+        mix1 = rows[3] - (h[1][0] * rows[0] + h[1][1] * rows[1])
+        solved = [rows[0], rows[1] - ratio0 * rows[0], mix0, mix1 - ratio1 * mix0]
+        inv_solved = [unit[0], unit[1] - ratio0 * unit[0], below[0], below[1] - ratio1 * below[0]]
+        pivots = [d[0][0], d[1][1] - d[0][1] * ratio0, t[0][0], t[1][1] - t01 * ratio1]
+        for i in range(4):
+            finish(j + i, solved[i][0:1], inv_solved[i][0:1], pivots[i][0:1])
+        if j % ORIENT == ORIENT - 4:
+            spread_inverse(j // ORIENT)
+        if j >= ORIENT and j % 8 == 4:
+            whiten_pair(j // ORIENT - 1, j % ORIENT // 8)
+        if j == CHAN - 4:
+            break
+        inside = (lane >= j) & (lane < j + 4)
+        for k in range(g, CHAN // 8):
+            if k > g:
+                cols = [spread_lane(blocks[k], j + i) for i in range(4)]
+            else:
+                if s == 4:
+                    continue
+                cols = [jnp.where(sub > s + 3, col, 0.0) for col in cols]
+            change = (cols[0] * ups[0] + cols[1] * ups[1]) + (cols[2] * ups[2] + cols[3] * ups[3])
+            blocks[k] = jnp.where(inside, 0.0, blocks[k]) - change
+
+    for pair in range(4):
+        whiten_pair(2, pair)
+    for level in range(3):
+        sent(level).wait()
 
 
 def local(seismic, trace_live, filter_taps):
@@ -489,7 +508,7 @@
         out_specs=(vmem,) * 3,
         compiler_params=pltpu.CompilerParams(vmem_limit_bytes=LIVE_VMEM),
         name="live",
-    )(trace_live, seismic)
+    )(trace_live.astype(F32), seismic)
     il_size = lax.axis_size("inline")
     near_pairs = [(i, i ^ 1) for i in range(il_size) if i ^ 1 < il_size]
     far_pairs = [(i, i - 1 if i % 2 == 0 else i + 1) for i in range(1, il_size)]
@@ -512,8 +531,8 @@
             jax.ShapeDtypeStruct((3 * 256, 128), BF16),
             jax.ShapeDtypeStruct((TAPS, CHAN, 128), F32),
             jax.ShapeDtypeStruct((TAPS, CHAN, 128), F32),
-            jax.ShapeDtypeStruct((35, 256, 256), F32),
-            jax.ShapeDtypeStruct((24, 512, 128), F32),
+            jax.ShapeDtypeStruct((xl_len, 256, 256), F32),
+            jax.ShapeDtypeStruct((xl_len // 2, 512, 128), F32),
             jax.ShapeDtypeStruct((32 * xl_len, 128), BF16),
         ),
         in_specs=[vmem] * 4,
@@ -530,7 +549,7 @@
     dh = jnp.concatenate([edge.reshape(32, xl_len, 128)] + [side(x) for x in xh], axis=1)
     dh = flipped(dh, [("depth", 1)])
     xrows = jnp.concatenate([x.reshape(256, t_len) for x in xh], axis=0)
-    extra0, second12 = pl.pallas_call(
+    edge0, second12 = pl.pallas_call(
         functools.partial(crossline_kernel, two_sided),
         out_shape=(
             jax.ShapeDtypeStruct((3, 256, 256), F32),
@@ -540,8 +559,7 @@
         out_specs=(vmem,) * 2,
         scratch_shapes=[
             pltpu.VMEM((16, 32, 256), BF16),
-            pltpu.VMEM((5, 256, 128), F32),
-            pltpu.VMEM((9, 256, 128), F32),
+            pltpu.VMEM((8, 512, 128), F32),
         ],
         compiler_params=pltpu.CompilerParams(vmem_limit_bytes=CROSS_VMEM),
         cost_estimate=pl.CostEstimate(flops=3 * 10**9, bytes_accessed=9 * 10**6, transcendentals=0),
@@ -550,7 +568,7 @@
     attr, gram = pl.pallas_call(
         functools.partial(attributes_kernel, two_sided),
         out_shape=(
-            jax.ShapeDtypeStruct((128, CHAN, 128), BF16),
+            jax.ShapeDtypeStruct((16, 3, 8, ORIENT, 128), BF16),
             jax.ShapeDtypeStruct((CHAN, 128), F32),
         ),
         in_specs=[smem] + [vmem] * 8,
@@ -562,22 +580,23 @@
         ],
         compiler_params=pltpu.CompilerParams(vmem_limit_bytes=ATTR_VMEM),
         name="attributes",
-    )(trace_live, trace_live, bands, w2, w3, first0, extra0, second12, dh)
+    )(trace_live, trace_live, bands, w2, w3, first0, edge0, second12, dh)
 
     mine, other = summed(gram)
     out, factor = pl.pallas_call(
         whiten_kernel,
-        grid=(4,),
         out_shape=(
             jax.ShapeDtypeStruct((CHAN, 8, 16, 128), BF16),
             jax.ShapeDtypeStruct((CHAN, CHAN), F32),
         ),
         in_specs=[vmem] * 3,
-        out_specs=(
-            pl.BlockSpec((CHAN, 2, 16, 128), lambda i: (0, i, 0, 0)),
-            pl.BlockSpec((CHAN, CHAN), lambda i: (0, 0)),
-        ),
-        scratch_shapes=[pltpu.VMEM((CHAN, 128), F32), pltpu.VMEM((768, 768), BF16)],
+        out_specs=(pl.BlockSpec(memory_space=pl.ANY), vmem),
+        scratch_shapes=[
+            pltpu.VMEM((CHAN, 128), F32),
+            pltpu.VMEM((3, 256, 768), BF16),
+            pltpu.VMEM((CHAN, 8, 16, 128), BF16),
+            pltpu.SemaphoreType.DMA((3,)),
+        ],
         compiler_params=pltpu.CompilerParams(vmem_limit_bytes=WHITEN_VMEM),
         name="whiten",
     )(mine, other, attr)

time: 53.8 us -> 52.1 us (0.968)
  Pallas kernels: 24.8 us -> 23 us
  other arithmetic: 0.1 us -> 0.8 us
  local copies, waits for them, and re-layouts: 2.49 us -> 1.8 us
    pallas_call x1, Pallas kernels: 9.06 us -> 7.49 us  [local(): pl.pallas_call(whiten_kernel, out_shape=(jax.ShapeDtypeStruct((CHAN, 8, 1...]
    convert_element_type x0 -> x1, other arithmetic: none -> 0.7 us  [local(): trace_live.astype(F32)]
    unnamed x6 -> x4, local copies, waits for them, and re-layouts: 1.65 us -> 0.96 us
  transfers between devices with their start and end apart: 9 -> 9, of which waited for: 6 -> 6; matrix products, arithmetic and copies ran while one was open for 2% -> 2% of each run, Pallas kernels for 12% -> 11%
where the time goes in v5:
time: 52.1 us; the launch traced here: 51.8 us
  Pallas kernels  23 us (44%)
  starting transfers between devices  13.7 us (26%)
  waiting for transfers between devices  11.8 us (23%)
  local copies, waits for them, and re-layouts  1.8 us (3%)
  other arithmetic  0.8 us (2%)
  between operations  0.76 us (1%)
    ppermute x7, starting transfers between devices, flipped(): return lax.ppermute(value, axes, pairs)  9.94 us
    ppermute x7, waiting for transfers between devices, flipped(): return lax.ppermute(value, axes, pairs)  9.83 us
    pallas_call x1, Pallas kernels, local(): pl.pallas_call(functools.partial(attributes_kernel, two_sided), out_shape...  9.34 us
    pallas_call x1, Pallas kernels, local(): pl.pallas_call(whiten_kernel, out_shape=(jax.ShapeDtypeStruct((CHAN, 8, 1...  7.49 us
    pallas_call x1, Pallas kernels, local(): pl.pallas_call(inline_kernel, out_shape=(jax.ShapeDtypeStruct((3 * 256, 1...  3.27 us
    ppermute x1, starting transfers between devices, local(): near = lax.ppermute(near, 'inline', near_pairs)  3.08 us
    pallas_call x1, Pallas kernels, local(): pl.pallas_call(functools.partial(crossline_kernel, two_sided), out_shape=...  2.67 us
    ppermute x1, waiting for transfers between devices, local(): near = lax.ppermute(near, 'inline', near_pairs)  1.97 us
  transfers between devices with their start and end apart: 9, of which 6 were waited for; matrix products, arithmetic and copies ran while one was open for 2% of the time, Pallas kernels for 11%

profile of v5, /device:TPU:0, one launch (start us, length us, event | category | flops | bytes accessed | tf_op | source)
XLA Modules:
  0.0 51.8 jit_solution(10460740680007407473)
XLA Ops:
  0.6 0.7 %convert_element_type.7.trace_ref = f32[16,32]{1,0:T(8,128)S(1)} convert(s32[16,32]{1,0:T(8,128)} %live_ref.1) | non-fusion elementwise | flops 512 | bytes 4096 | tf_op jit(solution)/shard_map/convert_element_type | solution.py:511
  1.3 0.0 copy-start
  1.3 0.9 %copy-done = bf16[16,32,256]{2,1,0:T(8,128)(2,1)S(1)} copy-done((bf16[16,32,256]{2,1,0:T(8,128)(2,1)S(1)}, bf16[16,32,256]{2,1,0:T(8,128)(2,1)}, u32[]{:S(2)}) %copy-start) | copy-done | bytes 262168
  2.3 0.2 live.1
  2.5 3.1 %collective-permute-start = (bf16[256,256]{1,0:T(8,128)(2,1)S(1)}, bf16[256,256]{1,0:T(8,128)(2,1)S(1)}, u32[]{:S(2)}, u32[]{:S(2)}) collective-permute-start(bf16[256,256]{1,0:T(8,128)(2,1)S(1)} %get-tuple-element.16), channel_id=1, source_target_pairs={{0,4},{4,0},{8,12},{12,8},{1,5},{5,1},{9,13},{13,9},{2,6},{6,2},{1... | collective-permute-start | bytes 393224 | tf_op jit(solution)/shard_map/ppermute | solution.py:516
  5.6 0.7 %collective-permute-start.1 = (bf16[256,256]{1,0:T(8,128)(2,1)S(1)}, bf16[256,256]{1,0:T(8,128)(2,1)S(1)}, u32[]{:S(2)}, u32[]{:S(2)}) collective-permute-start(bf16[256,256]{1,0:T(8,128)(2,1)S(1)} %get-tuple-element.17), channel_id=1, source_target_pairs={{4,8},{8,4},{5,9},{9,5},{6,10},{10,6},{7,11},{11,7},{20,24},{24,20... | collective-permute-start | bytes 393224 | tf_op jit(solution)/shard_map/ppermute | solution.py:517
  6.3 0.8 %copy.6.taps_ref = f32[3,96,5]{2,1,0:T(8,128)S(1)} copy(bf16[3,96,5]{1,0,2:T(4,128)(2,1)} %param.5) | data formatting | bytes 8640 | tf_op jit(solution)/shard_map/convert_element_type | solution.py:493
  7.1 2.0 %collective-permute-done.near_ref = bf16[256,256]{1,0:T(8,128)(2,1)S(1)} collective-permute-done((bf16[256,256]{1,0:T(8,128)(2,1)S(1)}, bf16[256,256]{1,0:T(8,128)(2,1)S(1)}, u32[]{:S(2)}, u32[]{:S(2)}) %collective-permute-start) | collective-permute-done | bytes 131104 | tf_op jit(solution)/shard_map/ppermute | solution.py:516
  9.1 0.0 collective-permute-done.1.far_ref
  9.2 1.7 %collective-permute-start.2 = (bf16[32,8,256]{2,1,0:T(8,128)(2,1)S(1)}, bf16[32,8,256]{2,1,0:T(8,128)(2,1)S(1)}, u32[]{:S(2)}, u32[]{:S(2)}) collective-permute-start(bf16[32,8,256]{2,1,0:T(8,128)(2,1)S(1)} %maximum_select_fusion), channel_id=1, source_target_pairs={{0,2},{2,0},{1,3},{3,1},{4,6},{6,4},{5,7},{7,5},{8,10},{10,8},{9,1... | collective-permute-start | bytes 393224 | tf_op jit(solution)/shard_map/ppermute | solution.py:56
  10.9 3.3 %inline.1 = (bf16[768,128]{1,0:T(8,128)(2,1)S(1)}, f32[5,96,128]{2,1,0:T(8,128)S(1)}, f32[5,96,128]{2,1,0:T(8,128)S(1)}, f32[32,256,256]{2,1,0:T(8,128)S(1)}, f3...) custom-call(f32[3,96,5]{2,1,0:T(8,128)S(1)} %copy.6.taps_ref, bf16[512,256]{1,0:T(8,128)(2,1)S(1)} %get-tuple-element.15.own_ref, ...), custom_call_target="tpu_custom_call" | custom-call | flops 4000000000 | bytes 16000000 | tf_op jit(solution)/shard_map/inline/pallas_call | solution.py:528
  14.2 0.0 collective-permute-done.2
  14.2 0.1 collective-permute-start.3
  14.3 0.0 copy-start.1
  14.3 2.7 %crossline.1 = (f32[3,256,256]{2,1,0:T(8,128)S(1)}, bf16[16,512,128]{2,1,0:T(8,128)(2,1)S(1)}) custom-call(bf16[768,128]{1,0:T(8,128)(2,1)S(1)} %get-tuple-element.18.bands, f32[5,96,128]{2,1,0:T(8,128)S(1)} %get-tuple-element.19.w2, f32[16,512,128]{2,1,0:T(8,128)S(1)} %get-tuple-element.22.first12, bf16[256,256]{1,0:T(8,128)(2,1)S(1)} %bitcast.6), custom_call_target="tpu_custom_call" | custom-call | flops 3000000000 | bytes 9000000 | tf_op jit(solution)/shard_map/crossline/pallas_call | solution.py:552
  17.0 0.0 collective-permute-done.3.dh_ref
  17.0 0.0 copy-done.1
  17.0 9.3 %attributes.1 = (bf16[16,3,8,32,128]{4,3,2,1,0:T(8,128)(2,1)S(1)}, f32[96,128]{1,0:T(8,128)S(1)}) custom-call(s32[16,32]{1,0:T(8,128)S(1)} %copy-done.1, s32[16,32]{1,0:T(8,128)S(1)} %copy-done.1, bf16[768,128]{1,0:T(8,128)(2,1)S(1)} %get-tuple-element.18.bands, f32[5,96,128]{2,1,0:T(8,128)S(1)} %get-tuple-element.19.w2, ...), custom_call_target="tpu_custom_call" | custom-call | tf_op jit(solution)/shard_map/attributes/pallas_call | solution.py:568
  26.4 0.5 %collective-permute-start.4 = (f32[96,128]{1,0:T(8,128)S(1)}, f32[96,128]{1,0:T(8,128)S(1)}, u32[]{:S(2)}, u32[]{:S(2)}) collective-permute-start(f32[96,128]{1,0:T(8,128)S(1)} %get-tuple-element.26), channel_id=1, source_target_pairs={{0,1},{1,0},{2,3},{3,2},{4,5},{5,4},{6,7},{7,6},{8,9},{9,8},{10,11... | collective-permute-start | bytes 147464 | tf_op jit(solution)/shard_map/ppermute | solution.py:56
  26.9 0.9 %collective-permute-done.4 = f32[96,128]{1,0:T(8,128)S(1)} collective-permute-done((f32[96,128]{1,0:T(8,128)S(1)}, f32[96,128]{1,0:T(8,128)S(1)}, u32[]{:S(2)}, u32[]{:S(2)}) %collective-permute-start.4) | collective-permute-done | bytes 49184 | tf_op jit(solution)/shard_map/ppermute | solution.py:56
  27.8 4.7 %collective-permute-start.5 = (f32[96,128]{1,0:T(8,128)S(1)}, f32[96,128]{1,0:T(8,128)S(1)}, u32[]{:S(2)}, u32[]{:S(2)}) collective-permute-start(f32[96,128]{1,0:T(8,128)S(1)} %add.12), channel_id=1, source_target_pairs={{0,4},{4,0},{8,12},{12,8},{1,5},{5,1},{9,13},{13,9},{2,6},{6,2},{1... | collective-permute-start | bytes 147464 | tf_op jit(solution)/shard_map/ppermute | solution.py:56
  32.5 1.5 %collective-permute-start.6 = (f32[96,128]{1,0:T(8,128)S(1)}, f32[96,128]{1,0:T(8,128)S(1)}, u32[]{:S(2)}, u32[]{:S(2)}) collective-permute-start(f32[96,128]{1,0:T(8,128)S(1)} %add.12), channel_id=1, source_target_pairs={{0,2},{2,0},{1,3},{3,1},{4,6},{6,4},{5,7},{7,5},{8,10},{10,8},{9,1... | collective-permute-start | bytes 147464 | tf_op jit(solution)/shard_map/ppermute | solution.py:56
  34.0 0.0 collective-permute-start.7
  34.1 0.8 %collective-permute-done.5 = f32[96,128]{1,0:T(8,128)S(1)} collective-permute-done((f32[96,128]{1,0:T(8,128)S(1)}, f32[96,128]{1,0:T(8,128)S(1)}, u32[]{:S(2)}, u32[]{:S(2)}) %collective-permute-start.5) | collective-permute-done | bytes 49184 | tf_op jit(solution)/shard_map/ppermute | solution.py:56
  34.9 1.8 %collective-permute-done.6 = f32[96,128]{1,0:T(8,128)S(1)} collective-permute-done((f32[96,128]{1,0:T(8,128)S(1)}, f32[96,128]{1,0:T(8,128)S(1)}, u32[]{:S(2)}, u32[]{:S(2)}) %collective-permute-start.6) | collective-permute-done | bytes 49184 | tf_op jit(solution)/shard_map/ppermute | solution.py:56
  36.6 2.4 %collective-permute-done.7 = f32[96,128]{1,0:T(8,128)S(1)} collective-permute-done((f32[96,128]{1,0:T(8,128)S(1)}, f32[96,128]{1,0:T(8,128)S(1)}, u32[]{:S(2)}, u32[]{:S(2)}) %collective-permute-start.7) | collective-permute-done | bytes 49184 | tf_op jit(solution)/shard_map/ppermute | solution.py:56
  39.0 1.3 %collective-permute-start.8 = (f32[96,128]{1,0:T(8,128)S(1)}, f32[96,128]{1,0:T(8,128)S(1)}, u32[]{:S(2)}, u32[]{:S(2)}) collective-permute-start(f32[96,128]{1,0:T(8,128)S(1)} %add_add_fusion.mine_ref), channel_id=1, source_target_pairs={{0,8},{4,12},{8,0},{12,4},{1,9},{5,13},{9,1},{13,5},{2,10},{6,14},... | collective-permute-start | bytes 147464 | tf_op jit(solution)/shard_map/ppermute | solution.py:56
  40.4 4.0 %collective-permute-done.8.other_ref = f32[96,128]{1,0:T(8,128)S(1)} collective-permute-done((f32[96,128]{1,0:T(8,128)S(1)}, f32[96,128]{1,0:T(8,128)S(1)}, u32[]{:S(2)}, u32[]{:S(2)}) %collective-permute-start.8) | collective-permute-done | bytes 49184 | tf_op jit(solution)/shard_map/ppermute | solution.py:56
  44.3 7.5 %whiten.1 = (bf16[96,8,16,128]{3,2,1,0:T(8,128)(2,1)}, f32[96,96]{1,0:T(8,128)}) custom-call(f32[96,128]{1,0:T(8,128)S(1)} %add_add_fusion.mine_ref, f32[96,128]{1,0:T(8,128)S(1)} %collective-permute-done.8.other_ref, bf16[16,3,8,32,128]{4,3,2,1,0:T(8,128)(2,1)S(1)} %get-tuple-element.27.attr_ref), custom_call_target="tpu_custom_call" | custom-call | tf_op jit(solution)/shard_map/whiten/pallas_call | solution.py:586
  (8 shorter events, 0.1 us)
Async XLA Ops:
  1.3 0.9 %copy-start = (bf16[16,32,256]{2,1,0:T(8,128)(2,1)S(1)}, bf16[16,32,256]{2,1,0:T(8,128)(2,1)}, u32[]{:S(2)}) copy-start(bf16[16,32,256]{2,1,0:T(8,128)(2,1)} %seismic_ref.1) | copy-start | bytes 786436
  2.5 6.6 %collective-permute-start = (bf16[256,256]{1,0:T(8,128)(2,1)S(1)}, bf16[256,256]{1,0:T(8,128)(2,1)S(1)}, u32[]{:S(2)}, u32[]{:S(2)}) collective-permute-start(bf16[256,256]{1,0:T(8,128)(2,1)S(1)} %get-tuple-element.16), channel_id=1, source_target_pairs={{0,4},{4,0},{8,12},{12,8},{1,5},{5,1},{9,13},{13,9},{2,6},{6,2},{1... | collective-permute-start | bytes 393224 | tf_op jit(solution)/shard_map/ppermute | solution.py:516
  5.6 3.5 %collective-permute-start.1 = (bf16[256,256]{1,0:T(8,128)(2,1)S(1)}, bf16[256,256]{1,0:T(8,128)(2,1)S(1)}, u32[]{:S(2)}, u32[]{:S(2)}) collective-permute-start(bf16[256,256]{1,0:T(8,128)(2,1)S(1)} %get-tuple-element.17), channel_id=1, source_target_pairs={{4,8},{8,4},{5,9},{9,5},{6,10},{10,6},{7,11},{11,7},{20,24},{24,20... | collective-permute-start | bytes 393224 | tf_op jit(solution)/shard_map/ppermute | solution.py:517
  9.2 5.0 %collective-permute-start.2 = (bf16[32,8,256]{2,1,0:T(8,128)(2,1)S(1)}, bf16[32,8,256]{2,1,0:T(8,128)(2,1)S(1)}, u32[]{:S(2)}, u32[]{:S(2)}) collective-permute-start(bf16[32,8,256]{2,1,0:T(8,128)(2,1)S(1)} %maximum_select_fusion), channel_id=1, source_target_pairs={{0,2},{2,0},{1,3},{3,1},{4,6},{6,4},{5,7},{7,5},{8,10},{10,8},{9,1... | collective-permute-start | bytes 393224 | tf_op jit(solution)/shard_map/ppermute | solution.py:56
  14.2 2.8 %collective-permute-start.3 = (bf16[32,40,128]{2,1,0:T(8,128)(2,1)S(1)}, bf16[32,40,128]{2,1,0:T(8,128)(2,1)S(1)}, u32[]{:S(2)}, u32[]{:S(2)}) collective-permute-start(bf16[32,40,128]{2,1,0:T(8,128)(2,1)S(1)} %pad_maximum_fusion), channel_id=1, source_target_pairs={{0,1},{1,0},{2,3},{3,2},{4,5},{5,4},{6,7},{7,6},{8,9},{9,8},{10,11... | collective-permute-start | bytes 983048 | tf_op jit(solution)/shard_map/ppermute | solution.py:56
  14.3 2.7 %copy-start.1 = (s32[16,32]{1,0:T(8,128)S(1)}, s32[16,32]{1,0:T(8,128)}, u32[]{:S(2)}) copy-start(s32[16,32]{1,0:T(8,128)} %live_ref.1) | copy-start | bytes 6148
  26.4 1.4 %collective-permute-start.4 = (f32[96,128]{1,0:T(8,128)S(1)}, f32[96,128]{1,0:T(8,128)S(1)}, u32[]{:S(2)}, u32[]{:S(2)}) collective-permute-start(f32[96,128]{1,0:T(8,128)S(1)} %get-tuple-element.26), channel_id=1, source_target_pairs={{0,1},{1,0},{2,3},{3,2},{4,5},{5,4},{6,7},{7,6},{8,9},{9,8},{10,11... | collective-permute-start | bytes 147464 | tf_op jit(solution)/shard_map/ppermute | solution.py:56
  27.8 7.1 %collective-permute-start.5 = (f32[96,128]{1,0:T(8,128)S(1)}, f32[96,128]{1,0:T(8,128)S(1)}, u32[]{:S(2)}, u32[]{:S(2)}) collective-permute-start(f32[96,128]{1,0:T(8,128)S(1)} %add.12), channel_id=1, source_target_pairs={{0,4},{4,0},{8,12},{12,8},{1,5},{5,1},{9,13},{13,9},{2,6},{6,2},{1... | collective-permute-start | bytes 147464 | tf_op jit(solution)/shard_map/ppermute | solution.py:56
  32.5 4.1 %collective-permute-start.6 = (f32[96,128]{1,0:T(8,128)S(1)}, f32[96,128]{1,0:T(8,128)S(1)}, u32[]{:S(2)}, u32[]{:S(2)}) collective-permute-start(f32[96,128]{1,0:T(8,128)S(1)} %add.12), channel_id=1, source_target_pairs={{0,2},{2,0},{1,3},{3,1},{4,6},{6,4},{5,7},{7,5},{8,10},{10,8},{9,1... | collective-permute-start | bytes 147464 | tf_op jit(solution)/shard_map/ppermute | solution.py:56
  34.0 5.0 %collective-permute-start.7 = (f32[96,128]{1,0:T(8,128)S(1)}, f32[96,128]{1,0:T(8,128)S(1)}, u32[]{:S(2)}, u32[]{:S(2)}) collective-permute-start(f32[96,128]{1,0:T(8,128)S(1)} %add.12), channel_id=1, source_target_pairs={{0,6},{2,4},{4,2},{6,0},{8,14},{10,12},{12,10},{14,8},{1,7},{3,5},... | collective-permute-start | bytes 147464 | tf_op jit(solution)/shard_map/ppermute | solution.py:56
  39.0 5.3 %collective-permute-start.8 = (f32[96,128]{1,0:T(8,128)S(1)}, f32[96,128]{1,0:T(8,128)S(1)}, u32[]{:S(2)}, u32[]{:S(2)}) collective-permute-start(f32[96,128]{1,0:T(8,128)S(1)} %add_add_fusion.mine_ref), channel_id=1, source_target_pairs={{0,8},{4,12},{8,0},{12,4},{1,9},{5,13},{9,1},{13,5},{2,10},{6,14},... | collective-permute-start | bytes 147464 | tf_op jit(solution)/shard_map/ppermute | solution.py:56

commit v6 on v5

--- a/solution.py
+++ b/solution.py
@@ -16,6 +16,7 @@
 F32 = jnp.float32
 BF16 = jnp.bfloat16
 LIVE_VMEM = 4 * 1024 * 1024
+PREPARE_VMEM = 8 * 1024 * 1024
 INLINE_VMEM = 22 * 1024 * 1024
 CROSS_VMEM = 16 * 1024 * 1024
 ATTR_VMEM = 22 * 1024 * 1024
@@ -157,34 +158,47 @@
     return ones_where(iota((256, 256), 0) == jnp.where(n < 128, 2 * n, 2 * n - 255))
 
 
-def inline_kernel(
-    taps_ref, own_ref, near_ref, far_ref, bands, w2, w3, first0, first12, edge_ref, planes
+def prepare_kernel(
+    stored, taps_ref, own_ref, bands, w2, w3, pick, turn, turn_x, own_out, moves1, moves2, select, gather
 ):
-    _, depth_first, il_odd = side_flags()
-
-    def put_edge(ts):
-        for at, ref in ((0, own_ref), (512, near_ref), (768, far_ref)):
-            edge_ref[at : at + ref.shape[0], :] = ref[:, ts]
-
-    pl.when(depth_first == 1)(lambda: put_edge(slice(128, 256)))
-    pl.when(depth_first == 0)(lambda: put_edge(slice(0, 128)))
+    x_left, depth_first, il_odd = side_flags()
     for k in range(TAPS):
         w2[k] = jnp.broadcast_to(taps_ref[1, :, k : k + 1], (CHAN, 128))
         w3[k] = jnp.broadcast_to(taps_ref[2, :, k : k + 1], (CHAN, 128))
     for level in range(3):
         banded(level, taps_ref, bands, il_odd)
-
-    pick = phase_pick()
+        select[level] = halo_select(level, stored, x_left, depth_first)
+    pick[...] = phase_pick()
+    own_out[...] = dot(own_ref[...], pick[...]).astype(BF16)
     r = iota((512, 512), 0)
     c = iota((512, 512), 1)
-    turn = ones_where((c // 16 == r % 32) & (c % 16 == r // 32))
-    own = dot(own_ref[...], pick).astype(BF16).reshape(16, 32, 256)
-    near = dot(near_ref[...], pick).astype(BF16).reshape(8, 32, 256)
-    far = dot(far_ref[...], pick).astype(BF16).reshape(8, 32, 256)
+    turn[...] = ones_where(c == r % 32 * 16 + r // 32)
+    turn_x[...] = ones_where(c == r // 256 * 256 + r % 32 * 8 + r // 32 % 8)
+    moves1[...] = shift_matrix((-2, -1, 1, 2))
+    moves2[...] = shift_matrix((-4, -2, 2, 4))
+    rows = 32 * stored
+    gather[...] = ones_where(iota((32, rows), 1) // stored == iota((32, rows), 0))
+
+
+def inline_kernel(
+    bands, pick, turn, own_ref, own_phases, near_ref, far_ref, first0, first12, edge_ref, planes
+):
+    depth_first = side_flags()[1]
+
+    def put_edge(ts):
+        for at, ref in ((0, own_ref), (512, near_ref), (768, far_ref)):
+            edge_ref[at : at + ref.shape[0], :] = ref[:, ts]
+
+    pl.when(depth_first == 1)(lambda: put_edge(slice(128, 256)))
+    pl.when(depth_first == 0)(lambda: put_edge(slice(0, 128)))
+
+    own = own_phases[...].reshape(16, 32, 256)
+    near = dot(near_ref[...], pick[...]).astype(BF16).reshape(8, 32, 256)
+    far = dot(far_ref[...], pick[...]).astype(BF16).reshape(8, 32, 256)
     for half in range(2):
         js = slice(half * 16, half * 16 + 16)
         block = jnp.concatenate([own[:, js], near[:, js], far[:, js]], axis=0).reshape(512, 256)
-        planes[half * 16 : half * 16 + 16] = dot(turn, block).astype(BF16).reshape(16, 32, 256)
+        planes[half * 16 : half * 16 + 16] = dot(turn[...], block).astype(BF16).reshape(16, 32, 256)
 
     a0 = bands[0:256, 0:32]
     a12 = bands[256:768, 0:32]
@@ -209,18 +223,15 @@
 
 
 def crossline_kernel(
-    two_sided, bands, w2, first12, xh_ref, edge0, second12, edges, edge12
+    two_sided, bands, w2, pick, turn_x, first12, xh_ref, edge0, second12, edges, edge12
 ):
     x_left = side_flags()[0]
 
-    r = iota((512, 512), 0)
-    c = iota((512, 512), 1)
-    turn_x = ones_where((c % 256 // 8 == r % 32) & (c // 256 * 8 + c % 8 == r // 32))
-    got = dot(xh_ref[...], phase_pick())
+    got = dot(xh_ref[...], pick[...])
     if not two_sided:
         left = jnp.where(x_left == 1, 1.0, 0.0)
         got = jnp.concatenate([got * left, got * (1.0 - left)], axis=0)
-    edges[...] = dot(turn_x, got.astype(BF16)).astype(BF16).reshape(16, 32, 256)
+    edges[...] = dot(turn_x[...], got.astype(BF16)).astype(BF16).reshape(16, 32, 256)
     a0 = bands[0:256, 0:32]
     a12 = bands[256:768, 0:32]
     for i, slot in enumerate((6, 7, 8)):
@@ -262,10 +273,10 @@
 
 
 def attributes_kernel(
-    two_sided, live_smem, live_ref, bands, w2, w3, first0, edge0, second12, dh_ref,
-    attr_ref, gram_ref, halo2, moves1, moves2,
+    two_sided, live_smem, live_ref, bands, w2, w3, moves1, moves2, select, gather, first0, edge0,
+    second12, dh_ref, attr_ref, gram_ref, halo2,
 ):
-    x_left, depth_first, _ = side_flags()
+    depth_first = side_flags()[1]
     stored = 48 if two_sided else 40
 
     n = iota((1, 256), 1)
@@ -276,10 +287,9 @@
     rows = 32 * stored
     wide = dot(dh_ref[...].reshape(rows, 128), spread)
     wide = jnp.where(iota((rows, 256), 0) % stored == n % stored, wide, 0.0).astype(BF16)
-    gather = ones_where(iota((32, rows), 1) // stored == iota((32, rows), 0))
-    lanes = dot(gather, wide).astype(BF16)
+    lanes = dot(gather[...], wide).astype(BF16)
     for level in range(3):
-        cols = dot(lanes, halo_select(level, stored, x_left, depth_first)).astype(BF16)
+        cols = dot(lanes, select[level]).astype(BF16)
         part = rounded(dot(bands[level * 256 : level * 256 + 256, 0:32], cols))
         total = jnp.zeros((256, 128), F32)
         for k in range(TAPS):
@@ -291,8 +301,6 @@
             total = jnp.where(iota((256, 128), 1) % 8 == 7, before_first, total * w3_4)
         halo2[level] = total
 
-    moves1[...] = shift_matrix((-2, -1, 1, 2))
-    moves2[...] = shift_matrix((-4, -2, 2, 4))
 
     def one_q(q, plane):
         align = (128 - 8 * q) % 128
@@ -516,6 +524,28 @@
     near = lax.ppermute(near, "inline", near_pairs)
     far = lax.ppermute(far, "inline", far_pairs)
     parts = [v.reshape(-1, xl_len, t_len) for v in (live, near, far)]
+    stored = 48 if two_sided else 40
+    bands, w2, w3, pick, turn, turn_x, own_phases, moves1, moves2, select, gather = pl.pallas_call(
+        functools.partial(prepare_kernel, stored),
+        out_shape=(
+            jax.ShapeDtypeStruct((3 * 256, 128), BF16),
+            jax.ShapeDtypeStruct((TAPS, CHAN, 128), F32),
+            jax.ShapeDtypeStruct((TAPS, CHAN, 128), F32),
+            jax.ShapeDtypeStruct((256, 256), BF16),
+            jax.ShapeDtypeStruct((512, 512), BF16),
+            jax.ShapeDtypeStruct((512, 512), BF16),
+            jax.ShapeDtypeStruct((512, 256), BF16),
+            jax.ShapeDtypeStruct((256, 512), BF16),
+            jax.ShapeDtypeStruct((256, 512), BF16),
+            jax.ShapeDtypeStruct((3, 256, TAPS * 128), BF16),
+            jax.ShapeDtypeStruct((32, 32 * stored), BF16),
+        ),
+        in_specs=[vmem] * 2,
+        out_specs=(vmem,) * 11,
+        compiler_params=pltpu.CompilerParams(vmem_limit_bytes=PREPARE_VMEM),
+        cost_estimate=pl.CostEstimate(flops=10**9, bytes_accessed=4 * 10**6, transcendentals=0),
+        name="prepare",
+    )(taps, live)
 
     def stack(js):
         return jnp.concatenate([v[:, js] for v in parts], axis=0)
@@ -525,23 +555,20 @@
         xh = [shifted(stack(high), "xline", 1), shifted(stack(low), "xline", -1)]
     else:
         xh = [flipped(jnp.where(x_index == 0, stack(high), stack(low)), [("xline", 1)])]
-    bands, w2, w3, first0, first12, edge = pl.pallas_call(
+    first0, first12, edge = pl.pallas_call(
         inline_kernel,
         out_shape=(
-            jax.ShapeDtypeStruct((3 * 256, 128), BF16),
-            jax.ShapeDtypeStruct((TAPS, CHAN, 128), F32),
-            jax.ShapeDtypeStruct((TAPS, CHAN, 128), F32),
             jax.ShapeDtypeStruct((xl_len, 256, 256), F32),
             jax.ShapeDtypeStruct((xl_len // 2, 512, 128), F32),
             jax.ShapeDtypeStruct((32 * xl_len, 128), BF16),
         ),
-        in_specs=[vmem] * 4,
-        out_specs=(vmem,) * 6,
+        in_specs=[vmem] * 7,
+        out_specs=(vmem,) * 3,
         scratch_shapes=[pltpu.VMEM((32, 32, 256), BF16)],
         compiler_params=pltpu.CompilerParams(vmem_limit_bytes=INLINE_VMEM),
         cost_estimate=pl.CostEstimate(flops=4 * 10**9, bytes_accessed=16 * 10**6, transcendentals=0),
         name="inline",
-    )(taps, live, near, far)
+    )(bands, pick, turn, live, own_phases, near, far)
 
     def side(x):
         return jnp.where(d_index == 0, x[:, :, t_len - 128 :], x[:, :, :128])
@@ -555,7 +582,7 @@
             jax.ShapeDtypeStruct((3, 256, 256), F32),
             jax.ShapeDtypeStruct((16, 512, 128), BF16),
         ),
-        in_specs=[vmem] * 4,
+        in_specs=[vmem] * 6,
         out_specs=(vmem,) * 2,
         scratch_shapes=[
             pltpu.VMEM((16, 32, 256), BF16),
@@ -564,23 +591,22 @@
         compiler_params=pltpu.CompilerParams(vmem_limit_bytes=CROSS_VMEM),
         cost_estimate=pl.CostEstimate(flops=3 * 10**9, bytes_accessed=9 * 10**6, transcendentals=0),
         name="crossline",
-    )(bands, w2, first12, xrows)
+    )(bands, w2, pick, turn_x, first12, xrows)
     attr, gram = pl.pallas_call(
         functools.partial(attributes_kernel, two_sided),
         out_shape=(
             jax.ShapeDtypeStruct((16, 3, 8, ORIENT, 128), BF16),
             jax.ShapeDtypeStruct((CHAN, 128), F32),
         ),
-        in_specs=[smem] + [vmem] * 8,
+        in_specs=[smem] + [vmem] * 12,
         out_specs=(vmem, vmem),
-        scratch_shapes=[
-            pltpu.VMEM((3, 256, 128), F32),
-            pltpu.VMEM((256, 512), BF16),
-            pltpu.VMEM((256, 512), BF16),
-        ],
+        scratch_shapes=[pltpu.VMEM((3, 256, 128), F32)],
         compiler_params=pltpu.CompilerParams(vmem_limit_bytes=ATTR_VMEM),
         name="attributes",
-    )(trace_live, trace_live, bands, w2, w3, first0, edge0, second12, dh)
+    )(
+        trace_live, trace_live, bands, w2, w3, moves1, moves2, select, gather, first0, edge0,
+        second12, dh,
+    )
 
     mine, other = summed(gram)
     out, factor = pl.pallas_call(

time: 52.1 us -> 50.8 us (0.975)
  waiting for transfers between devices: 11.8 us -> 8.58 us
  starting transfers between devices: 13.7 us -> 14.8 us
  Pallas kernels: 23 us -> 23.8 us
    ppermute x7, waiting for transfers between devices: 9.83 us -> 7.9 us  [flipped(): return lax.ppermute(value, axes, pairs)]
    ppermute x1, waiting for transfers between devices: 1.97 us -> 0.68 us  [local(): near = lax.ppermute(near, 'inline', near_pairs)]
    ppermute x7, starting transfers between devices: 9.94 us -> 11 us  [flipped(): return lax.ppermute(value, axes, pairs)]
    pallas_call x1 -> x2, Pallas kernels: 3.27 us -> 4.24 us  [the longest x1 2.98 us: local(): pl.pallas_call(inline_kernel, out_shape=(jax.ShapeDtypeStruct((xl_len, 25...]
  transfers between devices with their start and end apart: 9 -> 9, of which waited for: 6 -> 6; matrix products, arithmetic and copies ran while one was open for 2% -> 2% of each run, Pallas kernels for 11% -> 14%
where the time goes in v6:
time: 50.8 us; the launch traced here: 50.6 us
  Pallas kernels  23.8 us (47%)
  starting transfers between devices  14.8 us (29%)
  waiting for transfers between devices  8.58 us (17%)
  local copies, waits for them, and re-layouts  1.8 us (4%)
  other arithmetic  0.79 us (2%)
  between operations  0.77 us (2%)
    ppermute x7, starting transfers between devices, flipped(): return lax.ppermute(value, axes, pairs)  11 us
    pallas_call x1, Pallas kernels, local(): pl.pallas_call(functools.partial(attributes_kernel, two_sided), out_shape...  9.22 us
    ppermute x7, waiting for transfers between devices, flipped(): return lax.ppermute(value, axes, pairs)  7.9 us
    pallas_call x1, Pallas kernels, local(): pl.pallas_call(whiten_kernel, out_shape=(jax.ShapeDtypeStruct((CHAN, 8, 1...  7.5 us
    ppermute x1, starting transfers between devices, local(): near = lax.ppermute(near, 'inline', near_pairs)  3.08 us
    pallas_call x1, Pallas kernels, local(): pl.pallas_call(inline_kernel, out_shape=(jax.ShapeDtypeStruct((xl_len, 25...  2.98 us
    pallas_call x1, Pallas kernels, local(): pl.pallas_call(functools.partial(crossline_kernel, two_sided), out_shape=...  2.66 us
    pallas_call x1, Pallas kernels, local(): pl.pallas_call(functools.partial(prepare_kernel, stored), out_shape=(jax....  1.26 us
  transfers between devices with their start and end apart: 9, of which 6 were waited for; matrix products, arithmetic and copies ran while one was open for 2% of the time, Pallas kernels for 14%

profile of v6, /device:TPU:0, one launch (start us, length us, event | category | flops | bytes accessed | tf_op | source)
XLA Modules:
  0.0 50.6 jit_solution(18282893090390031024)
XLA Ops:
  0.6 0.7 %convert_element_type.7.trace_ref = f32[16,32]{1,0:T(8,128)S(1)} convert(s32[16,32]{1,0:T(8,128)} %live_ref.1) | non-fusion elementwise | flops 512 | bytes 4096 | tf_op jit(solution)/shard_map/convert_element_type | solution.py:519
  1.3 0.0 copy-start
  1.3 0.9 %copy-done = bf16[16,32,256]{2,1,0:T(8,128)(2,1)S(1)} copy-done((bf16[16,32,256]{2,1,0:T(8,128)(2,1)S(1)}, bf16[16,32,256]{2,1,0:T(8,128)(2,1)}, u32[]{:S(2)}) %copy-start) | copy-done | bytes 262168
  2.3 0.2 live.1
  2.5 3.1 %collective-permute-start = (bf16[256,256]{1,0:T(8,128)(2,1)S(1)}, bf16[256,256]{1,0:T(8,128)(2,1)S(1)}, u32[]{:S(2)}, u32[]{:S(2)}) collective-permute-start(bf16[256,256]{1,0:T(8,128)(2,1)S(1)} %get-tuple-element.34), channel_id=1, source_target_pairs={{0,4},{4,0},{8,12},{12,8},{1,5},{5,1},{9,13},{13,9},{2,6},{6,2},{1... | collective-permute-start | bytes 393224 | tf_op jit(solution)/shard_map/ppermute | solution.py:524
  5.6 0.7 %collective-permute-start.1 = (bf16[256,256]{1,0:T(8,128)(2,1)S(1)}, bf16[256,256]{1,0:T(8,128)(2,1)S(1)}, u32[]{:S(2)}, u32[]{:S(2)}) collective-permute-start(bf16[256,256]{1,0:T(8,128)(2,1)S(1)} %get-tuple-element.35), channel_id=1, source_target_pairs={{4,8},{8,4},{5,9},{9,5},{6,10},{10,6},{7,11},{11,7},{20,24},{24,20... | collective-permute-start | bytes 393224 | tf_op jit(solution)/shard_map/ppermute | solution.py:525
  6.3 0.8 %copy.6.taps_ref = f32[3,96,5]{2,1,0:T(8,128)S(1)} copy(bf16[3,96,5]{1,0,2:T(4,128)(2,1)} %param.5) | data formatting | bytes 8640 | tf_op jit(solution)/shard_map/convert_element_type | solution.py:501
  7.1 1.3 %prepare.1 = (bf16[768,128]{1,0:T(8,128)(2,1)S(1)}, f32[5,96,128]{2,1,0:T(8,128)S(1)}, f32[5,96,128]{2,1,0:T(8,128)S(1)}, bf16[256,256]{1,0:T(8,128)(2,1)S(1)}, ...) custom-call(f32[3,96,5]{2,1,0:T(8,128)S(1)} %copy.6.taps_ref, ...), custom_call_target="tpu_custom_call" | custom-call | flops 1000000000 | bytes 4000000 | tf_op jit(solution)/shard_map/prepare/pallas_call | solution.py:528
  8.4 0.0 collective-permute-done.1.far_ref
  8.4 0.7 %collective-permute-done.near_ref = bf16[256,256]{1,0:T(8,128)(2,1)S(1)} collective-permute-done((bf16[256,256]{1,0:T(8,128)(2,1)S(1)}, bf16[256,256]{1,0:T(8,128)(2,1)S(1)}, u32[]{:S(2)}, u32[]{:S(2)}) %collective-permute-start) | collective-permute-done | bytes 131104 | tf_op jit(solution)/shard_map/ppermute | solution.py:524
  9.1 1.7 %collective-permute-start.2 = (bf16[32,8,256]{2,1,0:T(8,128)(2,1)S(1)}, bf16[32,8,256]{2,1,0:T(8,128)(2,1)S(1)}, u32[]{:S(2)}, u32[]{:S(2)}) collective-permute-start(bf16[32,8,256]{2,1,0:T(8,128)(2,1)S(1)} %maximum_select_fusion), channel_id=1, source_target_pairs={{0,2},{2,0},{1,3},{3,1},{4,6},{6,4},{5,7},{7,5},{8,10},{10,8},{9,1... | collective-permute-start | bytes 393224 | tf_op jit(solution)/shard_map/ppermute | solution.py:57
  10.9 3.0 %inline.1 = (f32[32,256,256]{2,1,0:T(8,128)S(1)}, f32[16,512,128]{2,1,0:T(8,128)S(1)}, bf16[1024,128]{1,0:T(8,128)(2,1)S(1)}) custom-call(bf16[768,128]{1,0:T(8,128)(2,1)S(1)} %get-tuple-element.24.bands, bf16[256,256]{1,0:T(8,128)(2,1)S(1)} %get-tuple-element.31.pick, bf16[512,512]{1,0:T(8,128)(2,1)S(1)} %get-tuple-element.32.turn, ...), custom_call_target="tpu_custom_call" | custom-call | flops 4000000000 | bytes 16000000 | tf_op jit(solution)/shard_map/inline/pallas_call | solution.py:558
  13.8 0.3 collective-permute-done.2
  14.2 0.1 collective-permute-start.3
  14.3 0.0 copy-start.1
  14.3 2.7 %crossline.1 = (f32[3,256,256]{2,1,0:T(8,128)S(1)}, bf16[16,512,128]{2,1,0:T(8,128)(2,1)S(1)}) custom-call(bf16[768,128]{1,0:T(8,128)(2,1)S(1)} %get-tuple-element.24.bands, f32[5,96,128]{2,1,0:T(8,128)S(1)} %get-tuple-element.25.w2, bf16[256,256]{1,0:T(8,128)(2,1)S(1)} %get-tuple-element.31.pick, bf16[512,512]{1,0:T(8,128)(2,1)S(1)} %get-tuple-element.37.turn_x, ...), custom_call_target="tpu_custom_call" | custom-call | flops 3000000000 | bytes 9000000 | tf_op jit(solution)/shard_map/crossline/pallas_call | solution.py:579
  17.0 0.0 collective-permute-done.3.dh_ref
  17.0 0.0 copy-done.1
  17.0 9.2 %attributes.1 = (bf16[16,3,8,32,128]{4,3,2,1,0:T(8,128)(2,1)S(1)}, f32[96,128]{1,0:T(8,128)S(1)}) custom-call(s32[16,32]{1,0:T(8,128)S(1)} %copy-done.1, s32[16,32]{1,0:T(8,128)S(1)} %copy-done.1, bf16[768,128]{1,0:T(8,128)(2,1)S(1)} %get-tuple-element.24.bands, f32[5,96,128]{2,1,0:T(8,128)S(1)} %get-tuple-element.25.w2, ...), custom_call_target="tpu_custom_call" | custom-call | tf_op jit(solution)/shard_map/attributes/pallas_call | solution.py:595
  26.2 0.5 %collective-permute-start.4 = (f32[96,128]{1,0:T(8,128)S(1)}, f32[96,128]{1,0:T(8,128)S(1)}, u32[]{:S(2)}, u32[]{:S(2)}) collective-permute-start(f32[96,128]{1,0:T(8,128)S(1)} %get-tuple-element.42), channel_id=1, source_target_pairs={{0,1},{1,0},{2,3},{3,2},{4,5},{5,4},{6,7},{7,6},{8,9},{9,8},{10,11... | collective-permute-start | bytes 147464 | tf_op jit(solution)/shard_map/ppermute | solution.py:57
  26.8 0.9 %collective-permute-done.4 = f32[96,128]{1,0:T(8,128)S(1)} collective-permute-done((f32[96,128]{1,0:T(8,128)S(1)}, f32[96,128]{1,0:T(8,128)S(1)}, u32[]{:S(2)}, u32[]{:S(2)}) %collective-permute-start.4) | collective-permute-done | bytes 49184 | tf_op jit(solution)/shard_map/ppermute | solution.py:57
  27.6 1.7 %collective-permute-start.6 = (f32[96,128]{1,0:T(8,128)S(1)}, f32[96,128]{1,0:T(8,128)S(1)}, u32[]{:S(2)}, u32[]{:S(2)}) collective-permute-start(f32[96,128]{1,0:T(8,128)S(1)} %add.12), channel_id=1, source_target_pairs={{0,2},{2,0},{1,3},{3,1},{4,6},{6,4},{5,7},{7,5},{8,10},{10,8},{9,1... | collective-permute-start | bytes 147464 | tf_op jit(solution)/shard_map/ppermute | solution.py:57
  29.3 4.6 %collective-permute-start.7 = (f32[96,128]{1,0:T(8,128)S(1)}, f32[96,128]{1,0:T(8,128)S(1)}, u32[]{:S(2)}, u32[]{:S(2)}) collective-permute-start(f32[96,128]{1,0:T(8,128)S(1)} %add.12), channel_id=1, source_target_pairs={{0,6},{2,4},{4,2},{6,0},{8,14},{10,12},{12,10},{14,8},{1,7},{3,5},... | collective-permute-start | bytes 147464 | tf_op jit(solution)/shard_map/ppermute | solution.py:57
  33.9 0.0 collective-permute-start.5
  33.9 0.0 collective-permute-done.6
  33.9 2.0 %collective-permute-done.7 = f32[96,128]{1,0:T(8,128)S(1)} collective-permute-done((f32[96,128]{1,0:T(8,128)S(1)}, f32[96,128]{1,0:T(8,128)S(1)}, u32[]{:S(2)}, u32[]{:S(2)}) %collective-permute-start.7) | collective-permute-done | bytes 49184 | tf_op jit(solution)/shard_map/ppermute | solution.py:57
  36.0 2.0 %collective-permute-done.5 = f32[96,128]{1,0:T(8,128)S(1)} collective-permute-done((f32[96,128]{1,0:T(8,128)S(1)}, f32[96,128]{1,0:T(8,128)S(1)}, u32[]{:S(2)}, u32[]{:S(2)}) %collective-permute-start.5) | collective-permute-done | bytes 49184 | tf_op jit(solution)/shard_map/ppermute | solution.py:57
  38.0 2.4 %collective-permute-start.8 = (f32[96,128]{1,0:T(8,128)S(1)}, f32[96,128]{1,0:T(8,128)S(1)}, u32[]{:S(2)}, u32[]{:S(2)}) collective-permute-start(f32[96,128]{1,0:T(8,128)S(1)} %add_add_fusion.mine_ref), channel_id=1, source_target_pairs={{0,8},{4,12},{8,0},{12,4},{1,9},{5,13},{9,1},{13,5},{2,10},{6,14},... | collective-permute-start | bytes 147464 | tf_op jit(solution)/shard_map/ppermute | solution.py:57
  40.4 2.6 %collective-permute-done.8.other_ref = f32[96,128]{1,0:T(8,128)S(1)} collective-permute-done((f32[96,128]{1,0:T(8,128)S(1)}, f32[96,128]{1,0:T(8,128)S(1)}, u32[]{:S(2)}, u32[]{:S(2)}) %collective-permute-start.8) | collective-permute-done | bytes 49184 | tf_op jit(solution)/shard_map/ppermute | solution.py:57
  43.1 7.5 %whiten.1 = (bf16[96,8,16,128]{3,2,1,0:T(8,128)(2,1)}, f32[96,96]{1,0:T(8,128)}) custom-call(f32[96,128]{1,0:T(8,128)S(1)} %add_add_fusion.mine_ref, f32[96,128]{1,0:T(8,128)S(1)} %collective-permute-done.8.other_ref, bf16[16,3,8,32,128]{4,3,2,1,0:T(8,128)(2,1)S(1)} %get-tuple-element.43.attr_ref), custom_call_target="tpu_custom_call" | custom-call | tf_op jit(solution)/shard_map/whiten/pallas_call | solution.py:612
  (8 shorter events, 0.1 us)
Async XLA Ops:
  1.3 0.9 %copy-start = (bf16[16,32,256]{2,1,0:T(8,128)(2,1)S(1)}, bf16[16,32,256]{2,1,0:T(8,128)(2,1)}, u32[]{:S(2)}) copy-start(bf16[16,32,256]{2,1,0:T(8,128)(2,1)} %seismic_ref.1) | copy-start | bytes 786436
  2.5 6.6 %collective-permute-start = (bf16[256,256]{1,0:T(8,128)(2,1)S(1)}, bf16[256,256]{1,0:T(8,128)(2,1)S(1)}, u32[]{:S(2)}, u32[]{:S(2)}) collective-permute-start(bf16[256,256]{1,0:T(8,128)(2,1)S(1)} %get-tuple-element.34), channel_id=1, source_target_pairs={{0,4},{4,0},{8,12},{12,8},{1,5},{5,1},{9,13},{13,9},{2,6},{6,2},{1... | collective-permute-start | bytes 393224 | tf_op jit(solution)/shard_map/ppermute | solution.py:524
  5.6 2.8 %collective-permute-start.1 = (bf16[256,256]{1,0:T(8,128)(2,1)S(1)}, bf16[256,256]{1,0:T(8,128)(2,1)S(1)}, u32[]{:S(2)}, u32[]{:S(2)}) collective-permute-start(bf16[256,256]{1,0:T(8,128)(2,1)S(1)} %get-tuple-element.35), channel_id=1, source_target_pairs={{4,8},{8,4},{5,9},{9,5},{6,10},{10,6},{7,11},{11,7},{20,24},{24,20... | collective-permute-start | bytes 393224 | tf_op jit(solution)/shard_map/ppermute | solution.py:525
  9.1 5.0 %collective-permute-start.2 = (bf16[32,8,256]{2,1,0:T(8,128)(2,1)S(1)}, bf16[32,8,256]{2,1,0:T(8,128)(2,1)S(1)}, u32[]{:S(2)}, u32[]{:S(2)}) collective-permute-start(bf16[32,8,256]{2,1,0:T(8,128)(2,1)S(1)} %maximum_select_fusion), channel_id=1, source_target_pairs={{0,2},{2,0},{1,3},{3,1},{4,6},{6,4},{5,7},{7,5},{8,10},{10,8},{9,1... | collective-permute-start | bytes 393224 | tf_op jit(solution)/shard_map/ppermute | solution.py:57
  14.2 2.8 %collective-permute-start.3 = (bf16[32,40,128]{2,1,0:T(8,128)(2,1)S(1)}, bf16[32,40,128]{2,1,0:T(8,128)(2,1)S(1)}, u32[]{:S(2)}, u32[]{:S(2)}) collective-permute-start(bf16[32,40,128]{2,1,0:T(8,128)(2,1)S(1)} %pad_maximum_fusion), channel_id=1, source_target_pairs={{0,1},{1,0},{2,3},{3,2},{4,5},{5,4},{6,7},{7,6},{8,9},{9,8},{10,11... | collective-permute-start | bytes 983048 | tf_op jit(solution)/shard_map/ppermute | solution.py:57
  14.3 2.7 %copy-start.1 = (s32[16,32]{1,0:T(8,128)S(1)}, s32[16,32]{1,0:T(8,128)}, u32[]{:S(2)}) copy-start(s32[16,32]{1,0:T(8,128)} %live_ref.1) | copy-start | bytes 6148
  26.2 1.4 %collective-permute-start.4 = (f32[96,128]{1,0:T(8,128)S(1)}, f32[96,128]{1,0:T(8,128)S(1)}, u32[]{:S(2)}, u32[]{:S(2)}) collective-permute-start(f32[96,128]{1,0:T(8,128)S(1)} %get-tuple-element.42), channel_id=1, source_target_pairs={{0,1},{1,0},{2,3},{3,2},{4,5},{5,4},{6,7},{7,6},{8,9},{9,8},{10,11... | collective-permute-start | bytes 147464 | tf_op jit(solution)/shard_map/ppermute | solution.py:57
  27.6 6.3 %collective-permute-start.6 = (f32[96,128]{1,0:T(8,128)S(1)}, f32[96,128]{1,0:T(8,128)S(1)}, u32[]{:S(2)}, u32[]{:S(2)}) collective-permute-start(f32[96,128]{1,0:T(8,128)S(1)} %add.12), channel_id=1, source_target_pairs={{0,2},{2,0},{1,3},{3,1},{4,6},{6,4},{5,7},{7,5},{8,10},{10,8},{9,1... | collective-permute-start | bytes 147464 | tf_op jit(solution)/shard_map/ppermute | solution.py:57
  29.3 6.7 %collective-permute-start.7 = (f32[96,128]{1,0:T(8,128)S(1)}, f32[96,128]{1,0:T(8,128)S(1)}, u32[]{:S(2)}, u32[]{:S(2)}) collective-permute-start(f32[96,128]{1,0:T(8,128)S(1)} %add.12), channel_id=1, source_target_pairs={{0,6},{2,4},{4,2},{6,0},{8,14},{10,12},{12,10},{14,8},{1,7},{3,5},... | collective-permute-start | bytes 147464 | tf_op jit(solution)/shard_map/ppermute | solution.py:57
  33.9 4.1 %collective-permute-start.5 = (f32[96,128]{1,0:T(8,128)S(1)}, f32[96,128]{1,0:T(8,128)S(1)}, u32[]{:S(2)}, u32[]{:S(2)}) collective-permute-start(f32[96,128]{1,0:T(8,128)S(1)} %add.12), channel_id=1, source_target_pairs={{0,4},{4,0},{8,12},{12,8},{1,5},{5,1},{9,13},{13,9},{2,6},{6,2},{1... | collective-permute-start | bytes 147464 | tf_op jit(solution)/shard_map/ppermute | solution.py:57
  38.0 5.1 %collective-permute-start.8 = (f32[96,128]{1,0:T(8,128)S(1)}, f32[96,128]{1,0:T(8,128)S(1)}, u32[]{:S(2)}, u32[]{:S(2)}) collective-permute-start(f32[96,128]{1,0:T(8,128)S(1)} %add_add_fusion.mine_ref), channel_id=1, source_target_pairs={{0,8},{4,12},{8,0},{12,4},{1,9},{5,13},{9,1},{13,5},{2,10},{6,14},... | collective-permute-start | bytes 147464 | tf_op jit(solution)/shard_map/ppermute | solution.py:57

commit v7 on v6

--- a/solution.py
+++ b/solution.py
@@ -12,6 +12,10 @@
 TAPS = 5
 CHAN = 96
 REACH = 8
+LAST_ROWS = (8, 10, 12, 14, 15)
+FIRST_ROWS = (0, 2, 4, 6, 7)
+SENT = 5
+ROWS = 16 + 2 * SENT
 KEPT = 5
 F32 = jnp.float32
 BF16 = jnp.bfloat16
@@ -120,19 +124,21 @@
         row = jnp.broadcast_to(trace_ref[p : p + 1, :], (n_xl, n_xl))
         kept = dot(jnp.where(eye, row, 0.0).astype(BF16), seismic_ref[p])
         live_ref[p * n_xl : (p + 1) * n_xl, :] = kept.astype(BF16)
-    count = REACH * n_xl
-    start = (n_il - REACH) * n_xl
     odd = side_flags()[2]
+
+    def put(ref, rows):
+        for i, p in enumerate(rows):
+            ref[i * n_xl : (i + 1) * n_xl] = live_ref[p * n_xl : (p + 1) * n_xl]
 
     @pl.when(odd == 1)
     def _():
-        near_ref[...] = live_ref[0:count]
-        far_ref[...] = live_ref[start : start + count]
+        put(near_ref, FIRST_ROWS)
+        put(far_ref, LAST_ROWS)
 
     @pl.when(odd == 0)
     def _():
-        near_ref[...] = live_ref[start : start + count]
-        far_ref[...] = live_ref[0:count]
+        put(near_ref, LAST_ROWS)
+        put(far_ref, FIRST_ROWS)
 
 
 def banded(level, taps_ref, bands, il_odd):
@@ -144,9 +150,9 @@
         for k in range(TAPS):
             p = 2 * o + 2 ** level * (k - 2)
             if p < 0:
-                place = p + 32 - 8 * il_odd
+                place = 16 + SENT + LAST_ROWS.index(p + 16) - SENT * il_odd
             elif p >= 16:
-                place = p + 8 * il_odd
+                place = 16 + FIRST_ROWS.index(p - 16) + SENT * il_odd
             else:
                 place = p
             total = jnp.where(lane == place, cols[k], total)
@@ -173,7 +179,8 @@
     r = iota((512, 512), 0)
     c = iota((512, 512), 1)
     turn[...] = ones_where(c == r % 32 * 16 + r // 32)
-    turn_x[...] = ones_where(c == r // 256 * 256 + r % 32 * 8 + r // 32 % 8)
+    source = r // 256 * (8 * ROWS) + r % 32 * 8 + r // 32 % 8
+    turn_x[...] = ones_where(jnp.where(r % 32 < ROWS, source, -1) == c)
     moves1[...] = shift_matrix((-2, -1, 1, 2))
     moves2[...] = shift_matrix((-4, -2, 2, 4))
     rows = 32 * stored
@@ -186,18 +193,19 @@
     depth_first = side_flags()[1]
 
     def put_edge(ts):
-        for at, ref in ((0, own_ref), (512, near_ref), (768, far_ref)):
+        for at, ref in ((0, own_ref), (512, near_ref), (512 + near_ref.shape[0], far_ref)):
             edge_ref[at : at + ref.shape[0], :] = ref[:, ts]
 
     pl.when(depth_first == 1)(lambda: put_edge(slice(128, 256)))
     pl.when(depth_first == 0)(lambda: put_edge(slice(0, 128)))
 
     own = own_phases[...].reshape(16, 32, 256)
-    near = dot(near_ref[...], pick[...]).astype(BF16).reshape(8, 32, 256)
-    far = dot(far_ref[...], pick[...]).astype(BF16).reshape(8, 32, 256)
+    near = dot(near_ref[...], pick[...]).astype(BF16).reshape(SENT, 32, 256)
+    far = dot(far_ref[...], pick[...]).astype(BF16).reshape(SENT, 32, 256)
+    none = jnp.zeros((32 - ROWS, 16, 256), BF16)
     for half in range(2):
         js = slice(half * 16, half * 16 + 16)
-        block = jnp.concatenate([own[:, js], near[:, js], far[:, js]], axis=0).reshape(512, 256)
+        block = jnp.concatenate([own[:, js], near[:, js], far[:, js], none], axis=0).reshape(512, 256)
         planes[half * 16 : half * 16 + 16] = dot(turn[...], block).astype(BF16).reshape(16, 32, 256)
 
     a0 = bands[0:256, 0:32]
@@ -231,7 +239,8 @@
     if not two_sided:
         left = jnp.where(x_left == 1, 1.0, 0.0)
         got = jnp.concatenate([got * left, got * (1.0 - left)], axis=0)
-    edges[...] = dot(turn_x[...], got.astype(BF16)).astype(BF16).reshape(16, 32, 256)
+    got = jnp.concatenate([got.astype(BF16), jnp.zeros((512 - 16 * ROWS, 256), BF16)], axis=0)
+    edges[...] = dot(turn_x[...], got).astype(BF16).reshape(16, 32, 256)
     a0 = bands[0:256, 0:32]
     a12 = bands[256:768, 0:32]
     for i, slot in enumerate((6, 7, 8)):
@@ -285,7 +294,9 @@
     sample = jnp.where(kept < KEPT, sample, -1)
     spread = ones_where(iota((128, 256), 0) == sample)
     rows = 32 * stored
-    wide = dot(dh_ref[...].reshape(rows, 128), spread)
+    got = dh_ref[...].reshape(ROWS * stored, 128)
+    got = jnp.concatenate([got, jnp.zeros((rows - ROWS * stored, 128), BF16)], axis=0)
+    wide = dot(got, spread)
     wide = jnp.where(iota((rows, 256), 0) % stored == n % stored, wide, 0.0).astype(BF16)
     lanes = dot(gather[...], wide).astype(BF16)
     for level in range(3):
@@ -509,8 +520,8 @@
         live_kernel,
         out_shape=(
             jax.ShapeDtypeStruct((il_len * xl_len, t_len), BF16),
-            jax.ShapeDtypeStruct((REACH * xl_len, t_len), BF16),
-            jax.ShapeDtypeStruct((REACH * xl_len, t_len), BF16),
+            jax.ShapeDtypeStruct((SENT * xl_len, t_len), BF16),
+            jax.ShapeDtypeStruct((SENT * xl_len, t_len), BF16),
         ),
         in_specs=[vmem] * 2,
         out_specs=(vmem,) * 3,
@@ -560,7 +571,7 @@
         out_shape=(
             jax.ShapeDtypeStruct((xl_len, 256, 256), F32),
             jax.ShapeDtypeStruct((xl_len // 2, 512, 128), F32),
-            jax.ShapeDtypeStruct((32 * xl_len, 128), BF16),
+            jax.ShapeDtypeStruct((ROWS * xl_len, 128), BF16),
         ),
         in_specs=[vmem] * 7,
         out_specs=(vmem,) * 3,
@@ -573,9 +584,9 @@
     def side(x):
         return jnp.where(d_index == 0, x[:, :, t_len - 128 :], x[:, :, :128])
 
-    dh = jnp.concatenate([edge.reshape(32, xl_len, 128)] + [side(x) for x in xh], axis=1)
+    dh = jnp.concatenate([edge.reshape(ROWS, xl_len, 128)] + [side(x) for x in xh], axis=1)
     dh = flipped(dh, [("depth", 1)])
-    xrows = jnp.concatenate([x.reshape(256, t_len) for x in xh], axis=0)
+    xrows = jnp.concatenate([x.reshape(REACH * ROWS, t_len) for x in xh], axis=0)
     edge0, second12 = pl.pallas_call(
         functools.partial(crossline_kernel, two_sided),
         out_shape=(

time: 50.8 us -> 50.1 us (0.986)
  waiting for transfers between devices: 8.58 us -> 7.57 us
    ppermute x1, waiting for transfers between devices: 0.68 us -> 0.01 us  [local(): near = lax.ppermute(near, 'inline', near_pairs)]
  transfers between devices with their start and end apart: 9 -> 9, of which waited for: 6 -> 5; matrix products, arithmetic and copies ran while one was open for 2% -> 2% of each run, Pallas kernels for 14% -> 14%
where the time goes in v7:
time: 50.1 us; the launch traced here: 49.9 us
  Pallas kernels  24.2 us (48%)
  starting transfers between devices  14.7 us (29%)
  waiting for transfers between devices  7.57 us (15%)
  local copies, waits for them, and re-layouts  1.8 us (4%)
  other arithmetic  0.79 us (2%)
  between operations  0.78 us (2%)
    ppermute x7, starting transfers between devices, flipped(): return lax.ppermute(value, axes, pairs)  11 us
    pallas_call x1, Pallas kernels, local(): pl.pallas_call(functools.partial(attributes_kernel, two_sided), out_shape...  9.49 us
    ppermute x7, waiting for transfers between devices, flipped(): return lax.ppermute(value, axes, pairs)  7.57 us
    pallas_call x1, Pallas kernels, local(): pl.pallas_call(whiten_kernel, out_shape=(jax.ShapeDtypeStruct((CHAN, 8, 1...  7.51 us
    ppermute x1, starting transfers between devices, local(): near = lax.ppermute(near, 'inline', near_pairs)  3.09 us
    pallas_call x1, Pallas kernels, local(): pl.pallas_call(inline_kernel, out_shape=(jax.ShapeDtypeStruct((xl_len, 25...  2.94 us
    pallas_call x1, Pallas kernels, local(): pl.pallas_call(functools.partial(crossline_kernel, two_sided), out_shape=...  2.78 us
    pallas_call x1, Pallas kernels, local(): pl.pallas_call(functools.partial(prepare_kernel, stored), out_shape=(jax....  1.27 us
  transfers between devices with their start and end apart: 9, of which 5 were waited for; matrix products, arithmetic and copies ran while one was open for 2% of the time, Pallas kernels for 14%

profile of v7, /device:TPU:0, one launch (start us, length us, event | category | flops | bytes accessed | tf_op | source)
XLA Modules:
  0.0 49.9 jit_solution(4296831065017386743)
XLA Ops:
  0.6 0.7 %convert_element_type.7.trace_ref = f32[16,32]{1,0:T(8,128)S(1)} convert(s32[16,32]{1,0:T(8,128)} %live_ref.1) | non-fusion elementwise | flops 512 | bytes 4096 | tf_op jit(solution)/shard_map/convert_element_type | solution.py:530
  1.3 0.0 copy-start
  1.3 0.9 %copy-done = bf16[16,32,256]{2,1,0:T(8,128)(2,1)S(1)} copy-done((bf16[16,32,256]{2,1,0:T(8,128)(2,1)S(1)}, bf16[16,32,256]{2,1,0:T(8,128)(2,1)}, u32[]{:S(2)}) %copy-start) | copy-done | bytes 262168
  2.3 0.2 live.1
  2.5 3.1 %collective-permute-start = (bf16[160,256]{1,0:T(8,128)(2,1)S(1)}, bf16[160,256]{1,0:T(8,128)(2,1)S(1)}, u32[]{:S(2)}, u32[]{:S(2)}) collective-permute-start(bf16[160,256]{1,0:T(8,128)(2,1)S(1)} %get-tuple-element.34), channel_id=1, source_target_pairs={{0,4},{4,0},{8,12},{12,8},{1,5},{5,1},{9,13},{13,9},{2,6},{6,2},{1... | collective-permute-start | bytes 245768 | tf_op jit(solution)/shard_map/ppermute | solution.py:535
  5.6 0.7 %collective-permute-start.1 = (bf16[160,256]{1,0:T(8,128)(2,1)S(1)}, bf16[160,256]{1,0:T(8,128)(2,1)S(1)}, u32[]{:S(2)}, u32[]{:S(2)}) collective-permute-start(bf16[160,256]{1,0:T(8,128)(2,1)S(1)} %get-tuple-element.35), channel_id=1, source_target_pairs={{4,8},{8,4},{5,9},{9,5},{6,10},{10,6},{7,11},{11,7},{20,24},{24,20... | collective-permute-start | bytes 245768 | tf_op jit(solution)/shard_map/ppermute | solution.py:536
  6.3 0.8 %copy.6.taps_ref = f32[3,96,5]{2,1,0:T(8,128)S(1)} copy(bf16[3,96,5]{1,0,2:T(4,128)(2,1)} %param.5) | data formatting | bytes 8640 | tf_op jit(solution)/shard_map/convert_element_type | solution.py:512
  7.1 1.3 %prepare.1 = (bf16[768,128]{1,0:T(8,128)(2,1)S(1)}, f32[5,96,128]{2,1,0:T(8,128)S(1)}, f32[5,96,128]{2,1,0:T(8,128)S(1)}, bf16[256,256]{1,0:T(8,128)(2,1)S(1)}, ...) custom-call(f32[3,96,5]{2,1,0:T(8,128)S(1)} %copy.6.taps_ref, ...), custom_call_target="tpu_custom_call" | custom-call | flops 1000000000 | bytes 4000000 | tf_op jit(solution)/shard_map/prepare/pallas_call | solution.py:539
  8.4 0.0 collective-permute-done.1.far_ref
  8.4 0.0 collective-permute-done.near_ref
  8.5 1.6 %collective-permute-start.2 = (bf16[26,8,256]{2,1,0:T(8,128)(2,1)S(1)}, bf16[26,8,256]{2,1,0:T(8,128)(2,1)S(1)}, u32[]{:S(2)}, u32[]{:S(2)}) collective-permute-start(bf16[26,8,256]{2,1,0:T(8,128)(2,1)S(1)} %maximum_select_fusion), channel_id=1, source_target_pairs={{0,2},{2,0},{1,3},{3,1},{4,6},{6,4},{5,7},{7,5},{8,10},{10,8},{9,1... | collective-permute-start | bytes 319496 | tf_op jit(solution)/shard_map/ppermute | solution.py:61
  10.0 2.9 %inline.1 = (f32[32,256,256]{2,1,0:T(8,128)S(1)}, f32[16,512,128]{2,1,0:T(8,128)S(1)}, bf16[832,128]{1,0:T(8,128)(2,1)S(1)}) custom-call(bf16[768,128]{1,0:T(8,128)(2,1)S(1)} %get-tuple-element.24.bands, bf16[256,256]{1,0:T(8,128)(2,1)S(1)} %get-tuple-element.31.pick, bf16[512,512]{1,0:T(8,128)(2,1)S(1)} %get-tuple-element.32.turn, ...), custom_call_target="tpu_custom_call" | custom-call | flops 4000000000 | bytes 16000000 | tf_op jit(solution)/shard_map/inline/pallas_call | solution.py:569
  13.0 0.2 collective-permute-done.2
  13.3 0.1 collective-permute-start.3
  13.4 0.0 copy-start.1
  13.4 2.8 %crossline.1 = (f32[3,256,256]{2,1,0:T(8,128)S(1)}, bf16[16,512,128]{2,1,0:T(8,128)(2,1)S(1)}) custom-call(bf16[768,128]{1,0:T(8,128)(2,1)S(1)} %get-tuple-element.24.bands, f32[5,96,128]{2,1,0:T(8,128)S(1)} %get-tuple-element.25.w2, bf16[256,256]{1,0:T(8,128)(2,1)S(1)} %get-tuple-element.31.pick, bf16[512,512]{1,0:T(8,128)(2,1)S(1)} %get-tuple-element.37.turn_x, ...), custom_call_target="tpu_custom_call" | custom-call | flops 3000000000 | bytes 9000000 | tf_op jit(solution)/shard_map/crossline/pallas_call | solution.py:590
  16.2 0.0 collective-permute-done.3.dh_ref
  16.2 0.0 copy-done.1
  16.2 9.5 %attributes.1 = (bf16[16,3,8,32,128]{4,3,2,1,0:T(8,128)(2,1)S(1)}, f32[96,128]{1,0:T(8,128)S(1)}) custom-call(s32[16,32]{1,0:T(8,128)S(1)} %copy-done.1, s32[16,32]{1,0:T(8,128)S(1)} %copy-done.1, bf16[768,128]{1,0:T(8,128)(2,1)S(1)} %get-tuple-element.24.bands, f32[5,96,128]{2,1,0:T(8,128)S(1)} %get-tuple-element.25.w2, ...), custom_call_target="tpu_custom_call" | custom-call | tf_op jit(solution)/shard_map/attributes/pallas_call | solution.py:606
  25.7 0.5 %collective-permute-start.4 = (f32[96,128]{1,0:T(8,128)S(1)}, f32[96,128]{1,0:T(8,128)S(1)}, u32[]{:S(2)}, u32[]{:S(2)}) collective-permute-start(f32[96,128]{1,0:T(8,128)S(1)} %get-tuple-element.42), channel_id=1, source_target_pairs={{0,1},{1,0},{2,3},{3,2},{4,5},{5,4},{6,7},{7,6},{8,9},{9,8},{10,11... | collective-permute-start | bytes 147464 | tf_op jit(solution)/shard_map/ppermute | solution.py:61
  26.2 0.9 %collective-permute-done.4 = f32[96,128]{1,0:T(8,128)S(1)} collective-permute-done((f32[96,128]{1,0:T(8,128)S(1)}, f32[96,128]{1,0:T(8,128)S(1)}, u32[]{:S(2)}, u32[]{:S(2)}) %collective-permute-start.4) | collective-permute-done | bytes 49184 | tf_op jit(solution)/shard_map/ppermute | solution.py:61
  27.1 1.5 %collective-permute-start.6 = (f32[96,128]{1,0:T(8,128)S(1)}, f32[96,128]{1,0:T(8,128)S(1)}, u32[]{:S(2)}, u32[]{:S(2)}) collective-permute-start(f32[96,128]{1,0:T(8,128)S(1)} %add.12), channel_id=1, source_target_pairs={{0,2},{2,0},{1,3},{3,1},{4,6},{6,4},{5,7},{7,5},{8,10},{10,8},{9,1... | collective-permute-start | bytes 147464 | tf_op jit(solution)/shard_map/ppermute | solution.py:61
  28.6 4.6 %collective-permute-start.7 = (f32[96,128]{1,0:T(8,128)S(1)}, f32[96,128]{1,0:T(8,128)S(1)}, u32[]{:S(2)}, u32[]{:S(2)}) collective-permute-start(f32[96,128]{1,0:T(8,128)S(1)} %add.12), channel_id=1, source_target_pairs={{0,6},{2,4},{4,2},{6,0},{8,14},{10,12},{12,10},{14,8},{1,7},{3,5},... | collective-permute-start | bytes 147464 | tf_op jit(solution)/shard_map/ppermute | solution.py:61
  33.2 0.0 collective-permute-start.5
  33.2 0.0 collective-permute-done.6
  33.2 2.0 %collective-permute-done.7 = f32[96,128]{1,0:T(8,128)S(1)} collective-permute-done((f32[96,128]{1,0:T(8,128)S(1)}, f32[96,128]{1,0:T(8,128)S(1)}, u32[]{:S(2)}, u32[]{:S(2)}) %collective-permute-start.7) | collective-permute-done | bytes 49184 | tf_op jit(solution)/shard_map/ppermute | solution.py:61
  35.3 2.0 %collective-permute-done.5 = f32[96,128]{1,0:T(8,128)S(1)} collective-permute-done((f32[96,128]{1,0:T(8,128)S(1)}, f32[96,128]{1,0:T(8,128)S(1)}, u32[]{:S(2)}, u32[]{:S(2)}) %collective-permute-start.5) | collective-permute-done | bytes 49184 | tf_op jit(solution)/shard_map/ppermute | solution.py:61
  37.3 2.7 %collective-permute-start.8 = (f32[96,128]{1,0:T(8,128)S(1)}, f32[96,128]{1,0:T(8,128)S(1)}, u32[]{:S(2)}, u32[]{:S(2)}) collective-permute-start(f32[96,128]{1,0:T(8,128)S(1)} %add_add_fusion.mine_ref), channel_id=1, source_target_pairs={{0,8},{4,12},{8,0},{12,4},{1,9},{5,13},{9,1},{13,5},{2,10},{6,14},... | collective-permute-start | bytes 147464 | tf_op jit(solution)/shard_map/ppermute | solution.py:61
  40.0 2.4 %collective-permute-done.8.other_ref = f32[96,128]{1,0:T(8,128)S(1)} collective-permute-done((f32[96,128]{1,0:T(8,128)S(1)}, f32[96,128]{1,0:T(8,128)S(1)}, u32[]{:S(2)}, u32[]{:S(2)}) %collective-permute-start.8) | collective-permute-done | bytes 49184 | tf_op jit(solution)/shard_map/ppermute | solution.py:61
  42.4 7.5 %whiten.1 = (bf16[96,8,16,128]{3,2,1,0:T(8,128)(2,1)}, f32[96,96]{1,0:T(8,128)}) custom-call(f32[96,128]{1,0:T(8,128)S(1)} %add_add_fusion.mine_ref, f32[96,128]{1,0:T(8,128)S(1)} %collective-permute-done.8.other_ref, bf16[16,3,8,32,128]{4,3,2,1,0:T(8,128)(2,1)S(1)} %get-tuple-element.43.attr_ref), custom_call_target="tpu_custom_call" | custom-call | tf_op jit(solution)/shard_map/whiten/pallas_call | solution.py:623
  (8 shorter events, 0.1 us)
Async XLA Ops:
  1.3 0.9 %copy-start = (bf16[16,32,256]{2,1,0:T(8,128)(2,1)S(1)}, bf16[16,32,256]{2,1,0:T(8,128)(2,1)}, u32[]{:S(2)}) copy-start(bf16[16,32,256]{2,1,0:T(8,128)(2,1)} %seismic_ref.1) | copy-start | bytes 786436
  2.5 5.9 %collective-permute-start = (bf16[160,256]{1,0:T(8,128)(2,1)S(1)}, bf16[160,256]{1,0:T(8,128)(2,1)S(1)}, u32[]{:S(2)}, u32[]{:S(2)}) collective-permute-start(bf16[160,256]{1,0:T(8,128)(2,1)S(1)} %get-tuple-element.34), channel_id=1, source_target_pairs={{0,4},{4,0},{8,12},{12,8},{1,5},{5,1},{9,13},{13,9},{2,6},{6,2},{1... | collective-permute-start | bytes 245768 | tf_op jit(solution)/shard_map/ppermute | solution.py:535
  5.6 2.8 %collective-permute-start.1 = (bf16[160,256]{1,0:T(8,128)(2,1)S(1)}, bf16[160,256]{1,0:T(8,128)(2,1)S(1)}, u32[]{:S(2)}, u32[]{:S(2)}) collective-permute-start(bf16[160,256]{1,0:T(8,128)(2,1)S(1)} %get-tuple-element.35), channel_id=1, source_target_pairs={{4,8},{8,4},{5,9},{9,5},{6,10},{10,6},{7,11},{11,7},{20,24},{24,20... | collective-permute-start | bytes 245768 | tf_op jit(solution)/shard_map/ppermute | solution.py:536
  8.5 4.8 %collective-permute-start.2 = (bf16[26,8,256]{2,1,0:T(8,128)(2,1)S(1)}, bf16[26,8,256]{2,1,0:T(8,128)(2,1)S(1)}, u32[]{:S(2)}, u32[]{:S(2)}) collective-permute-start(bf16[26,8,256]{2,1,0:T(8,128)(2,1)S(1)} %maximum_select_fusion), channel_id=1, source_target_pairs={{0,2},{2,0},{1,3},{3,1},{4,6},{6,4},{5,7},{7,5},{8,10},{10,8},{9,1... | collective-permute-start | bytes 319496 | tf_op jit(solution)/shard_map/ppermute | solution.py:61
  13.3 2.9 %collective-permute-start.3 = (bf16[26,40,128]{2,1,0:T(8,128)(2,1)S(1)}, bf16[26,40,128]{2,1,0:T(8,128)(2,1)S(1)}, u32[]{:S(2)}, u32[]{:S(2)}) collective-permute-start(bf16[26,40,128]{2,1,0:T(8,128)(2,1)S(1)} %pad_maximum_fusion), channel_id=1, source_target_pairs={{0,1},{1,0},{2,3},{3,2},{4,5},{5,4},{6,7},{7,6},{8,9},{9,8},{10,11... | collective-permute-start | bytes 798728 | tf_op jit(solution)/shard_map/ppermute | solution.py:61
  13.4 2.8 %copy-start.1 = (s32[16,32]{1,0:T(8,128)S(1)}, s32[16,32]{1,0:T(8,128)}, u32[]{:S(2)}) copy-start(s32[16,32]{1,0:T(8,128)} %live_ref.1) | copy-start | bytes 6148
  25.7 1.4 %collective-permute-start.4 = (f32[96,128]{1,0:T(8,128)S(1)}, f32[96,128]{1,0:T(8,128)S(1)}, u32[]{:S(2)}, u32[]{:S(2)}) collective-permute-start(f32[96,128]{1,0:T(8,128)S(1)} %get-tuple-element.42), channel_id=1, source_target_pairs={{0,1},{1,0},{2,3},{3,2},{4,5},{5,4},{6,7},{7,6},{8,9},{9,8},{10,11... | collective-permute-start | bytes 147464 | tf_op jit(solution)/shard_map/ppermute | solution.py:61
  27.1 6.1 %collective-permute-start.6 = (f32[96,128]{1,0:T(8,128)S(1)}, f32[96,128]{1,0:T(8,128)S(1)}, u32[]{:S(2)}, u32[]{:S(2)}) collective-permute-start(f32[96,128]{1,0:T(8,128)S(1)} %add.12), channel_id=1, source_target_pairs={{0,2},{2,0},{1,3},{3,1},{4,6},{6,4},{5,7},{7,5},{8,10},{10,8},{9,1... | collective-permute-start | bytes 147464 | tf_op jit(solution)/shard_map/ppermute | solution.py:61
  28.6 6.7 %collective-permute-start.7 = (f32[96,128]{1,0:T(8,128)S(1)}, f32[96,128]{1,0:T(8,128)S(1)}, u32[]{:S(2)}, u32[]{:S(2)}) collective-permute-start(f32[96,128]{1,0:T(8,128)S(1)} %add.12), channel_id=1, source_target_pairs={{0,6},{2,4},{4,2},{6,0},{8,14},{10,12},{12,10},{14,8},{1,7},{3,5},... | collective-permute-start | bytes 147464 | tf_op jit(solution)/shard_map/ppermute | solution.py:61
  33.2 4.1 %collective-permute-start.5 = (f32[96,128]{1,0:T(8,128)S(1)}, f32[96,128]{1,0:T(8,128)S(1)}, u32[]{:S(2)}, u32[]{:S(2)}) collective-permute-start(f32[96,128]{1,0:T(8,128)S(1)} %add.12), channel_id=1, source_target_pairs={{0,4},{4,0},{8,12},{12,8},{1,5},{5,1},{9,13},{13,9},{2,6},{6,2},{1... | collective-permute-start | bytes 147464 | tf_op jit(solution)/shard_map/ppermute | solution.py:61
  37.3 5.1 %collective-permute-start.8 = (f32[96,128]{1,0:T(8,128)S(1)}, f32[96,128]{1,0:T(8,128)S(1)}, u32[]{:S(2)}, u32[]{:S(2)}) collective-permute-start(f32[96,128]{1,0:T(8,128)S(1)} %add_add_fusion.mine_ref), channel_id=1, source_target_pairs={{0,8},{4,12},{8,0},{12,4},{1,9},{5,13},{9,1},{13,5},{2,10},{6,14},... | collective-permute-start | bytes 147464 | tf_op jit(solution)/shard_map/ppermute | solution.py:61

commit v8 on v7

--- a/solution.py
+++ b/solution.py
@@ -165,32 +165,36 @@
 
 
 def prepare_kernel(
-    stored, taps_ref, own_ref, bands, w2, w3, pick, turn, turn_x, own_out, moves1, moves2, select, gather
+    taps_ref, own_ref, bands, w2, w3, pick, turn, own_out
 ):
-    x_left, depth_first, il_odd = side_flags()
+    il_odd = side_flags()[2]
     for k in range(TAPS):
         w2[k] = jnp.broadcast_to(taps_ref[1, :, k : k + 1], (CHAN, 128))
         w3[k] = jnp.broadcast_to(taps_ref[2, :, k : k + 1], (CHAN, 128))
     for level in range(3):
         banded(level, taps_ref, bands, il_odd)
-        select[level] = halo_select(level, stored, x_left, depth_first)
     pick[...] = phase_pick()
     own_out[...] = dot(own_ref[...], pick[...]).astype(BF16)
     r = iota((512, 512), 0)
     c = iota((512, 512), 1)
     turn[...] = ones_where(c == r % 32 * 16 + r // 32)
+
+
+def inline_kernel(
+    stored, bands, pick, turn, own_ref, own_phases, near_ref, far_ref, first0, first12, edge_ref,
+    turn_x, moves1, moves2, select, gather, planes,
+):
+    x_left, depth_first, _ = side_flags()
+    r = iota((512, 512), 0)
+    c = iota((512, 512), 1)
     source = r // 256 * (8 * ROWS) + r % 32 * 8 + r // 32 % 8
     turn_x[...] = ones_where(jnp.where(r % 32 < ROWS, source, -1) == c)
     moves1[...] = shift_matrix((-2, -1, 1, 2))
     moves2[...] = shift_matrix((-4, -2, 2, 4))
     rows = 32 * stored
     gather[...] = ones_where(iota((32, rows), 1) // stored == iota((32, rows), 0))
-
-
-def inline_kernel(
-    bands, pick, turn, own_ref, own_phases, near_ref, far_ref, first0, first12, edge_ref, planes
-):
-    depth_first = side_flags()[1]
+    for level in range(3):
+        select[level] = halo_select(level, stored, x_left, depth_first)
 
     def put_edge(ts):
         for at, ref in ((0, own_ref), (512, near_ref), (512 + near_ref.shape[0], far_ref)):
@@ -214,7 +218,7 @@
         first0[j] = rounded(dot(a0, planes[j]))
         return 0
 
-    lax.fori_loop(0, 32, level0_first, 0, unroll=8)
+    lax.fori_loop(0, 32, level0_first, 0, unroll=16)
 
     def even_first(pair, _):
         both = jnp.concatenate([planes[4 * pair, :, 0:128], planes[4 * pair + 2, :, 0:128]], axis=1)
@@ -223,7 +227,7 @@
         first12[2 * pair + 1] = out[:, 128:256]
         return 0
 
-    lax.fori_loop(0, 8, even_first, 0, unroll=4)
+    lax.fori_loop(0, 8, even_first, 0, unroll=8)
 
 
 def tall(ref, level, k):
@@ -536,45 +540,45 @@
     far = lax.ppermute(far, "inline", far_pairs)
     parts = [v.reshape(-1, xl_len, t_len) for v in (live, near, far)]
     stored = 48 if two_sided else 40
-    bands, w2, w3, pick, turn, turn_x, own_phases, moves1, moves2, select, gather = pl.pallas_call(
-        functools.partial(prepare_kernel, stored),
+    bands, w2, w3, pick, turn, own_phases = pl.pallas_call(
+        prepare_kernel,
         out_shape=(
             jax.ShapeDtypeStruct((3 * 256, 128), BF16),
             jax.ShapeDtypeStruct((TAPS, CHAN, 128), F32),
             jax.ShapeDtypeStruct((TAPS, CHAN, 128), F32),
             jax.ShapeDtypeStruct((256, 256), BF16),
             jax.ShapeDtypeStruct((512, 512), BF16),
+            jax.ShapeDtypeStruct((512, 256), BF16),
+        ),
+        in_specs=[vmem] * 2,
+        out_specs=(vmem,) * 6,
+        compiler_params=pltpu.CompilerParams(vmem_limit_bytes=PREPARE_VMEM),
+        cost_estimate=pl.CostEstimate(flops=10**9, bytes_accessed=4 * 10**6, transcendentals=0),
+        name="prepare",
+    )(taps, live)
+
+    def stack(js):
+        return jnp.concatenate([v[:, js] for v in parts], axis=0)
+
+    low, high = slice(0, REACH), slice(xl_len - REACH, xl_len)
+    if two_sided:
+        xh = [shifted(stack(high), "xline", 1), shifted(stack(low), "xline", -1)]
+    else:
+        xh = [flipped(jnp.where(x_index == 0, stack(high), stack(low)), [("xline", 1)])]
+    first0, first12, edge, turn_x, moves1, moves2, select, gather = pl.pallas_call(
+        functools.partial(inline_kernel, stored),
+        out_shape=(
+            jax.ShapeDtypeStruct((xl_len, 256, 256), F32),
+            jax.ShapeDtypeStruct((xl_len // 2, 512, 128), F32),
+            jax.ShapeDtypeStruct((ROWS * xl_len, 128), BF16),
             jax.ShapeDtypeStruct((512, 512), BF16),
-            jax.ShapeDtypeStruct((512, 256), BF16),
             jax.ShapeDtypeStruct((256, 512), BF16),
             jax.ShapeDtypeStruct((256, 512), BF16),
             jax.ShapeDtypeStruct((3, 256, TAPS * 128), BF16),
             jax.ShapeDtypeStruct((32, 32 * stored), BF16),
         ),
-        in_specs=[vmem] * 2,
-        out_specs=(vmem,) * 11,
-        compiler_params=pltpu.CompilerParams(vmem_limit_bytes=PREPARE_VMEM),
-        cost_estimate=pl.CostEstimate(flops=10**9, bytes_accessed=4 * 10**6, transcendentals=0),
-        name="prepare",
-    )(taps, live)
-
-    def stack(js):
-        return jnp.concatenate([v[:, js] for v in parts], axis=0)
-
-    low, high = slice(0, REACH), slice(xl_len - REACH, xl_len)
-    if two_sided:
-        xh = [shifted(stack(high), "xline", 1), shifted(stack(low), "xline", -1)]
-    else:
-        xh = [flipped(jnp.where(x_index == 0, stack(high), stack(low)), [("xline", 1)])]
-    first0, first12, edge = pl.pallas_call(
-        inline_kernel,
-        out_shape=(
-            jax.ShapeDtypeStruct((xl_len, 256, 256), F32),
-            jax.ShapeDtypeStruct((xl_len // 2, 512, 128), F32),
-            jax.ShapeDtypeStruct((ROWS * xl_len, 128), BF16),
-        ),
         in_specs=[vmem] * 7,
-        out_specs=(vmem,) * 3,
+        out_specs=(vmem,) * 8,
         scratch_shapes=[pltpu.VMEM((32, 32, 256), BF16)],
         compiler_params=pltpu.CompilerParams(vmem_limit_bytes=INLINE_VMEM),
         cost_estimate=pl.CostEstimate(flops=4 * 10**9, bytes_accessed=16 * 10**6, transcendentals=0),

time: 50.1 us -> 49.9 us (level)
  Pallas kernels: 24.2 us -> 23.3 us
    pallas_call x2, Pallas kernels: 4.21 us -> 3.56 us  [the longest x1 3.12 us: local(): pl.pallas_call(functools.partial(inline_kernel, stored), out_shape=(jax.S...]
  transfers between devices with their start and end apart: 9 -> 9, of which waited for: 5 -> 5; matrix products, arithmetic and copies ran while one was open for 2% -> 2% of each run, Pallas kernels for 14% -> 13%
where the time goes in v8:
time: 49.9 us; the launch traced here: 49.7 us
  Pallas kernels  23.3 us (47%)
  starting transfers between devices  15.2 us (30%)
  waiting for transfers between devices  7.77 us (16%)
  local copies, waits for them, and re-layouts  1.8 us (4%)
  other arithmetic  0.79 us (2%)
  between operations  0.78 us (2%)
    ppermute x7, starting transfers between devices, flipped(): return lax.ppermute(value, axes, pairs)  11.5 us
    pallas_call x1, Pallas kernels, local(): pl.pallas_call(functools.partial(attributes_kernel, two_sided), out_shape...  9.39 us
    pallas_call x1, Pallas kernels, local(): pl.pallas_call(whiten_kernel, out_shape=(jax.ShapeDtypeStruct((CHAN, 8, 1...  7.52 us
    ppermute x7, waiting for transfers between devices, flipped(): return lax.ppermute(value, axes, pairs)  7.32 us
    pallas_call x1, Pallas kernels, local(): pl.pallas_call(functools.partial(inline_kernel, stored), out_shape=(jax.S...  3.12 us
    ppermute x1, starting transfers between devices, local(): near = lax.ppermute(near, 'inline', near_pairs)  3.09 us
    pallas_call x1, Pallas kernels, local(): pl.pallas_call(functools.partial(crossline_kernel, two_sided), out_shape=...  2.66 us
  transfers between devices with their start and end apart: 9, of which 5 were waited for; matrix products, arithmetic and copies ran while one was open for 2% of the time, Pallas kernels for 13%

profile of v8, /device:TPU:0, one launch (start us, length us, event | category | flops | bytes accessed | tf_op | source)
XLA Modules:
  0.0 49.7 jit_solution(6785559728446195975)
XLA Ops:
  0.6 0.7 %convert_element_type.7.trace_ref = f32[16,32]{1,0:T(8,128)S(1)} convert(s32[16,32]{1,0:T(8,128)} %live_ref.1) | non-fusion elementwise | flops 512 | bytes 4096 | tf_op jit(solution)/shard_map/convert_element_type | solution.py:534
  1.3 0.0 copy-start
  1.3 0.9 %copy-done = bf16[16,32,256]{2,1,0:T(8,128)(2,1)S(1)} copy-done((bf16[16,32,256]{2,1,0:T(8,128)(2,1)S(1)}, bf16[16,32,256]{2,1,0:T(8,128)(2,1)}, u32[]{:S(2)}) %copy-start) | copy-done | bytes 262168
  2.3 0.2 live.1
  2.5 3.1 %collective-permute-start = (bf16[160,256]{1,0:T(8,128)(2,1)S(1)}, bf16[160,256]{1,0:T(8,128)(2,1)S(1)}, u32[]{:S(2)}, u32[]{:S(2)}) collective-permute-start(bf16[160,256]{1,0:T(8,128)(2,1)S(1)} %get-tuple-element.30), channel_id=1, source_target_pairs={{0,4},{4,0},{8,12},{12,8},{1,5},{5,1},{9,13},{13,9},{2,6},{6,2},{1... | collective-permute-start | bytes 245768 | tf_op jit(solution)/shard_map/ppermute | solution.py:539
  5.6 0.7 %collective-permute-start.1 = (bf16[160,256]{1,0:T(8,128)(2,1)S(1)}, bf16[160,256]{1,0:T(8,128)(2,1)S(1)}, u32[]{:S(2)}, u32[]{:S(2)}) collective-permute-start(bf16[160,256]{1,0:T(8,128)(2,1)S(1)} %get-tuple-element.31), channel_id=1, source_target_pairs={{4,8},{8,4},{5,9},{9,5},{6,10},{10,6},{7,11},{11,7},{20,24},{24,20... | collective-permute-start | bytes 245768 | tf_op jit(solution)/shard_map/ppermute | solution.py:540
  6.3 0.8 %copy.6.taps_ref = f32[3,96,5]{2,1,0:T(8,128)S(1)} copy(bf16[3,96,5]{1,0,2:T(4,128)(2,1)} %param.5) | data formatting | bytes 8640 | tf_op jit(solution)/shard_map/convert_element_type | solution.py:516
  7.1 0.4 prepare.1
  7.6 0.0 collective-permute-done.1.far_ref
  7.6 0.5 collective-permute-done.near_ref
  8.1 2.0 %collective-permute-start.2 = (bf16[26,8,256]{2,1,0:T(8,128)(2,1)S(1)}, bf16[26,8,256]{2,1,0:T(8,128)(2,1)S(1)}, u32[]{:S(2)}, u32[]{:S(2)}) collective-permute-start(bf16[26,8,256]{2,1,0:T(8,128)(2,1)S(1)} %maximum_select_fusion), channel_id=1, source_target_pairs={{0,2},{2,0},{1,3},{3,1},{4,6},{6,4},{5,7},{7,5},{8,10},{10,8},{9,1... | collective-permute-start | bytes 319496 | tf_op jit(solution)/shard_map/ppermute | solution.py:61
  10.0 3.1 %inline.1 = (f32[32,256,256]{2,1,0:T(8,128)S(1)}, f32[16,512,128]{2,1,0:T(8,128)S(1)}, bf16[832,128]{1,0:T(8,128)(2,1)S(1)}, bf16[512,512]{1,0:T(8,128)(2,1)S(1)...) custom-call(bf16[768,128]{1,0:T(8,128)(2,1)S(1)} %get-tuple-element., ...), custom_call_target="tpu_custom_call" | custom-call | flops 4000000000 | bytes 16000000 | tf_op jit(solution)/shard_map/inline/pallas_call | solution.py:568
  13.2 0.0 collective-permute-done.2
  13.2 0.1 collective-permute-start.3
  13.3 0.0 copy-start.1
  13.3 2.7 %crossline.1 = (f32[3,256,256]{2,1,0:T(8,128)S(1)}, bf16[16,512,128]{2,1,0:T(8,128)(2,1)S(1)}) custom-call(bf16[768,128]{1,0:T(8,128)(2,1)S(1)} %get-tuple-element.24.bands, f32[5,96,128]{2,1,0:T(8,128)S(1)} %get-tuple-element.25.w2, bf16[256,256]{1,0:T(8,128)(2,1)S(1)} %get-tuple-element.27.pick, bf16[512,512]{1,0:T(8,128)(2,1)S(1)} %get-tuple-element.37.turn_x, ...), custom_call_target="tpu_custom_call" | custom-call | flops 3000000000 | bytes 9000000 | tf_op jit(solution)/shard_map/crossline/pallas_call | solution.py:594
  16.0 0.0 collective-permute-done.3.dh_ref
  16.0 0.0 copy-done.1
  16.0 9.4 %attributes.1 = (bf16[16,3,8,32,128]{4,3,2,1,0:T(8,128)(2,1)S(1)}, f32[96,128]{1,0:T(8,128)S(1)}) custom-call(s32[16,32]{1,0:T(8,128)S(1)} %copy-done.1, s32[16,32]{1,0:T(8,128)S(1)} %copy-done.1, bf16[768,128]{1,0:T(8,128)(2,1)S(1)} %get-tuple-element.24.bands, f32[5,96,128]{2,1,0:T(8,128)S(1)} %get-tuple-element.25.w2, ...), custom_call_target="tpu_custom_call" | custom-call | tf_op jit(solution)/shard_map/attributes/pallas_call | solution.py:610
  25.4 0.5 %collective-permute-start.4 = (f32[96,128]{1,0:T(8,128)S(1)}, f32[96,128]{1,0:T(8,128)S(1)}, u32[]{:S(2)}, u32[]{:S(2)}) collective-permute-start(f32[96,128]{1,0:T(8,128)S(1)} %get-tuple-element.42), channel_id=1, source_target_pairs={{0,1},{1,0},{2,3},{3,2},{4,5},{5,4},{6,7},{7,6},{8,9},{9,8},{10,11... | collective-permute-start | bytes 147464 | tf_op jit(solution)/shard_map/ppermute | solution.py:61
  26.0 0.9 %collective-permute-done.4 = f32[96,128]{1,0:T(8,128)S(1)} collective-permute-done((f32[96,128]{1,0:T(8,128)S(1)}, f32[96,128]{1,0:T(8,128)S(1)}, u32[]{:S(2)}, u32[]{:S(2)}) %collective-permute-start.4) | collective-permute-done | bytes 49184 | tf_op jit(solution)/shard_map/ppermute | solution.py:61
  26.8 1.6 %collective-permute-start.6 = (f32[96,128]{1,0:T(8,128)S(1)}, f32[96,128]{1,0:T(8,128)S(1)}, u32[]{:S(2)}, u32[]{:S(2)}) collective-permute-start(f32[96,128]{1,0:T(8,128)S(1)} %add.12), channel_id=1, source_target_pairs={{0,2},{2,0},{1,3},{3,1},{4,6},{6,4},{5,7},{7,5},{8,10},{10,8},{9,1... | collective-permute-start | bytes 147464 | tf_op jit(solution)/shard_map/ppermute | solution.py:61
  28.4 4.6 %collective-permute-start.7 = (f32[96,128]{1,0:T(8,128)S(1)}, f32[96,128]{1,0:T(8,128)S(1)}, u32[]{:S(2)}, u32[]{:S(2)}) collective-permute-start(f32[96,128]{1,0:T(8,128)S(1)} %add.12), channel_id=1, source_target_pairs={{0,6},{2,4},{4,2},{6,0},{8,14},{10,12},{12,10},{14,8},{1,7},{3,5},... | collective-permute-start | bytes 147464 | tf_op jit(solution)/shard_map/ppermute | solution.py:61
  33.0 0.0 collective-permute-start.5
  33.0 0.0 collective-permute-done.6
  33.0 2.0 %collective-permute-done.7 = f32[96,128]{1,0:T(8,128)S(1)} collective-permute-done((f32[96,128]{1,0:T(8,128)S(1)}, f32[96,128]{1,0:T(8,128)S(1)}, u32[]{:S(2)}, u32[]{:S(2)}) %collective-permute-start.7) | collective-permute-done | bytes 49184 | tf_op jit(solution)/shard_map/ppermute | solution.py:61
  35.1 2.0 %collective-permute-done.5 = f32[96,128]{1,0:T(8,128)S(1)} collective-permute-done((f32[96,128]{1,0:T(8,128)S(1)}, f32[96,128]{1,0:T(8,128)S(1)}, u32[]{:S(2)}, u32[]{:S(2)}) %collective-permute-start.5) | collective-permute-done | bytes 49184 | tf_op jit(solution)/shard_map/ppermute | solution.py:61
  37.1 2.7 %collective-permute-start.8 = (f32[96,128]{1,0:T(8,128)S(1)}, f32[96,128]{1,0:T(8,128)S(1)}, u32[]{:S(2)}, u32[]{:S(2)}) collective-permute-start(f32[96,128]{1,0:T(8,128)S(1)} %add_add_fusion.mine_ref), channel_id=1, source_target_pairs={{0,8},{4,12},{8,0},{12,4},{1,9},{5,13},{9,1},{13,5},{2,10},{6,14},... | collective-permute-start | bytes 147464 | tf_op jit(solution)/shard_map/ppermute | solution.py:61
  39.8 2.4 %collective-permute-done.8.other_ref = f32[96,128]{1,0:T(8,128)S(1)} collective-permute-done((f32[96,128]{1,0:T(8,128)S(1)}, f32[96,128]{1,0:T(8,128)S(1)}, u32[]{:S(2)}, u32[]{:S(2)}) %collective-permute-start.8) | collective-permute-done | bytes 49184 | tf_op jit(solution)/shard_map/ppermute | solution.py:61
  42.2 7.5 %whiten.1 = (bf16[96,8,16,128]{3,2,1,0:T(8,128)(2,1)}, f32[96,96]{1,0:T(8,128)}) custom-call(f32[96,128]{1,0:T(8,128)S(1)} %add_add_fusion.mine_ref, f32[96,128]{1,0:T(8,128)S(1)} %collective-permute-done.8.other_ref, bf16[16,3,8,32,128]{4,3,2,1,0:T(8,128)(2,1)S(1)} %get-tuple-element.43.attr_ref), custom_call_target="tpu_custom_call" | custom-call | tf_op jit(solution)/shard_map/whiten/pallas_call | solution.py:627
  (8 shorter events, 0.1 us)
Async XLA Ops:
  1.3 0.9 %copy-start = (bf16[16,32,256]{2,1,0:T(8,128)(2,1)S(1)}, bf16[16,32,256]{2,1,0:T(8,128)(2,1)}, u32[]{:S(2)}) copy-start(bf16[16,32,256]{2,1,0:T(8,128)(2,1)} %seismic_ref.1) | copy-start | bytes 786436
  2.5 5.5 %collective-permute-start = (bf16[160,256]{1,0:T(8,128)(2,1)S(1)}, bf16[160,256]{1,0:T(8,128)(2,1)S(1)}, u32[]{:S(2)}, u32[]{:S(2)}) collective-permute-start(bf16[160,256]{1,0:T(8,128)(2,1)S(1)} %get-tuple-element.30), channel_id=1, source_target_pairs={{0,4},{4,0},{8,12},{12,8},{1,5},{5,1},{9,13},{13,9},{2,6},{6,2},{1... | collective-permute-start | bytes 245768 | tf_op jit(solution)/shard_map/ppermute | solution.py:539
  5.6 2.0 %collective-permute-start.1 = (bf16[160,256]{1,0:T(8,128)(2,1)S(1)}, bf16[160,256]{1,0:T(8,128)(2,1)S(1)}, u32[]{:S(2)}, u32[]{:S(2)}) collective-permute-start(bf16[160,256]{1,0:T(8,128)(2,1)S(1)} %get-tuple-element.31), channel_id=1, source_target_pairs={{4,8},{8,4},{5,9},{9,5},{6,10},{10,6},{7,11},{11,7},{20,24},{24,20... | collective-permute-start | bytes 245768 | tf_op jit(solution)/shard_map/ppermute | solution.py:540
  8.1 5.1 %collective-permute-start.2 = (bf16[26,8,256]{2,1,0:T(8,128)(2,1)S(1)}, bf16[26,8,256]{2,1,0:T(8,128)(2,1)S(1)}, u32[]{:S(2)}, u32[]{:S(2)}) collective-permute-start(bf16[26,8,256]{2,1,0:T(8,128)(2,1)S(1)} %maximum_select_fusion), channel_id=1, source_target_pairs={{0,2},{2,0},{1,3},{3,1},{4,6},{6,4},{5,7},{7,5},{8,10},{10,8},{9,1... | collective-permute-start | bytes 319496 | tf_op jit(solution)/shard_map/ppermute | solution.py:61
  13.2 2.8 %collective-permute-start.3 = (bf16[26,40,128]{2,1,0:T(8,128)(2,1)S(1)}, bf16[26,40,128]{2,1,0:T(8,128)(2,1)S(1)}, u32[]{:S(2)}, u32[]{:S(2)}) collective-permute-start(bf16[26,40,128]{2,1,0:T(8,128)(2,1)S(1)} %pad_maximum_fusion), channel_id=1, source_target_pairs={{0,1},{1,0},{2,3},{3,2},{4,5},{5,4},{6,7},{7,6},{8,9},{9,8},{10,11... | collective-permute-start | bytes 798728 | tf_op jit(solution)/shard_map/ppermute | solution.py:61
  13.3 2.7 %copy-start.1 = (s32[16,32]{1,0:T(8,128)S(1)}, s32[16,32]{1,0:T(8,128)}, u32[]{:S(2)}) copy-start(s32[16,32]{1,0:T(8,128)} %live_ref.1) | copy-start | bytes 6148
  25.4 1.4 %collective-permute-start.4 = (f32[96,128]{1,0:T(8,128)S(1)}, f32[96,128]{1,0:T(8,128)S(1)}, u32[]{:S(2)}, u32[]{:S(2)}) collective-permute-start(f32[96,128]{1,0:T(8,128)S(1)} %get-tuple-element.42), channel_id=1, source_target_pairs={{0,1},{1,0},{2,3},{3,2},{4,5},{5,4},{6,7},{7,6},{8,9},{9,8},{10,11... | collective-permute-start | bytes 147464 | tf_op jit(solution)/shard_map/ppermute | solution.py:61
  26.8 6.2 %collective-permute-start.6 = (f32[96,128]{1,0:T(8,128)S(1)}, f32[96,128]{1,0:T(8,128)S(1)}, u32[]{:S(2)}, u32[]{:S(2)}) collective-permute-start(f32[96,128]{1,0:T(8,128)S(1)} %add.12), channel_id=1, source_target_pairs={{0,2},{2,0},{1,3},{3,1},{4,6},{6,4},{5,7},{7,5},{8,10},{10,8},{9,1... | collective-permute-start | bytes 147464 | tf_op jit(solution)/shard_map/ppermute | solution.py:61
  28.4 6.7 %collective-permute-start.7 = (f32[96,128]{1,0:T(8,128)S(1)}, f32[96,128]{1,0:T(8,128)S(1)}, u32[]{:S(2)}, u32[]{:S(2)}) collective-permute-start(f32[96,128]{1,0:T(8,128)S(1)} %add.12), channel_id=1, source_target_pairs={{0,6},{2,4},{4,2},{6,0},{8,14},{10,12},{12,10},{14,8},{1,7},{3,5},... | collective-permute-start | bytes 147464 | tf_op jit(solution)/shard_map/ppermute | solution.py:61
  33.0 4.1 %collective-permute-start.5 = (f32[96,128]{1,0:T(8,128)S(1)}, f32[96,128]{1,0:T(8,128)S(1)}, u32[]{:S(2)}, u32[]{:S(2)}) collective-permute-start(f32[96,128]{1,0:T(8,128)S(1)} %add.12), channel_id=1, source_target_pairs={{0,4},{4,0},{8,12},{12,8},{1,5},{5,1},{9,13},{13,9},{2,6},{6,2},{1... | collective-permute-start | bytes 147464 | tf_op jit(solution)/shard_map/ppermute | solution.py:61
  37.1 5.1 %collective-permute-start.8 = (f32[96,128]{1,0:T(8,128)S(1)}, f32[96,128]{1,0:T(8,128)S(1)}, u32[]{:S(2)}, u32[]{:S(2)}) collective-permute-start(f32[96,128]{1,0:T(8,128)S(1)} %add_add_fusion.mine_ref), channel_id=1, source_target_pairs={{0,8},{4,12},{8,0},{12,4},{1,9},{5,13},{9,1},{13,5},{2,10},{6,14},... | collective-permute-start | bytes 147464 | tf_op jit(solution)/shard_map/ppermute | solution.py:61

commit v9 on v8

--- a/solution.py
+++ b/solution.py
@@ -279,7 +279,7 @@
             filtered(level, q, own_plane)
             return 0
 
-        lax.fori_loop(reach, 16 - reach, inner, 0)
+        lax.fori_loop(reach, 16 - reach, inner, 0, unroll=4)
         for i in range(reach):
             filtered(level, i, any_plane)
             filtered(level, 15 - i, any_plane)

time: 49.9 us -> 49.8 us (level)
  transfers between devices with their start and end apart: 9 -> 9, of which waited for: 5 -> 5; matrix products, arithmetic and copies ran while one was open for 2% -> 2% of each run, Pallas kernels for 13% -> 12%
where the time goes in v9:
time: 49.8 us; the launch traced here: 49.5 us
  Pallas kernels  23.2 us (47%)
  starting transfers between devices  15.2 us (31%)
  waiting for transfers between devices  7.77 us (16%)
  local copies, waits for them, and re-layouts  1.8 us (4%)
  other arithmetic  0.79 us (2%)
  between operations  0.78 us (2%)
    ppermute x7, starting transfers between devices, flipped(): return lax.ppermute(value, axes, pairs)  11.5 us
    pallas_call x1, Pallas kernels, local(): pl.pallas_call(functools.partial(attributes_kernel, two_sided), out_shape...  9.39 us
    pallas_call x1, Pallas kernels, local(): pl.pallas_call(whiten_kernel, out_shape=(jax.ShapeDtypeStruct((CHAN, 8, 1...  7.52 us
    ppermute x7, waiting for transfers between devices, flipped(): return lax.ppermute(value, axes, pairs)  7.32 us
    pallas_call x1, Pallas kernels, local(): pl.pallas_call(functools.partial(inline_kernel, stored), out_shape=(jax.S...  3.12 us
    ppermute x1, starting transfers between devices, local(): near = lax.ppermute(near, 'inline', near_pairs)  3.09 us
    pallas_call x1, Pallas kernels, local(): pl.pallas_call(functools.partial(crossline_kernel, two_sided), out_shape=...  2.52 us
  transfers between devices with their start and end apart: 9, of which 5 were waited for; matrix products, arithmetic and copies ran while one was open for 2% of the time, Pallas kernels for 12%

profile of v9, /device:TPU:0, one launch (start us, length us, event | category | flops | bytes accessed | tf_op | source)
XLA Modules:
  0.0 49.5 jit_solution(15862586138033799145)
XLA Ops:
  0.6 0.7 %convert_element_type.7.trace_ref = f32[16,32]{1,0:T(8,128)S(1)} convert(s32[16,32]{1,0:T(8,128)} %live_ref.1) | non-fusion elementwise | flops 512 | bytes 4096 | tf_op jit(solution)/shard_map/convert_element_type | solution.py:534
  1.3 0.0 copy-start
  1.3 0.9 %copy-done = bf16[16,32,256]{2,1,0:T(8,128)(2,1)S(1)} copy-done((bf16[16,32,256]{2,1,0:T(8,128)(2,1)S(1)}, bf16[16,32,256]{2,1,0:T(8,128)(2,1)}, u32[]{:S(2)}) %copy-start) | copy-done | bytes 262168
  2.3 0.2 live.1
  2.5 3.1 %collective-permute-start = (bf16[160,256]{1,0:T(8,128)(2,1)S(1)}, bf16[160,256]{1,0:T(8,128)(2,1)S(1)}, u32[]{:S(2)}, u32[]{:S(2)}) collective-permute-start(bf16[160,256]{1,0:T(8,128)(2,1)S(1)} %get-tuple-element.30), channel_id=1, source_target_pairs={{0,4},{4,0},{8,12},{12,8},{1,5},{5,1},{9,13},{13,9},{2,6},{6,2},{1... | collective-permute-start | bytes 245768 | tf_op jit(solution)/shard_map/ppermute | solution.py:539
  5.6 0.7 %collective-permute-start.1 = (bf16[160,256]{1,0:T(8,128)(2,1)S(1)}, bf16[160,256]{1,0:T(8,128)(2,1)S(1)}, u32[]{:S(2)}, u32[]{:S(2)}) collective-permute-start(bf16[160,256]{1,0:T(8,128)(2,1)S(1)} %get-tuple-element.31), channel_id=1, source_target_pairs={{4,8},{8,4},{5,9},{9,5},{6,10},{10,6},{7,11},{11,7},{20,24},{24,20... | collective-permute-start | bytes 245768 | tf_op jit(solution)/shard_map/ppermute | solution.py:540
  6.3 0.8 %copy.6.taps_ref = f32[3,96,5]{2,1,0:T(8,128)S(1)} copy(bf16[3,96,5]{1,0,2:T(4,128)(2,1)} %param.5) | data formatting | bytes 8640 | tf_op jit(solution)/shard_map/convert_element_type | solution.py:516
  7.1 0.4 prepare.1
  7.6 0.0 collective-permute-done.1.far_ref
  7.6 0.5 collective-permute-done.near_ref
  8.1 2.0 %collective-permute-start.2 = (bf16[26,8,256]{2,1,0:T(8,128)(2,1)S(1)}, bf16[26,8,256]{2,1,0:T(8,128)(2,1)S(1)}, u32[]{:S(2)}, u32[]{:S(2)}) collective-permute-start(bf16[26,8,256]{2,1,0:T(8,128)(2,1)S(1)} %maximum_select_fusion), channel_id=1, source_target_pairs={{0,2},{2,0},{1,3},{3,1},{4,6},{6,4},{5,7},{7,5},{8,10},{10,8},{9,1... | collective-permute-start | bytes 319496 | tf_op jit(solution)/shard_map/ppermute | solution.py:61
  10.0 3.1 %inline.1 = (f32[32,256,256]{2,1,0:T(8,128)S(1)}, f32[16,512,128]{2,1,0:T(8,128)S(1)}, bf16[832,128]{1,0:T(8,128)(2,1)S(1)}, bf16[512,512]{1,0:T(8,128)(2,1)S(1)...) custom-call(bf16[768,128]{1,0:T(8,128)(2,1)S(1)} %get-tuple-element., ...), custom_call_target="tpu_custom_call" | custom-call | flops 4000000000 | bytes 16000000 | tf_op jit(solution)/shard_map/inline/pallas_call | solution.py:568
  13.2 0.0 collective-permute-done.2
  13.2 0.1 collective-permute-start.3
  13.3 0.0 copy-start.1
  13.3 2.5 %crossline.1 = (f32[3,256,256]{2,1,0:T(8,128)S(1)}, bf16[16,512,128]{2,1,0:T(8,128)(2,1)S(1)}) custom-call(bf16[768,128]{1,0:T(8,128)(2,1)S(1)} %get-tuple-element.24.bands, f32[5,96,128]{2,1,0:T(8,128)S(1)} %get-tuple-element.25.w2, bf16[256,256]{1,0:T(8,128)(2,1)S(1)} %get-tuple-element.27.pick, bf16[512,512]{1,0:T(8,128)(2,1)S(1)} %get-tuple-element.37.turn_x, ...), custom_call_target="tpu_custom_call" | custom-call | flops 3000000000 | bytes 9000000 | tf_op jit(solution)/shard_map/crossline/pallas_call | solution.py:594
  15.9 0.0 collective-permute-done.3.dh_ref
  15.9 0.0 copy-done.1
  15.9 9.4 %attributes.1 = (bf16[16,3,8,32,128]{4,3,2,1,0:T(8,128)(2,1)S(1)}, f32[96,128]{1,0:T(8,128)S(1)}) custom-call(s32[16,32]{1,0:T(8,128)S(1)} %copy-done.1, s32[16,32]{1,0:T(8,128)S(1)} %copy-done.1, bf16[768,128]{1,0:T(8,128)(2,1)S(1)} %get-tuple-element.24.bands, f32[5,96,128]{2,1,0:T(8,128)S(1)} %get-tuple-element.25.w2, ...), custom_call_target="tpu_custom_call" | custom-call | tf_op jit(solution)/shard_map/attributes/pallas_call | solution.py:610
  25.3 0.5 %collective-permute-start.4 = (f32[96,128]{1,0:T(8,128)S(1)}, f32[96,128]{1,0:T(8,128)S(1)}, u32[]{:S(2)}, u32[]{:S(2)}) collective-permute-start(f32[96,128]{1,0:T(8,128)S(1)} %get-tuple-element.42), channel_id=1, source_target_pairs={{0,1},{1,0},{2,3},{3,2},{4,5},{5,4},{6,7},{7,6},{8,9},{9,8},{10,11... | collective-permute-start | bytes 147464 | tf_op jit(solution)/shard_map/ppermute | solution.py:61
  25.8 0.9 %collective-permute-done.4 = f32[96,128]{1,0:T(8,128)S(1)} collective-permute-done((f32[96,128]{1,0:T(8,128)S(1)}, f32[96,128]{1,0:T(8,128)S(1)}, u32[]{:S(2)}, u32[]{:S(2)}) %collective-permute-start.4) | collective-permute-done | bytes 49184 | tf_op jit(solution)/shard_map/ppermute | solution.py:61
  26.7 1.6 %collective-permute-start.6 = (f32[96,128]{1,0:T(8,128)S(1)}, f32[96,128]{1,0:T(8,128)S(1)}, u32[]{:S(2)}, u32[]{:S(2)}) collective-permute-start(f32[96,128]{1,0:T(8,128)S(1)} %add.12), channel_id=1, source_target_pairs={{0,2},{2,0},{1,3},{3,1},{4,6},{6,4},{5,7},{7,5},{8,10},{10,8},{9,1... | collective-permute-start | bytes 147464 | tf_op jit(solution)/shard_map/ppermute | solution.py:61
  28.3 4.6 %collective-permute-start.7 = (f32[96,128]{1,0:T(8,128)S(1)}, f32[96,128]{1,0:T(8,128)S(1)}, u32[]{:S(2)}, u32[]{:S(2)}) collective-permute-start(f32[96,128]{1,0:T(8,128)S(1)} %add.12), channel_id=1, source_target_pairs={{0,6},{2,4},{4,2},{6,0},{8,14},{10,12},{12,10},{14,8},{1,7},{3,5},... | collective-permute-start | bytes 147464 | tf_op jit(solution)/shard_map/ppermute | solution.py:61
  32.9 0.0 collective-permute-start.5
  32.9 0.0 collective-permute-done.6
  32.9 2.0 %collective-permute-done.7 = f32[96,128]{1,0:T(8,128)S(1)} collective-permute-done((f32[96,128]{1,0:T(8,128)S(1)}, f32[96,128]{1,0:T(8,128)S(1)}, u32[]{:S(2)}, u32[]{:S(2)}) %collective-permute-start.7) | collective-permute-done | bytes 49184 | tf_op jit(solution)/shard_map/ppermute | solution.py:61
  34.9 2.0 %collective-permute-done.5 = f32[96,128]{1,0:T(8,128)S(1)} collective-permute-done((f32[96,128]{1,0:T(8,128)S(1)}, f32[96,128]{1,0:T(8,128)S(1)}, u32[]{:S(2)}, u32[]{:S(2)}) %collective-permute-start.5) | collective-permute-done | bytes 49184 | tf_op jit(solution)/shard_map/ppermute | solution.py:61
  37.0 2.7 %collective-permute-start.8 = (f32[96,128]{1,0:T(8,128)S(1)}, f32[96,128]{1,0:T(8,128)S(1)}, u32[]{:S(2)}, u32[]{:S(2)}) collective-permute-start(f32[96,128]{1,0:T(8,128)S(1)} %add_add_fusion.mine_ref), channel_id=1, source_target_pairs={{0,8},{4,12},{8,0},{12,4},{1,9},{5,13},{9,1},{13,5},{2,10},{6,14},... | collective-permute-start | bytes 147464 | tf_op jit(solution)/shard_map/ppermute | solution.py:61
  39.6 2.4 %collective-permute-done.8.other_ref = f32[96,128]{1,0:T(8,128)S(1)} collective-permute-done((f32[96,128]{1,0:T(8,128)S(1)}, f32[96,128]{1,0:T(8,128)S(1)}, u32[]{:S(2)}, u32[]{:S(2)}) %collective-permute-start.8) | collective-permute-done | bytes 49184 | tf_op jit(solution)/shard_map/ppermute | solution.py:61
  42.0 7.5 %whiten.1 = (bf16[96,8,16,128]{3,2,1,0:T(8,128)(2,1)}, f32[96,96]{1,0:T(8,128)}) custom-call(f32[96,128]{1,0:T(8,128)S(1)} %add_add_fusion.mine_ref, f32[96,128]{1,0:T(8,128)S(1)} %collective-permute-done.8.other_ref, bf16[16,3,8,32,128]{4,3,2,1,0:T(8,128)(2,1)S(1)} %get-tuple-element.43.attr_ref), custom_call_target="tpu_custom_call" | custom-call | tf_op jit(solution)/shard_map/whiten/pallas_call | solution.py:627
  (8 shorter events, 0.1 us)
Async XLA Ops:
  1.3 0.9 %copy-start = (bf16[16,32,256]{2,1,0:T(8,128)(2,1)S(1)}, bf16[16,32,256]{2,1,0:T(8,128)(2,1)}, u32[]{:S(2)}) copy-start(bf16[16,32,256]{2,1,0:T(8,128)(2,1)} %seismic_ref.1) | copy-start | bytes 786436
  2.5 5.5 %collective-permute-start = (bf16[160,256]{1,0:T(8,128)(2,1)S(1)}, bf16[160,256]{1,0:T(8,128)(2,1)S(1)}, u32[]{:S(2)}, u32[]{:S(2)}) collective-permute-start(bf16[160,256]{1,0:T(8,128)(2,1)S(1)} %get-tuple-element.30), channel_id=1, source_target_pairs={{0,4},{4,0},{8,12},{12,8},{1,5},{5,1},{9,13},{13,9},{2,6},{6,2},{1... | collective-permute-start | bytes 245768 | tf_op jit(solution)/shard_map/ppermute | solution.py:539
  5.6 2.0 %collective-permute-start.1 = (bf16[160,256]{1,0:T(8,128)(2,1)S(1)}, bf16[160,256]{1,0:T(8,128)(2,1)S(1)}, u32[]{:S(2)}, u32[]{:S(2)}) collective-permute-start(bf16[160,256]{1,0:T(8,128)(2,1)S(1)} %get-tuple-element.31), channel_id=1, source_target_pairs={{4,8},{8,4},{5,9},{9,5},{6,10},{10,6},{7,11},{11,7},{20,24},{24,20... | collective-permute-start | bytes 245768 | tf_op jit(solution)/shard_map/ppermute | solution.py:540
  8.1 5.1 %collective-permute-start.2 = (bf16[26,8,256]{2,1,0:T(8,128)(2,1)S(1)}, bf16[26,8,256]{2,1,0:T(8,128)(2,1)S(1)}, u32[]{:S(2)}, u32[]{:S(2)}) collective-permute-start(bf16[26,8,256]{2,1,0:T(8,128)(2,1)S(1)} %maximum_select_fusion), channel_id=1, source_target_pairs={{0,2},{2,0},{1,3},{3,1},{4,6},{6,4},{5,7},{7,5},{8,10},{10,8},{9,1... | collective-permute-start | bytes 319496 | tf_op jit(solution)/shard_map/ppermute | solution.py:61
  13.2 2.6 %collective-permute-start.3 = (bf16[26,40,128]{2,1,0:T(8,128)(2,1)S(1)}, bf16[26,40,128]{2,1,0:T(8,128)(2,1)S(1)}, u32[]{:S(2)}, u32[]{:S(2)}) collective-permute-start(bf16[26,40,128]{2,1,0:T(8,128)(2,1)S(1)} %pad_maximum_fusion), channel_id=1, source_target_pairs={{0,1},{1,0},{2,3},{3,2},{4,5},{5,4},{6,7},{7,6},{8,9},{9,8},{10,11... | collective-permute-start | bytes 798728 | tf_op jit(solution)/shard_map/ppermute | solution.py:61
  13.3 2.5 %copy-start.1 = (s32[16,32]{1,0:T(8,128)S(1)}, s32[16,32]{1,0:T(8,128)}, u32[]{:S(2)}) copy-start(s32[16,32]{1,0:T(8,128)} %live_ref.1) | copy-start | bytes 6148
  25.3 1.4 %collective-permute-start.4 = (f32[96,128]{1,0:T(8,128)S(1)}, f32[96,128]{1,0:T(8,128)S(1)}, u32[]{:S(2)}, u32[]{:S(2)}) collective-permute-start(f32[96,128]{1,0:T(8,128)S(1)} %get-tuple-element.42), channel_id=1, source_target_pairs={{0,1},{1,0},{2,3},{3,2},{4,5},{5,4},{6,7},{7,6},{8,9},{9,8},{10,11... | collective-permute-start | bytes 147464 | tf_op jit(solution)/shard_map/ppermute | solution.py:61
  26.7 6.2 %collective-permute-start.6 = (f32[96,128]{1,0:T(8,128)S(1)}, f32[96,128]{1,0:T(8,128)S(1)}, u32[]{:S(2)}, u32[]{:S(2)}) collective-permute-start(f32[96,128]{1,0:T(8,128)S(1)} %add.12), channel_id=1, source_target_pairs={{0,2},{2,0},{1,3},{3,1},{4,6},{6,4},{5,7},{7,5},{8,10},{10,8},{9,1... | collective-permute-start | bytes 147464 | tf_op jit(solution)/shard_map/ppermute | solution.py:61
  28.3 6.7 %collective-permute-start.7 = (f32[96,128]{1,0:T(8,128)S(1)}, f32[96,128]{1,0:T(8,128)S(1)}, u32[]{:S(2)}, u32[]{:S(2)}) collective-permute-start(f32[96,128]{1,0:T(8,128)S(1)} %add.12), channel_id=1, source_target_pairs={{0,6},{2,4},{4,2},{6,0},{8,14},{10,12},{12,10},{14,8},{1,7},{3,5},... | collective-permute-start | bytes 147464 | tf_op jit(solution)/shard_map/ppermute | solution.py:61
  32.9 4.1 %collective-permute-start.5 = (f32[96,128]{1,0:T(8,128)S(1)}, f32[96,128]{1,0:T(8,128)S(1)}, u32[]{:S(2)}, u32[]{:S(2)}) collective-permute-start(f32[96,128]{1,0:T(8,128)S(1)} %add.12), channel_id=1, source_target_pairs={{0,4},{4,0},{8,12},{12,8},{1,5},{5,1},{9,13},{13,9},{2,6},{6,2},{1... | collective-permute-start | bytes 147464 | tf_op jit(solution)/shard_map/ppermute | solution.py:61
  37.0 5.1 %collective-permute-start.8 = (f32[96,128]{1,0:T(8,128)S(1)}, f32[96,128]{1,0:T(8,128)S(1)}, u32[]{:S(2)}, u32[]{:S(2)}) collective-permute-start(f32[96,128]{1,0:T(8,128)S(1)} %add_add_fusion.mine_ref), channel_id=1, source_target_pairs={{0,8},{4,12},{8,0},{12,4},{1,9},{5,13},{9,1},{13,5},{2,10},{6,14},... | collective-permute-start | bytes 147464 | tf_op jit(solution)/shard_map/ppermute | solution.py:61
